TPU v7x, 32 devices: a whole 2x2x4 slice. The times are simulated.
32 devices in a mesh: fsdp: 8 (over z, y), rep: 4 (over x, core).
Axes of the slice: x: 2, y: 2, z: 4, core: 2. Of those that a mesh axis runs over, the one named last changes fastest.
Arguments:
- hidden_in: bfloat16 [8192, 2048], P(('fsdp', 'rep')), may hold values from -6 to 6
- segment_ids: int32 [8192], P(('fsdp', 'rep')), may hold values from 0 to 8191, as said below
- w_attn: bfloat16 [2048, 5120], P(('fsdp', 'rep'))
- w_ffn: bfloat16 [2048, 24576], P(('fsdp', 'rep'))
- gains: bfloat16 [2, 2048], P(None, ('fsdp', 'rep')), may hold values from 0.25 to 1.75
- out_grad: bfloat16 [8192, 2048], P(('fsdp', 'rep')), may hold values from -6 to 6
Outputs:
- hidden_out: bfloat16 [8192, 2048], P(('fsdp', 'rep'))
- in_grad: bfloat16 [8192, 2048], P(('fsdp', 'rep'))
- attn_grad: float32 [2048, 5120], P(('fsdp', 'rep'))
- ffn_grad: float32 [2048, 24576], P(('fsdp', 'rep'))
- gains_grad: float32 [2, 2048], P(None, ('fsdp', 'rep'))
Inputs may be any that keep to these rules, and one draw needn't show every extreme that they name: `segment_ids`: each id is the index of its segment's first token, so ids never fall; a segment has 1 to 512 tokens and meets at most two of the aligned blocks of 256 tokens; some segment has exactly 512 tokens, and the last token is a segment of its own.
All inputs are finite; a program needn't handle non-finite values.
Results may differ from a plain program's by a relative error of at most 0.014.
Values may be sent and summed in bfloat16 or wider, within the bound.
No kernel may reach another device: no remote copies, remote signals or barrier semaphores. Data moves between devices by JAX's collectives and lax.ppermute only.
A program may use at most 832 MiB of HBM per device.

v0:
```python
import jax
import jax.numpy as jnp
from jax import lax
from jax.sharding import PartitionSpec as P

D = 2048
H = 32
KV = 8
HD = 64
FF = 8192


NORM_EPS = 1e-05
ROPE_BASE = 500000.0


def from_behind(value, axis, steps):
    count = lax.axis_size(axis)
    leading, last = (max(0, -steps), min(count, count - steps))
    return lax.ppermute(value, axis, [(source, source + steps) for source in range(leading, last)])


def rms_norm(values, scales):
    return values * lax.rsqrt(jnp.mean(values * values, axis=-1, keepdims=True) + NORM_EPS) * scales


def swiglu(gate, upward):
    return gate * jax.nn.sigmoid(gate) * upward


def rotary(positions):
    freqs = 1.0 / ROPE_BASE ** (jnp.arange(HD // 2, dtype=jnp.float32) * (2.0 / HD))
    angles = positions.astype(jnp.float32)[..., None] * freqs
    cosine = jnp.concatenate([jnp.cos(angles), jnp.cos(angles)], axis=-1)
    sine = jnp.concatenate([jnp.sin(angles), jnp.sin(angles)], axis=-1)
    return (cosine, sine)


def rotate(values, cosine, sine):
    halfway = values.shape[-1] // 2
    turned = jnp.concatenate([-values[..., halfway:], values[..., :halfway]], axis=-1)
    return values * cosine + turned * sine


def contract_rows(left, right):
    return lax.dot_general(
        left, right, (((0,), (0,)), ((), ())), preferred_element_type=jnp.float32
    )


def contract_cols(left, right):
    return lax.dot_general(
        left, right, (((1,), (1,)), ((), ())), preferred_element_type=jnp.float32
    )


def masked_scores(q_rot, k_rot, allowed):
    raw_scores = jnp.einsum(
        "tkrd,skd->krts", q_rot, k_rot, preferred_element_type=jnp.float32
    ) * HD ** (-0.5)
    return jnp.where(allowed, raw_scores, -1e30)


def fetch_attn(w_attn, gains):
    fetched = (
        lax.all_gather(w_attn, ("fsdp", "rep"), axis=0, tiled=True),
        lax.all_gather(gains, ("fsdp", "rep"), axis=1, tiled=True),
    )
    return fetched


def fetch_ffn(w_ffn):
    fetched = lax.all_gather(w_ffn, ("fsdp", "rep"), axis=0, tiled=True)
    return fetched


def sum_attn(term_fn, shard_rows):
    result = lax.psum_scatter(
        term_fn(jnp.int32(0), shard_rows * lax.axis_size(("fsdp", "rep"))),
        ("fsdp", "rep"),
        scatter_dimension=0,
        tiled=True,
    )
    return result


def sum_ffn(term_fn, shard_rows):
    result = lax.psum_scatter(
        term_fn(jnp.int32(0), shard_rows * lax.axis_size(("fsdp", "rep"))),
        ("fsdp", "rep"),
        scatter_dimension=0,
        tiled=True,
    )
    return result


def on_device(hidden_in, segment_ids, w_attn, w_ffn, gains, out_grad):
    inputs = hidden_in.astype(jnp.float32)
    tok_rows = inputs.shape[0]
    shard_rows = w_attn.shape[0]
    qkv_cols = D + 2 * KV * HD
    group = H // KV
    global_rows = lax.axis_index(("fsdp", "rep")) * tok_rows + jnp.arange(tok_rows, dtype=jnp.int32)
    positions = global_rows - segment_ids
    key_rows = global_rows[0] - tok_rows + jnp.arange(2 * tok_rows, dtype=jnp.int32)
    allowed = (segment_ids[:, None] <= key_rows[None, :]) & (
        key_rows[None, :] <= global_rows[:, None]
    )
    cosine, sine = rotary(positions)
    attn_full, gains_full = fetch_attn(w_attn, gains)
    normed_f, norm_one_back = jax.vjp(rms_norm, inputs, gains_full[0].astype(jnp.float32))
    normed = normed_f.astype(jnp.bfloat16)
    qkv = jnp.dot(normed, attn_full[:, :qkv_cols], preferred_element_type=jnp.float32)
    query = qkv[:, :D].reshape(tok_rows, KV, group, HD)
    keys = qkv[:, D : D + KV * HD].reshape(tok_rows, KV, HD)
    values = qkv[:, D + KV * HD :].reshape(tok_rows, KV, HD).astype(jnp.bfloat16)
    q_rot = rotate(query, cosine[:, None, None], sine[:, None, None]).astype(jnp.bfloat16)
    k_rot = rotate(keys, cosine[:, None], sine[:, None]).astype(jnp.bfloat16)
    earlier_keys, earlier_values = from_behind((k_rot, values), ("fsdp", "rep"), 1)
    keys_two = jnp.concatenate([earlier_keys, k_rot], axis=0)
    values_two = jnp.concatenate([earlier_values, values], axis=0)
    scores = masked_scores(q_rot, keys_two, allowed)
    row_max = jnp.max(scores, axis=-1, keepdims=True)
    expo = jnp.exp(scores - row_max)
    row_total = jnp.sum(expo, axis=-1, keepdims=True)
    log_total = row_max + jnp.log(row_total)
    probs = (expo / row_total).astype(jnp.bfloat16)
    mixed = jnp.einsum("krts,skd->tkrd", probs, values_two, preferred_element_type=jnp.float32)
    mixed = mixed.reshape(tok_rows, D).astype(jnp.bfloat16)
    residual = inputs + contract_cols(mixed, attn_full[:, qkv_cols:])
    normed_two_f, norm_two_back = jax.vjp(rms_norm, residual, gains_full[1].astype(jnp.float32))
    normed_two = normed_two_f.astype(jnp.bfloat16)
    ffn_full = fetch_ffn(w_ffn)
    gate_up = jnp.dot(normed_two, ffn_full[:, : 2 * FF], preferred_element_type=jnp.float32)
    activated, act_back = jax.vjp(swiglu, gate_up[:, :FF], gate_up[:, FF:])
    hidden = activated.astype(jnp.bfloat16)
    hidden_out = (residual + contract_cols(hidden, ffn_full[:, 2 * FF :])).astype(jnp.bfloat16)
    back_attn, unused_gains = fetch_attn(w_attn, gains)
    back_ffn = fetch_ffn(w_ffn)
    d_hidden = jnp.dot(out_grad, back_ffn[:, 2 * FF :], preferred_element_type=jnp.float32)
    d_gate, d_upward = act_back(d_hidden)
    d_gate_up = jnp.concatenate([d_gate, d_upward], axis=1).astype(jnp.bfloat16)
    d_normed_two = contract_cols(d_gate_up, back_ffn[:, : 2 * FF])
    d_resid_norm, d_gain_two = norm_two_back(d_normed_two)
    d_resid = out_grad.astype(jnp.float32) + d_resid_norm
    d_attended = d_resid.astype(jnp.bfloat16)

    def ffn_term(first_row, row_count):
        return jnp.concatenate(
            [contract_rows(normed_two, d_gate_up), contract_rows(out_grad, hidden)], axis=1
        )

    ffn_grad = sum_ffn(ffn_term, shard_rows)
    d_mixed = jnp.dot(d_attended, back_attn[:, qkv_cols:], preferred_element_type=jnp.float32)
    d_mixed = d_mixed.astype(jnp.bfloat16).reshape(tok_rows, KV, group, HD)
    scores_again = masked_scores(q_rot, keys_two, allowed)
    probs_full = jnp.exp(scores_again - log_total)
    d_probs = jnp.einsum("tkrd,skd->krts", d_mixed, values_two, preferred_element_type=jnp.float32)
    d_values_two = jnp.einsum(
        "krts,tkrd->skd",
        probs_full.astype(jnp.bfloat16),
        d_mixed,
        preferred_element_type=jnp.float32,
    )
    row_shift = jnp.sum(d_probs * probs_full, axis=-1, keepdims=True)
    d_scores = (probs_full * (d_probs - row_shift)).astype(jnp.bfloat16)
    d_q_rot = jnp.einsum(
        "krts,skd->tkrd", d_scores, keys_two, preferred_element_type=jnp.float32
    ) * HD ** (-0.5)
    d_k_two = jnp.einsum(
        "krts,tkrd->skd", d_scores, q_rot, preferred_element_type=jnp.float32
    ) * HD ** (-0.5)
    later_keys, later_values = (
        from_behind(d_k_two[:tok_rows].astype(jnp.bfloat16), ("fsdp", "rep"), -1).astype(
            jnp.float32
        ),
        from_behind(d_values_two[:tok_rows].astype(jnp.bfloat16), ("fsdp", "rep"), -1).astype(
            jnp.float32
        ),
    )
    d_k_rot = d_k_two[tok_rows:] + later_keys
    d_values = d_values_two[tok_rows:] + later_values
    d_query = rotate(d_q_rot, cosine[:, None, None], -sine[:, None, None])
    d_keys = rotate(d_k_rot, cosine[:, None], -sine[:, None])
    d_qkv = jnp.concatenate(
        [
            d_query.reshape(tok_rows, D),
            d_keys.reshape(tok_rows, KV * HD),
            d_values.reshape(tok_rows, KV * HD),
        ],
        axis=1,
    ).astype(jnp.bfloat16)
    d_normed = contract_cols(d_qkv, back_attn[:, :qkv_cols])
    d_input_norm, d_gain_one = norm_one_back(d_normed)
    in_grad = (d_resid + d_input_norm).astype(jnp.bfloat16)

    def attn_term(first_row, row_count):
        return jnp.concatenate(
            [contract_rows(normed, d_qkv), contract_rows(d_attended, mixed)], axis=1
        )

    attn_grad = sum_attn(attn_term, shard_rows)
    gains_grad = lax.psum_scatter(
        jnp.stack([d_gain_one, d_gain_two]), ("fsdp", "rep"), scatter_dimension=1, tiled=True
    )
    return (hidden_out, in_grad, attn_grad, ffn_grad, gains_grad)


def solution(mesh):
    in_specs = (
        P(("fsdp", "rep"), None),
        P(("fsdp", "rep")),
        P(("fsdp", "rep"), None),
        P(("fsdp", "rep"), None),
        P(None, ("fsdp", "rep")),
        P(("fsdp", "rep"), None),
    )
    out_specs = (
        P(("fsdp", "rep"), None),
        P(("fsdp", "rep"), None),
        P(("fsdp", "rep"), None),
        P(("fsdp", "rep"), None),
        P(None, ("fsdp", "rep")),
    )
    return jax.shard_map(
        on_device, mesh=mesh, in_specs=in_specs, out_specs=out_specs, check_vma=False
    )
```

profile of v0, /device:TPU:0, one launch (start us, length us, event | category | flops | bytes accessed | tf_op | source)
XLA Modules:
  0.0 3037.1 jit_solution(15099166013553156018)
XLA Ops:
  9.2 43.4 %all-gather = bf16[32,64,2]{1,2,0:T(2,128)(2,1)S(1)} all-gather(bf16[1,64,2]{1,2,0:T(2,128)(2,1)} %bitcast.125), channel_id=1, replica_groups=mesh['fsdp'=8,'rep'=4] {'fsdp','rep'}, dimensions={0}, use_global_device_ids=true | all-gather | bytes 8448 | tf_op jit(solution)/shard_map/all_gather | solution.py:67
  56.1 92.1 %all-gather.4.cloned.1.call-done = bf16[2048,5120]{1,0:T(8,128)(2,1)} async-done(((bf16[64,5120]{1,0:T(8,128)(2,1)}), bf16[2048,5120]{1,0:T(8,128)(2,1)}) %all-gather.4.cloned.1.call-update) | async-done | bytes 20971536 | tf_op jit(solution)/shard_map/all_gather | solution.py:66
  148.2 6.5 fusion.15
  170.4 7.2 fusion.84
  177.6 8.9 fusion.11
  186.6 8.9 fusion.54
  195.5 6.3 multiply_reduce_fusion.2
  202.6 467.3 %all-gather.6.cloned.1.call-done = bf16[2048,24576]{1,0:T(8,128)(2,1)} async-done(((bf16[64,24576]{1,0:T(8,128)(2,1)}), bf16[2048,24576]{1,0:T(8,128)(2,1)}) %all-gather.6.cloned.1.call-update) | async-done | bytes 100663312 | tf_op jit(solution)/shard_map/all_gather | solution.py:73
  669.8 31.3 %fusion.2 = f32[256,16384]{1,0:T(8,128)} fusion(bf16[2048,24576]{1,0:T(8,128)(2,1)} %all-gather.6.cloned.1.call-done, f32[256,2048]{1,0:T(8,128)S(1)} %get-tuple-element.31, f32[2048]{0:T(1024)S(1)} %bitcast.108, f32[256]{0:T(256)S(1)} %fusion.75), kind=kOutput, calls=%fused_computation.3 | convolution fusion | flops 17181442048 | bytes 85992448 | tf_op jit(solution)/shard_map/dot_general | solution.py:134
  701.2 24.6 fusion.19
  725.7 30.5 %multiply_reduce_fusion = (f32[2048]{0:T(1024)}, f32[256]{0:T(256)S(1)}, f32[256,2048]{1,0:T(8,128)}) fusion(f32[256,2048]{1,0:T(8,128)S(1)} %get-tuple-element.31, f32[256]{0:T(256)S(1)} %fusion.75, f32[2048]{0:T(1024)S(1)} %bitcast.109, bf16[2048,24576]{1,0:T(8,128)(2,1)} %all-gather.6.cloned.1.call-done, bf16[256,8192]{1,0:T(8,128)(2,1)} %get-tuple-element.10, ...), kind=kOutput, calls=%fused_computation.70 | convolution fusion | flops 17199790080 | bytes 79710208 | tf_op jit(solution)/shard_map/dot_general | solution.py:52
  758.5 8.2 fusion.66
  773.1 8.2 fusion.55
  784.6 12.4 fusion.8
  797.0 7.7 fusion.10
  813.9 10.9 fusion.60
  824.8 10.3 fusion.44
  836.7 27.8 pad_maximum_fusion.1
  865.7 25.6 convolution_bitcast_fusion
  891.3 47.1 %fusion.29 = f32[2048,16384]{1,0:T(8,128)} fusion(bf16[256,8192]{1,0:T(8,128)(2,1)} %get-tuple-element.10, bf16[256,8192]{1,0:T(8,128)(2,1)} %get-tuple-element.9, f32[256,2048]{1,0:T(8,128)S(1)} %copy-done.8, f32[2048]{0:T(1024)S(1)} %bitcast.111, f32[256]{0:T(256)S(1)} %fusion.75), kind=kOutput, calls=%fused_computation.42 | convolution fusion | flops 17198219264 | bytes 144712704 | tf_op jit(solution)/shard_map/dot_general | solution.py:46
  938.4 132.1 %pad_maximum_fusion = f32[2048,24576]{1,0:T(8,128)} fusion(f32[2048,8192]{1,0:T(8,128)} %convolution_bitcast_fusion, f32[2048,16384]{1,0:T(8,128)} %fusion.29), kind=kLoop, calls=%fused_computation | loop fusion | flops 50331648 | bytes 402653184 | tf_op jit(solution)/shard_map/concatenate | solution.py:149
  1070.6 18.0 fusion.35
  1093.2 323.3 %reduce-scatter.6.cloned.1.call-done = f32[64,5120]{1,0:T(8,128)} async-done(((f32[2048,5120]{1,0:T(8,128)}), f32[64,5120]{1,0:T(8,128)}) %reduce-scatter.6.cloned.1.call-update) | async-done | bytes 1310736 | tf_op jit(solution)/shard_map/reduce_scatter | solution.py:78
  1416.6 1613.7 %reduce-scatter.8.cloned.1.call-done = f32[64,24576]{1,0:T(8,128)} async-done(((f32[2048,24576]{1,0:T(8,128)}), f32[64,24576]{1,0:T(8,128)}) %reduce-scatter.8.cloned.1.call-update) | async-done | bytes 6291472 | tf_op jit(solution)/shard_map/reduce_scatter | solution.py:88
  (146 shorter events, 49.4 us)
Async XLA Ops:
  7.2 48.7 %copy-start.35 = (s32[256]{0:T(256)S(1)}, s32[256]{0:T(256)}, u32[]{:S(2)}) copy-start(s32[256]{0:T(256)} %param.7) | copy-start | bytes 3076
  7.2 47.8 %copy-start.4 = (bf16[256,2048]{1,0:T(8,128)(2,1)S(1)}, bf16[256,2048]{1,0:T(8,128)(2,1)}, u32[]{:S(2)}) copy-start(bf16[256,2048]{1,0:T(8,128)(2,1)} %param.6) | copy-start | bytes 3145732
  7.2 141.0 %all-gather.4.cloned.1.call-start = ((), (), s32[]{:S(2)}) async-start(), calls=%async_computation.3 | async-start | bytes 21626880 | tf_op jit(solution)/shard_map/all_gather | solution.py:66
  7.9 661.9 %all-gather.6.cloned.1.call-start = ((), (), s32[]{:S(2)}) async-start(), calls=%async_computation.4 | async-start | bytes 103809024 | tf_op jit(solution)/shard_map/all_gather | solution.py:73
  8.7 1083.2 %reduce-scatter.10.cloned.1.call-start = ((), (), s32[]{:S(2)}) async-start(), calls=%async_computation.7 | async-start | bytes 1081344
  55.9 98.8 %copy-start.29 = (f32[256]{0:T(256)}, f32[256]{0:T(256)S(1)}, u32[]{:S(2)}) copy-start(f32[256]{0:T(256)S(1)} %fusion.74) | copy-start | bytes 3076
  56.1 98.6 %copy-start.26 = (f32[1,2048]{1,0:T(1,128)}, f32[1,2048]{1,0:T(1,128)S(1)}, u32[]{:S(2)}) copy-start(f32[1,2048]{1,0:T(1,128)S(1)} %get-tuple-element.25) | copy-start | bytes 24580
  157.2 29.4 copy-start.17
  157.2 29.4 collective-permute-start
  166.8 3.6 collective-permute-start.1
  201.8 554.4 %copy-start.7 = (f32[256,2048]{1,0:T(8,128)}, f32[256,2048]{1,0:T(8,128)S(1)}, u32[]{:S(2)}) copy-start(f32[256,2048]{1,0:T(8,128)S(1)} %get-tuple-element.31) | copy-start | bytes 6291460
  669.8 31.3 %copy-start.9 = (bf16[256,2048]{1,0:T(8,128)(2,1)S(1)}, bf16[256,2048]{1,0:T(8,128)(2,1)}, u32[]{:S(2)}) copy-start(bf16[256,2048]{1,0:T(8,128)(2,1)} %param.11) | copy-start | bytes 3145732
  773.0 23.9 slice-start
  773.1 23.9 slice-start.1
  783.0 29.8 collective-permute-start.3
  809.1 3.5 collective-permute-start.2
  836.6 580.0 %reduce-scatter.6.cloned.1.call-start = ((), (), s32[]{:S(2)}) async-start(), calls=%async_computation.5 | async-start | bytes 43253760 | tf_op jit(solution)/shard_map/reduce_scatter | solution.py:78
  864.5 2165.8 %reduce-scatter.8.cloned.1.call-start = ((), (), s32[]{:S(2)}) async-start(), calls=%async_computation.6 | async-start | bytes 207618048 | tf_op jit(solution)/shard_map/reduce_scatter | solution.py:88
  865.7 25.6 copy-start.8
  1070.5 18.1 copy-start.33
  1070.5 18.1 copy-start.3
  1070.5 18.1 copy-start.6
  1070.6 18.1 copy-start.28
  1070.6 18.1 copy-start.31
  (26 other events, 143.4 us)
Sparse Core Ops, SparseCore 0:
  10.9 137.2 all-gather.3
  151.1 518.7 all-gather.5
  836.7 139.1 reduce-scatter.9
  978.7 437.8 reduce-scatter.5
  1424.6 1605.6 reduce-scatter.7
where the time goes:
time: 3040 us
  waiting for transfers between devices  2500 us (82%)
  matrix products  266 us (9%)
  other arithmetic  190 us (6%)
  blocking collectives  43.4 us (1%)
    reduce_scatter x1, waiting for transfers between devices, sum_ffn(): lax.psum_scatter(term_fn(jnp.int32(0), shard_rows * lax.axis_size(('fsdp'...  1610 us
    all_gather x1, waiting for transfers between devices, fetch_ffn(): fetched = lax.all_gather(w_ffn, ('fsdp', 'rep'), axis=0, tiled=True)  467 us
    reduce_scatter x1, waiting for transfers between devices, sum_attn(): lax.psum_scatter(term_fn(jnp.int32(0), shard_rows * lax.axis_size(('fsdp'...  323 us
    concatenate x1, other arithmetic, ffn_term(): jnp.concatenate([contract_rows(normed_two, d_gate_up), contract_rows(out_...  132 us
    all_gather x1, waiting for transfers between devices, fetch_attn(): lax.all_gather(w_attn, ('fsdp', 'rep'), axis=0, tiled=True)  92.1 us
    dot_general x4, matrix products, contract_rows(): lax.dot_general(left, right, (((0,), (0,)), ((), ())), preferred_element_...  91.7 us
    dot_general x4, matrix products, contract_cols(): lax.dot_general(left, right, (((1,), (1,)), ((), ())), preferred_element_...  65.2 us
  transfers between devices with their start and end apart: 9, of which 6 were waited for; matrix products, arithmetic and copies ran while one was open for 11% of the time, Pallas kernels for 0%

commit v1 on v0

v1 whole, which is shorter than its diff:
```python
import jax
import jax.numpy as jnp
from jax import lax
from jax.sharding import Mesh, PartitionSpec as P

D = 2048
H = 32
KV = 8
HD = 64
FF = 8192
GROUP = H // KV
TP = 8
CHUNKS = 4

NORM_EPS = 1e-05
ROPE_BASE = 500000.0

PLANE = ("y", "x", "c")
EVERY = ("z", "y", "x", "c")
BF = jnp.bfloat16
F32 = jnp.float32


def swap(value, rel):
    return lax.ppermute(value, PLANE, [(i, i ^ rel) for i in range(TP)])


def gather_plane(own):
    half = own.shape[0] // 2
    blk = [own] + [None] * 7
    blk[2] = swap(own, 2)
    blk[4] = swap(own, 4)
    blk[1] = swap(own, 1)
    first = swap(blk[2][:half], 4)
    second = swap(blk[4][half:], 2)
    blk[3] = swap(blk[2], 1)
    blk[5] = swap(blk[4], 1)
    blk[6] = jnp.concatenate([first, second], axis=0)
    blk[7] = swap(blk[6], 1)
    return blk


def scatter_plane(parts):
    half = parts.shape[1] // 2
    arrived = swap(parts[1::2], 1)
    both = (parts[0::2].astype(F32) + arrived.astype(F32)).astype(BF)
    from_x = swap(both[3, :half], 2)
    from_y = swap(both[3, half:], 4)
    x_first = swap(both[1, :half], 2)
    y_second = swap(both[2, half:], 4)
    y_first = swap((both[2, :half].astype(F32) + from_x.astype(F32)).astype(BF), 4)
    x_second = swap((both[1, half:].astype(F32) + from_y.astype(F32)).astype(BF), 2)
    x_part = jnp.concatenate([x_first, x_second], axis=0).astype(F32)
    y_part = jnp.concatenate([y_first, y_second], axis=0).astype(F32)
    return both[0].astype(F32) + x_part + y_part


def exchange(blocks):
    return [blocks[0]] + [swap(blocks[r], r) for r in range(1, TP)]


def along_z(value, steps):
    count = lax.axis_size("z")
    return lax.ppermute(
        value, "z", [(i, i + steps) for i in range(count) if 0 <= i + steps < count]
    )


def fetch(pieces):
    rows, cols = pieces.shape[1:]
    mine = lax.all_to_all(pieces, PLANE, 0, 0, tiled=True).reshape(TP * rows, cols)
    return lax.all_gather(mine, "z", axis=0, tiled=True)


def give_back(grad):
    cols = grad.shape[1]
    summed = lax.psum_scatter(grad.astype(BF), "z", scatter_dimension=0, tiled=True)
    return lax.all_to_all(
        summed.reshape(TP, summed.shape[0] // TP, cols), PLANE, 0, 0, tiled=True
    )


def rms_norm(values, scales):
    return values * lax.rsqrt(jnp.mean(values * values, axis=-1, keepdims=True) + NORM_EPS) * scales


def rotary(positions):
    freqs = 1.0 / ROPE_BASE ** (jnp.arange(HD // 2, dtype=F32) * (2.0 / HD))
    angles = positions.astype(F32)[..., None] * freqs
    return jnp.cos(angles), jnp.sin(angles)


def turn(first, second, cosine, sine):
    return first * cosine - second * sine, second * cosine + first * sine


def mm(left, right, dims):
    return lax.dot_general(left, right, (dims, ((), ())), preferred_element_type=F32)


def on_device(hidden_in, segment_ids, w_attn, w_ffn, gains, out_grad):
    tok = hidden_in.shape[0]
    rows = w_attn.shape[0]
    me = lax.axis_index(PLANE)
    z = lax.axis_index("z")
    kv_cols = KV * HD
    qkv_cols = D + 2 * kv_cols
    tokens = TP * tok
    rel = me ^ jnp.arange(TP, dtype=jnp.int32)

    w_q = w_attn[:, :D].reshape(rows, TP, GROUP, 2, HD // 2).transpose(1, 0, 3, 2, 4)
    w_q = w_q.reshape(TP, rows, GROUP * HD)
    w_k = w_attn[:, D : D + kv_cols].reshape(rows, TP, HD).transpose(1, 0, 2)
    w_v = w_attn[:, D + kv_cols : qkv_cols].reshape(rows, TP, HD).transpose(1, 0, 2)
    w_o = w_attn[:, qkv_cols:].reshape(rows, TP, GROUP * HD).transpose(1, 0, 2)
    wqkv = fetch(jnp.concatenate([w_q, w_k, w_v], axis=2))
    wo = fetch(w_o)
    step = FF // TP // CHUNKS
    ffn_cut = w_ffn.reshape(rows, 3, CHUNKS, TP, step).transpose(2, 3, 0, 1, 4)
    ffn = [fetch(ffn_cut[j].reshape(TP, rows, 3 * step)) for j in range(CHUNKS)]

    gains_full = lax.all_gather(gains, EVERY, axis=1, tiled=True).astype(F32)
    seg_all = lax.all_gather(segment_ids, PLANE, axis=0, tiled=True).reshape(TP, tok)
    seg_rel = jnp.take(seg_all, rel, axis=0)
    starts = (z * TP + rel) * tok
    positions = starts[:, None] + jnp.arange(tok, dtype=jnp.int32)[None] - seg_rel
    cosine, sine = rotary(positions.reshape(tokens))

    x_all = jnp.concatenate(gather_plane(hidden_in), axis=0).astype(F32)
    normed = rms_norm(x_all, gains_full[0]).astype(BF)
    qkv = mm(normed, wqkv, ((1,), (0,)))
    half = HD // 2
    q4 = qkv[:, : GROUP * HD].reshape(tokens, 2, GROUP, half)
    qa, qb = turn(q4[:, 0], q4[:, 1], cosine[:, None], sine[:, None])
    q_rot = jnp.concatenate([qa, qb], axis=-1).astype(BF)
    k_raw = qkv[:, GROUP * HD : GROUP * HD + HD]
    ka, kb = turn(k_raw[:, :half], k_raw[:, half:], cosine, sine)
    k_rot = jnp.concatenate([ka, kb], axis=-1).astype(BF)
    v = qkv[:, GROUP * HD + HD :].astype(BF)
    kv = jnp.concatenate([k_rot, v], axis=1).reshape(TP, tok, 2 * HD)
    last = jnp.take(kv, me ^ (TP - 1), axis=0)
    before = along_z(last, 1)
    kv9 = jnp.concatenate([kv, before[None]], axis=0)
    prev_at = jnp.where(rel == 0, TP, (rel - 1) ^ me)
    kv_prev = jnp.take(kv9, prev_at, axis=0)
    kv_two = jnp.concatenate([kv_prev, kv], axis=1)
    k_two, v_two = kv_two[..., :HD], kv_two[..., HD:]
    lo = seg_rel - starts[:, None] + tok
    key_at = jnp.arange(2 * tok, dtype=jnp.int32)
    allowed = (lo[:, :, None] <= key_at) & (key_at <= jnp.arange(tok, dtype=jnp.int32)[:, None] + tok)
    q_blk = q_rot.reshape(TP, tok, GROUP, HD)

    def scores():
        s = jnp.einsum("btrd,bsd->brts", q_blk, k_two, preferred_element_type=F32) * HD ** (-0.5)
        return jnp.where(allowed[:, None], s, -1e30)

    s = scores()
    row_max = jnp.max(s, axis=-1, keepdims=True)
    expo = jnp.exp(s - row_max)
    total = jnp.sum(expo, axis=-1, keepdims=True)
    lse = row_max + jnp.log(total)
    probs = (expo / total).astype(BF)
    mixed = jnp.einsum("brts,bsd->btrd", probs, v_two, preferred_element_type=F32)
    mixed = mixed.astype(BF).reshape(TP, tok, GROUP * HD)

    wo_rel = jnp.concatenate(gather_plane(wo), axis=1)
    o_mine = jnp.concatenate(exchange([mixed[r] for r in range(TP)]), axis=1)
    x_own = hidden_in.astype(F32)
    residual = x_own + mm(o_mine, wo_rel, ((1,), (1,)))
    normed_two, norm_two_back = jax.vjp(rms_norm, residual, gains_full[1])
    n2 = jnp.concatenate(gather_plane(normed_two.astype(BF)), axis=0)
    dy = jnp.concatenate(gather_plane(out_grad), axis=0)

    acts, d_gus, ffn_grads = [], [], []
    for w in ffn:
        gate_up = mm(n2, w[:, : 2 * step], ((1,), (0,)))
        d_act = mm(dy, w[:, 2 * step :], ((1,), (0,)))
        g, u = gate_up[:, :step], gate_up[:, step:]
        sg = jax.nn.sigmoid(g)
        act = (g * sg * u).astype(BF)
        d_g = (d_act * u * (sg * (1.0 + g * (1.0 - sg)))).astype(BF)
        d_u = (d_act * g * sg).astype(BF)
        d_gu = jnp.concatenate([d_g, d_u], axis=1)
        acts.append(act)
        d_gus.append(d_gu)
        grad = jnp.concatenate([mm(n2, d_gu, ((0,), (0,))), mm(dy, act, ((0,), (0,)))], axis=1)
        ffn_grads.append(give_back(grad))
    w_all = jnp.concatenate([w[:, : 2 * step] for w in ffn], axis=1)
    wd_all = jnp.concatenate([w[:, 2 * step :] for w in ffn], axis=1)
    d_n2 = mm(jnp.concatenate(d_gus, axis=1), w_all, ((1,), (1,))).astype(BF)
    d_normed_two = scatter_plane(d_n2.reshape(TP, tok, D))
    f_out = mm(jnp.concatenate(acts, axis=1), wd_all, ((1,), (1,))).astype(BF)
    hidden_out = (residual + scatter_plane(f_out.reshape(TP, tok, D))).astype(BF)

    d_resid_norm, d_gain_two = norm_two_back(d_normed_two)
    d_resid = out_grad.astype(F32) + d_resid_norm
    d_att = d_resid.astype(BF)
    d_mixed = mm(d_att, wo_rel, ((1,), (0,))).astype(BF).reshape(tok, TP, GROUP * HD)
    d_o = jnp.stack(exchange([d_mixed[:, r] for r in range(TP)]), axis=0)
    d_att_all = jnp.concatenate(gather_plane(d_att), axis=0)
    wo_grad = give_back(mm(d_att_all, mixed.reshape(tokens, GROUP * HD), ((0,), (0,))))

    d_o = d_o.reshape(TP, tok, GROUP, HD)
    p_full = jnp.exp(scores() - lse)
    d_p = jnp.einsum("btrd,bsd->brts", d_o, v_two, preferred_element_type=F32)
    d_v_two = jnp.einsum("brts,btrd->bsd", p_full.astype(BF), d_o, preferred_element_type=F32)
    shift = jnp.sum(d_p * p_full, axis=-1, keepdims=True)
    d_s = (p_full * (d_p - shift)).astype(BF)
    d_q = jnp.einsum("brts,bsd->btrd", d_s, k_two, preferred_element_type=F32) * HD ** (-0.5)
    d_k_two = jnp.einsum("brts,btrd->bsd", d_s, q_blk, preferred_element_type=F32) * HD ** (-0.5)
    d_kv_two = jnp.concatenate([d_k_two, d_v_two], axis=2)
    d_prev = d_kv_two[:, :tok]
    back = along_z(jnp.take(d_prev, me, axis=0).astype(BF), -1).astype(F32)
    d_prev9 = jnp.concatenate([d_prev, back[None]], axis=0)
    next_at = jnp.where(rel == TP - 1, TP, (rel + 1) ^ me)
    d_kv = (d_kv_two[:, tok:] + jnp.take(d_prev9, next_at, axis=0)).reshape(tokens, 2 * HD)
    d_q = d_q.reshape(tokens, GROUP, HD)
    dqa, dqb = turn(d_q[..., :half], d_q[..., half:], cosine[:, None], -sine[:, None])
    dka, dkb = turn(d_kv[:, :half], d_kv[:, half:HD], cosine, -sine)
    d_qkv = jnp.concatenate(
        [
            dqa.reshape(tokens, GROUP * half),
            dqb.reshape(tokens, GROUP * half),
            dka,
            dkb,
            d_kv[:, HD:],
        ],
        axis=1,
    ).astype(BF)
    d_n1 = mm(d_qkv, wqkv, ((1,), (1,))).astype(BF)
    d_normed = scatter_plane(d_n1.reshape(TP, tok, D))
    qkv_grad = give_back(mm(normed, d_qkv, ((0,), (0,))))
    unused, norm_one_back = jax.vjp(rms_norm, x_own, gains_full[0])
    d_in_norm, d_gain_one = norm_one_back(d_normed)
    in_grad = (d_resid + d_in_norm).astype(BF)
    gains_grad = lax.psum_scatter(
        jnp.stack([d_gain_one, d_gain_two]), EVERY, scatter_dimension=1, tiled=True
    )

    g_q = qkv_grad[:, :, : GROUP * HD].reshape(TP, rows, 2, GROUP, half).transpose(1, 0, 3, 2, 4)
    g_k = qkv_grad[:, :, GROUP * HD : GROUP * HD + HD].transpose(1, 0, 2)
    g_v = qkv_grad[:, :, GROUP * HD + HD :].transpose(1, 0, 2)
    attn_grad = jnp.concatenate(
        [
            g_q.reshape(rows, D),
            g_k.reshape(rows, kv_cols),
            g_v.reshape(rows, kv_cols),
            wo_grad.transpose(1, 0, 2).reshape(rows, D),
        ],
        axis=1,
    ).astype(F32)
    f_stack = jnp.stack(ffn_grads, axis=0).reshape(CHUNKS, TP, rows, 3, step)
    ffn_grad = f_stack.transpose(2, 3, 0, 1, 4).reshape(rows, 3 * FF).astype(F32)
    return hidden_out, in_grad, attn_grad, ffn_grad, gains_grad


def solution(mesh):
    fine = Mesh(mesh.devices.reshape(-1, 2, 2, 2), EVERY)
    rows = P(EVERY, None)
    in_specs = (rows, P(EVERY), rows, rows, P(None, EVERY), rows)
    out_specs = (rows, rows, rows, rows, P(None, EVERY))
    return jax.shard_map(
        on_device, mesh=fine, in_specs=in_specs, out_specs=out_specs, check_vma=False
    )
```

time: 3040 us -> 1110 us (0.37)
  waiting for transfers between devices: 2500 us -> 285 us
  local copies, waits for them, and re-layouts: 14.2 us -> 195 us
  blocking collectives: 43.4 us -> 163 us
  starting transfers between devices: 9.19 us -> 93.9 us
  other arithmetic: 190 us -> 107 us
    reduce_scatter x2 -> x6, waiting for transfers between devices: 1940 us -> 0.05 us  [give_back(): lax.psum_scatter(grad.astype(BF), 'z', scatter_dimension=0, tiled=True)]
    all_gather x2 -> x6, waiting for transfers between devices: 559 us -> 0.03 us  [fetch(): return lax.all_gather(mine, 'z', axis=0, tiled=True)]
    concatenate x2 -> x15, other arithmetic: 160 us -> 15.2 us  [the longest x4 7.59 us: on_device(): jnp.concatenate([mm(n2, d_gu, ((0,), (0,))), mm(dy, act, ((0,), (0,)))],...]
    ppermute x4 -> x77, waiting for transfers between devices: 1.64 us -> 139 us  [the longest x75 139 us: swap(): return lax.ppermute(value, PLANE, [(i, i ^ rel) for i in range(TP)])]
    unnamed x6 -> x14, waiting for transfers between devices: 1.43 us -> 131 us
    unnamed x85 -> x248, local copies, waits for them, and re-layouts: 5.48 us -> 105 us
    all_to_all x0 -> x5, blocking collectives: none -> 72.8 us  [fetch(): lax.all_to_all(pieces, PLANE, 0, 0, tiled=True).reshape(TP * rows, cols)]
    ppermute x4 -> x77, starting transfers between devices: 8.74 us -> 64.9 us  [the longest x75 61.9 us: swap(): return lax.ppermute(value, PLANE, [(i, i ^ rel) for i in range(TP)])]
  transfers between devices with their start and end apart: 9 -> 97, of which waited for: 6 -> 26; matrix products, arithmetic and copies ran while one was open for 11% -> 41% of each run, Pallas kernels for 0% -> 0%
where the time goes in v1:
time: 1110 us; the launch traced here: 1100 us
  waiting for transfers between devices  285 us (26%)
  matrix products  236 us (21%)
  local copies, waits for them, and re-layouts  195 us (18%)
  blocking collectives  163 us (15%)
  other arithmetic  107 us (10%)
  starting transfers between devices  93.9 us (8%)
  between operations  16.6 us (1%)
    dot_general x24, matrix products, mm(): lax.dot_general(left, right, (dims, ((), ())), preferred_element_type=F32)  186 us
    ppermute x75, waiting for transfers between devices, swap(): return lax.ppermute(value, PLANE, [(i, i ^ rel) for i in range(TP)])  139 us
    unnamed x14, waiting for transfers between devices  131 us
    unnamed x248, local copies, waits for them, and re-layouts  105 us
    all_to_all x5, blocking collectives, fetch(): lax.all_to_all(pieces, PLANE, 0, 0, tiled=True).reshape(TP * rows, cols)  72.8 us
    ppermute x75, starting transfers between devices, swap(): return lax.ppermute(value, PLANE, [(i, i ^ rel) for i in range(TP)])  61.9 us
    all_gather x1, blocking collectives, on_device(): lax.all_gather(segment_ids, PLANE, axis=0, tiled=True).reshape(TP, tok)  51 us
    all_gather x1, blocking collectives, on_device(): gains_full = lax.all_gather(gains, EVERY, axis=1, tiled=True).astype(F32)  39.4 us
  transfers between devices with their start and end apart: 97, of which 26 were waited for; matrix products, arithmetic and copies ran while one was open for 41% of the time, Pallas kernels for 0%

profile of v1, /device:TPU:0, one launch (start us, length us, event | category | flops | bytes accessed | tf_op | source)
XLA Modules:
  0.0 1096.8 jit_solution(3764443822516946717)
XLA Ops:
  8.4 12.3 %all_to_all.60 = bf16[8,64,256]{2,1,0:T(8,128)(2,1)} all-to-all(bf16[8,64,256]{2,1,0:T(8,128)(2,1)S(1)} %copy.243), channel_id=1, replica_groups=mesh['z'=4,'y'=2,'x'=2,'c'=2] {'y','x','c'}, dimensions={0} | all-to-all | bytes 524288 | tf_op jit(solution)/shard_map/all_to_all | solution.py:71
  28.3 11.4 %all_to_all.61 = bf16[8,64,384]{2,1,0:T(8,128)(2,1)} all-to-all(bf16[8,64,384]{2,1,0:T(8,128)(2,1)S(1)} %copy.233), channel_id=1, replica_groups=mesh['z'=4,'y'=2,'x'=2,'c'=2] {'y','x','c'}, dimensions={0} | all-to-all | bytes 786432 | tf_op jit(solution)/shard_map/all_to_all | solution.py:71
  47.2 15.6 %all_to_all.62 = bf16[8,64,768]{2,1,0:T(8,128)(2,1)} all-to-all(bf16[8,64,768]{2,1,0:T(8,128)(2,1)S(1)} %reshape_squeeze.12), channel_id=1, replica_groups=mesh['z'=4,'y'=2,'x'=2,'c'=2] {'y','x','c'}, dimensions={0} | all-to-all | bytes 1572864 | tf_op jit(solution)/shard_map/all_to_all | solution.py:71
  66.4 16.8 %all_to_all.63 = bf16[8,64,768]{2,1,0:T(8,128)(2,1)} all-to-all(bf16[8,64,768]{2,1,0:T(8,128)(2,1)} %reshape_squeeze.13), channel_id=1, replica_groups=mesh['z'=4,'y'=2,'x'=2,'c'=2] {'y','x','c'}, dimensions={0} | all-to-all | bytes 1572864 | tf_op jit(solution)/shard_map/all_to_all | solution.py:71
  86.6 16.7 %all_to_all.64 = bf16[8,64,768]{2,1,0:T(8,128)(2,1)} all-to-all(bf16[8,64,768]{2,1,0:T(8,128)(2,1)} %reshape_squeeze.14), channel_id=1, replica_groups=mesh['z'=4,'y'=2,'x'=2,'c'=2] {'y','x','c'}, dimensions={0} | all-to-all | bytes 1572864 | tf_op jit(solution)/shard_map/all_to_all | solution.py:71
  111.4 51.0 %all-gather.1 = s32[8,1,256]{2,1,0:T(1,128)S(1)} all-gather(s32[1,1,256]{2,1,0:T(1,128)S(1)} %bitcast.425), channel_id=1, replica_groups=mesh['z'=4,'y'=2,'x'=2,'c'=2] {'y','x','c'}, dimensions={0}, use_global_device_ids=true | all-gather | bytes 9216 | tf_op jit(solution)/shard_map/all_gather | solution.py:123
  162.4 39.4 %all-gather = bf16[32,64,2]{1,2,0:T(2,128)(2,1)S(1)} all-gather(bf16[1,64,2]{1,2,0:T(2,128)(2,1)S(1)} %bitcast.426), channel_id=1, replica_groups=mesh['z'=4,'y'=2,'x'=2,'c'=2] {'z','y','x','c'}, dimensions={0}, use_global_device_ids=true | all-gather | bytes 8448 | tf_op jit(solution)/shard_map/all_gather | solution.py:122
  294.2 8.8 fusion.6
  326.0 10.2 collective-permute-done.13
  343.4 13.6 %collective-permute-done.15 = bf16[256,256]{0,1:T(8,128)(2,1)S(1)} collective-permute-done((bf16[256,256]{0,1:T(8,128)(2,1)S(1)}, bf16[256,256]{0,1:T(8,128)(2,1)S(1)}, u32[]{:S(2)}, u32[]{:S(2)}) %collective-permute-start.15) | collective-permute-done | bytes 131104 | tf_op jit(solution)/shard_map/ppermute | solution.py:25
  382.1 17.4 %collective-permute-done.25 = bf16[256,2048]{1,0:T(8,128)(2,1)S(1)} collective-permute-done((bf16[256,2048]{1,0:T(8,128)(2,1)}, bf16[256,2048]{1,0:T(8,128)(2,1)S(1)}, u32[]{:S(2)}, u32[]{:S(2)}) %collective-permute-start.25) | collective-permute-done | bytes 1048608 | tf_op jit(solution)/shard_map/ppermute | solution.py:25
  490.3 12.1 %convolution_convert_fusion.1 = bf16[2048,2048]{1,0:T(8,128)(2,1)S(1)} fusion(bf16[2048,256]{0,1:T(8,128)(2,1)} %multiply_convert_fusion.8, bf16[2048,256]{0,1:T(8,128)(2,1)} %multiply_convert_fusion.9, bf16[2048,256]{0,1:T(8,128)(2,1)} %multiply_convert_fusion.10, bf16[2048,256]{0,1:T(8,128)(2,1)} %copy-done.44, bf16[2048,256]{1,0:T(8,128)(2,1)} %slice.477, ...), kind=kOutput, calls=%fused_computation.36 | convolution fusion | flops 8627683328 | bytes 16777216 | tf_op jit(solution)/shard_map/dot_general | solution.py:98
  533.4 9.1 constant_dynamic-update-slice_fusion.46
  544.9 9.0 constant_dynamic-update-slice_fusion.44
  557.2 21.0 %fusion.20 = bf16[2048,2048]{1,0:T(8,128)(2,1)S(1)} fusion(bf16[2048,2048]{0,1:T(8,128)(2,1)} %get-tuple-element.59, bf16[2048,512]{1,0:T(8,128)(2,1)S(1)} %slice-done.9, bf16[2048,512]{1,0:T(8,128)(2,1)S(1)} %slice-done.6, bf16[2048,512]{1,0:T(8,128)(2,1)S(1)} %slice-done.7, bf16[2048,512]{1,0:T(8,128)(2,1)S(1)} %slice-done.8), kind=kOutput, calls=%fused_computation.34 | convolution fusion | flops 17217617920 | bytes 25165824 | tf_op jit(solution)/shard_map/dot_general | solution.py:98
  591.0 8.8 convolution_convert_fusion.3
  637.4 9.3 collective-permute-done.33
  648.7 9.2 collective-permute-done.48
  669.1 10.1 collective-permute-done.50
  698.0 23.6 %collective-permute-done.55 = bf16[256,256]{1,0:T(8,128)(2,1)S(1)} collective-permute-done((bf16[256,256]{1,0:T(8,128)(2,1)S(1)}, bf16[256,256]{1,0:T(8,128)(2,1)S(1)}, u32[]{:S(2)}, u32[]{:S(2)}) %collective-permute-start.55) | collective-permute-done | bytes 131104 | tf_op jit(solution)/shard_map/ppermute | solution.py:25
  735.0 14.9 %fusion.3 = (f32[8,4,256]{2,1,0:T(4,128)}, f32[8,512,256,4]{2,1,3,0:T(8,128)}) fusion(f32[8,4,256,512]{2,3,1,0:T(8,128)} %get-tuple-element.139, f32[8,4,256]{2,1,0:T(4,128)} %bitcast.382, bf16[8,256,4,64]{1,3,2,0:T(8,128)(2,1)S(1)} %constant_dynamic-update-slice_fusion.51, bf16[8,256,128]{1,2,0:T(8,128)(2,1)} %copy-done.18, bf16[8,256,128]{1,2,0:T(8,128)(2,1)} %bitcast.337), kind=kOutput, calls=%fused_computation.10 | convolution fusion | flops 550494208 | bytes 35717120 | tf_op jit(solution)/shard_map/btrd,bsd->brts/dot_general | solution.py:205
  751.7 10.1 fusion.5
  830.5 10.1 convolution_convert_fusion.6
  957.1 131.2 %reduce-scatter.22.cloned.1.call-done = f32[64,2]{1,0:T(8,128)} async-done(((f32[2048,2]{1,0:T(8,128)}), f32[64,2]{1,0:T(8,128)}) %reduce-scatter.22.cloned.1.call-update) | async-done | bytes 528
  (635 shorter events, 588.5 us)
Async XLA Ops:
  7.2 239.4 %all-gather.11.cloned.1.call-start = ((), (), s32[]{:S(2)}) async-start(), calls=%async_computation.20 | async-start | bytes 1310720 | tf_op jit(solution)/shard_map/all_gather | solution.py:72
  20.7 244.0 %all-gather.9.cloned.1.call-start = ((), (), s32[]{:S(2)}) async-start(), calls=%async_computation.19 | async-start | bytes 1966080 | tf_op jit(solution)/shard_map/all_gather | solution.py:72
  39.8 365.4 %all-gather.13.cloned.1.call-start = ((), (), s32[]{:S(2)}) async-start(), calls=%async_computation.21 | async-start | bytes 3932160 | tf_op jit(solution)/shard_map/all_gather | solution.py:72
  62.9 344.6 %all-gather.15.cloned.1.call-start = ((), (), s32[]{:S(2)}) async-start(), calls=%async_computation.22 | async-start | bytes 3932160 | tf_op jit(solution)/shard_map/all_gather | solution.py:72
  83.2 326.5 %all-gather.17.cloned.1.call-start = ((), (), s32[]{:S(2)}) async-start(), calls=%async_computation.23 | async-start | bytes 3932160 | tf_op jit(solution)/shard_map/all_gather | solution.py:72
  103.4 105.5 %collective-permute-start.1 = (bf16[256,2048]{1,0:T(8,128)(2,1)S(1)}, bf16[256,2048]{1,0:T(8,128)(2,1)}, u32[]{:S(2)}, u32[]{:S(2)}) collective-permute-start(bf16[256,2048]{1,0:T(8,128)(2,1)S(1)} %copy-done.3), channel_id=1, source_target_pairs={{0,2},{1,3},{2,0},{3,1},{4,6},{5,7},{6,4},{7,5},{8,10},{9,11},{10,... | collective-permute-start | bytes 3145736 | tf_op jit(solution)/shard_map/ppermute | solution.py:25
  104.1 110.4 %collective-permute-start = (bf16[256,2048]{1,0:T(8,128)(2,1)S(1)}, bf16[256,2048]{1,0:T(8,128)(2,1)}, u32[]{:S(2)}, u32[]{:S(2)}) collective-permute-start(bf16[256,2048]{1,0:T(8,128)(2,1)S(1)} %copy-done.3), channel_id=1, source_target_pairs={{0,1},{1,0},{2,3},{3,2},{4,5},{5,4},{6,7},{7,6},{8,9},{9,8},{10,11... | collective-permute-start | bytes 3145736 | tf_op jit(solution)/shard_map/ppermute | solution.py:25
  104.1 107.2 %collective-permute-start.3 = (bf16[256,2048]{1,0:T(8,128)(2,1)S(1)}, bf16[256,2048]{1,0:T(8,128)(2,1)}, u32[]{:S(2)}, u32[]{:S(2)}) collective-permute-start(bf16[256,2048]{1,0:T(8,128)(2,1)S(1)} %copy-done.3), channel_id=1, source_target_pairs={{0,4},{1,5},{2,6},{3,7},{4,0},{5,1},{6,2},{7,3},{8,12},{9,13},{10,... | collective-permute-start | bytes 3145736 | tf_op jit(solution)/shard_map/ppermute | solution.py:25
  104.6 116.9 %collective-permute-start.40 = (bf16[256,2048]{1,0:T(8,128)(2,1)S(1)}, bf16[256,2048]{1,0:T(8,128)(2,1)}, u32[]{:S(2)}, u32[]{:S(2)}) collective-permute-start(bf16[256,2048]{1,0:T(8,128)(2,1)S(1)} %copy-done.22), channel_id=1, source_target_pairs={{0,2},{1,3},{2,0},{3,1},{4,6},{5,7},{6,4},{7,5},{8,10},{9,11},{10,... | collective-permute-start | bytes 3145736 | tf_op jit(solution)/shard_map/ppermute | solution.py:25
  106.1 110.8 %collective-permute-start.39 = (bf16[256,2048]{1,0:T(8,128)(2,1)S(1)}, bf16[256,2048]{1,0:T(8,128)(2,1)}, u32[]{:S(2)}, u32[]{:S(2)}) collective-permute-start(bf16[256,2048]{1,0:T(8,128)(2,1)S(1)} %copy-done.22), channel_id=1, source_target_pairs={{0,1},{1,0},{2,3},{3,2},{4,5},{5,4},{6,7},{7,6},{8,9},{9,8},{10,11... | collective-permute-start | bytes 3145736 | tf_op jit(solution)/shard_map/ppermute | solution.py:25
  107.7 101.3 %all-to-all-start.5 = ((bf16[8,64,768]{2,1,0:T(8,128)(2,1)}), bf16[8,64,768]{2,1,0:T(8,128)(2,1)S(1)}, u32[]{:S(2)}, u32[]{:S(2)}) async-start(bf16[8,64,768]{2,1,0:T(8,128)(2,1)} %reshape_squeeze.15), calls=%async_computation.5 | async-start | bytes 1572864 | tf_op jit(solution)/shard_map/all_to_all | solution.py:71
  111.3 298.4 %all-gather.19.cloned.1.call-start = ((), (), s32[]{:S(2)}) async-start(), calls=%async_computation.24 | async-start | bytes 3932160 | tf_op jit(solution)/shard_map/all_gather | solution.py:72
  209.9 578.4 %reduce-scatter.14.cloned.1.call-start = ((), (), s32[]{:S(2)}) async-start(), calls=%async_computation.27 | async-start | bytes 3932160 | tf_op jit(solution)/shard_map/reduce_scatter | solution.py:77
  247.1 68.5 %collective-permute-start.17 = (bf16[2048,256]{1,0:T(8,128)(2,1)}, bf16[2048,256]{1,0:T(8,128)(2,1)}, u32[]{:S(2)}, u32[]{:S(2)}) collective-permute-start(bf16[2048,256]{1,0:T(8,128)(2,1)} %all-gather.11.cloned.1.call-done), channel_id=1, source_target_pairs={{0,2},{1,3},{2,0},{3,1},{4,6},{5,7},{6,4},{7,5},{8,10},{9,11},{10,... | collective-permute-start | bytes 3145736 | tf_op jit(solution)/shard_map/ppermute | solution.py:25
  249.5 71.3 %collective-permute-start.19 = (bf16[2048,256]{1,0:T(8,128)(2,1)}, bf16[2048,256]{1,0:T(8,128)(2,1)}, u32[]{:S(2)}, u32[]{:S(2)}) collective-permute-start(bf16[2048,256]{1,0:T(8,128)(2,1)} %all-gather.11.cloned.1.call-done), channel_id=1, source_target_pairs={{0,4},{1,5},{2,6},{3,7},{4,0},{5,1},{6,2},{7,3},{8,12},{9,13},{10,... | collective-permute-start | bytes 3145736 | tf_op jit(solution)/shard_map/ppermute | solution.py:25
  490.1 308.5 %reduce-scatter.16.cloned.1.call-start = ((), (), s32[]{:S(2)}) async-start(), calls=%async_computation.28 | async-start | bytes 3932160 | tf_op jit(solution)/shard_map/reduce_scatter | solution.py:77
  508.6 93.2 %collective-permute-start.32 = (bf16[4,256,2048]{2,1,0:T(8,128)(2,1)}, bf16[4,256,2048]{2,1,0:T(8,128)(2,1)}, u32[]{:S(2)}, u32[]{:S(2)}) collective-permute-start(bf16[4,256,2048]{2,1,0:T(8,128)(2,1)} %slice.362), channel_id=1, source_target_pairs={{0,1},{1,0},{2,3},{3,2},{4,5},{5,4},{6,7},{7,6},{8,9},{9,8},{10,11... | collective-permute-start | bytes 12582920 | tf_op jit(solution)/shard_map/ppermute | solution.py:25
  544.5 279.0 %reduce-scatter.18.cloned.1.call-start = ((), (), s32[]{:S(2)}) async-start(), calls=%async_computation.29 | async-start | bytes 3932160 | tf_op jit(solution)/shard_map/reduce_scatter | solution.py:77
  601.7 248.6 %reduce-scatter.20.cloned.1.call-start = ((), (), s32[]{:S(2)}) async-start(), calls=%async_computation.30 | async-start | bytes 3932160 | tf_op jit(solution)/shard_map/reduce_scatter | solution.py:77
  692.5 133.3 %collective-permute-start.70 = (bf16[256,2048]{1,0:T(8,128)(2,1)}, bf16[256,2048]{1,0:T(8,128)(2,1)}, u32[]{:S(2)}, u32[]{:S(2)}) collective-permute-start(bf16[256,2048]{1,0:T(8,128)(2,1)} %get-tuple-element.57), channel_id=1, source_target_pairs={{0,2},{1,3},{2,0},{3,1},{4,6},{5,7},{6,4},{7,5},{8,10},{9,11},{10,... | collective-permute-start | bytes 3145736 | tf_op jit(solution)/shard_map/ppermute | solution.py:25
  694.2 150.3 %collective-permute-start.72 = (bf16[256,2048]{1,0:T(8,128)(2,1)}, bf16[256,2048]{1,0:T(8,128)(2,1)}, u32[]{:S(2)}, u32[]{:S(2)}) collective-permute-start(bf16[256,2048]{1,0:T(8,128)(2,1)} %get-tuple-element.57), channel_id=1, source_target_pairs={{0,4},{1,5},{2,6},{3,7},{4,0},{5,1},{6,2},{7,3},{8,12},{9,13},{10,... | collective-permute-start | bytes 3145736 | tf_op jit(solution)/shard_map/ppermute | solution.py:25
  694.6 162.6 %collective-permute-start.69 = (bf16[256,2048]{1,0:T(8,128)(2,1)}, bf16[256,2048]{1,0:T(8,128)(2,1)}, u32[]{:S(2)}, u32[]{:S(2)}) collective-permute-start(bf16[256,2048]{1,0:T(8,128)(2,1)} %get-tuple-element.57), channel_id=1, source_target_pairs={{0,1},{1,0},{2,3},{3,2},{4,5},{5,4},{6,7},{7,6},{8,9},{9,8},{10,11... | collective-permute-start | bytes 3145736 | tf_op jit(solution)/shard_map/ppermute | solution.py:25
  823.1 72.7 %collective-permute-start.62 = (bf16[4,256,2048]{2,1,0:T(8,128)(2,1)}, bf16[4,256,2048]{2,1,0:T(8,128)(2,1)}, u32[]{:S(2)}, u32[]{:S(2)}) collective-permute-start(bf16[4,256,2048]{2,1,0:T(8,128)(2,1)} %slice.397), channel_id=1, source_target_pairs={{0,1},{1,0},{2,3},{3,2},{4,5},{5,4},{6,7},{7,6},{8,9},{9,8},{10,11... | collective-permute-start | bytes 12582920 | tf_op jit(solution)/shard_map/ppermute | solution.py:25
  925.7 162.6 %reduce-scatter.22.cloned.1.call-start = ((), (), s32[]{:S(2)}) async-start(), calls=%async_computation.31 | async-start | bytes 1081344
  (165 other events, 2931.2 us)
Sparse Core Ops, SparseCore 0:
  20.8 27.2 all-gather.10
  49.7 36.5 all-gather.8
  87.9 62.3 all-gather.12
  151.8 62.2 all-gather.14
  215.4 62.1 all-gather.16
  279.6 62.1 all-gather.18
  490.2 59.1 reduce-scatter.13
  551.7 60.2 reduce-scatter.15
  614.3 60.2 reduce-scatter.17
  692.6 58.3 reduce-scatter.19
  840.7 35.8 reduce-scatter.9
  892.1 26.2 reduce-scatter.11
  953.3 134.9 reduce-scatter.21

commit v2 on v1

v2 whole, which is shorter than its diff:
```python
import functools

import jax
import jax.numpy as jnp
from jax import lax
from jax.experimental import pallas as pl
from jax.experimental.pallas import tpu as pltpu
from jax.sharding import Mesh, PartitionSpec as P

D = 2048
H = 32
KV = 8
HD = 64
FF = 8192
GROUP = H // KV
TP = 8
WIDTHS = (512, 512)
CHUNKS = len(WIDTHS)
HALF = HD // 2
QW = GROUP * HD
STARTS = [TP * sum(WIDTHS[:k]) for k in range(CHUNKS)]
EXTRA = 8
AW = 2 * QW + 2 * HD

NORM_EPS = 1e-05
ROPE_BASE = 500000.0
SCALE = HD ** (-0.5)

PLANE = ("y", "x", "c")
EVERY = ("z", "y", "x", "c")
BF = jnp.bfloat16
F32 = jnp.float32
ANY = pl.BlockSpec(memory_space=pl.ANY)
VMEM = pl.BlockSpec(memory_space=pltpu.VMEM)
SMEM = pl.BlockSpec(memory_space=pltpu.SMEM)
BIG = pltpu.CompilerParams(vmem_limit_bytes=56 * 1024 * 1024)


def cost(flops, size):
    return pl.CostEstimate(flops=int(flops), bytes_accessed=int(size), transcendentals=0)


def mm(left, right, dims):
    return lax.dot_general(left, right, (dims, ((), ())), preferred_element_type=F32)


NN = ((1,), (0,))
NT = ((1,), (1,))
TN = ((0,), (0,))


def swap(value, rel):
    return lax.ppermute(value, PLANE, [(i, i ^ rel) for i in range(TP)])


def swap_across(value):
    return lax.ppermute(value, PLANE, [(i, i ^ (2 + 2 * (i % 2))) for i in range(TP)])


def on_first():
    return lax.axis_index(PLANE) % 2 == 0


def gather_begin(own):
    return own, swap(own, 2), swap(own, 4), swap(own, 1)


def gather_end(own, from_x, from_y, from_c):
    across = swap_across(jnp.where(on_first(), from_y, from_x))
    return [own, from_c, from_x, swap(from_x, 1), from_y, swap(from_y, 1), across, swap(across, 1)]


def gather_plane(own):
    return gather_end(*gather_begin(own))


def add(left, right):
    return (left.astype(F32) + right.astype(F32)).astype(BF)


def scatter_plane(part):
    even, odd = part((3, 2))
    both = add(even, swap(odd, 1))
    across, over_y = swap_across(both[0]), both[1]
    even, odd = part((1, 0))
    both = add(even, swap(odd, 1))
    over_x, own = both[0], both[1]
    first = on_first()
    over_x = jnp.where(first, over_x, add(over_x, across))
    over_y = jnp.where(first, add(over_y, across), over_y)
    return own, swap(over_x, 2), swap(over_y, 4)


def total(own, from_x, from_y):
    return own.astype(F32) + from_x.astype(F32) + from_y.astype(F32)


def trade(blocks):
    return lax.all_to_all(blocks, PLANE, 0, 0, tiled=True)


def along_z(value, steps):
    count = lax.axis_size("z")
    return lax.ppermute(
        value, "z", [(i, i + steps) for i in range(count) if 0 <= i + steps < count]
    )


def gather_z(own):
    return lax.all_gather(own, "z", axis=0, tiled=True)


def start_rows(refs, dst, sems, first=0):
    each = dst.shape[0] // TP
    for r, ref in enumerate(refs):
        pltpu.make_async_copy(ref.at[pl.ds(first, each)], dst.at[pl.ds(r * each, each)], sems.at[r]).start()


def wait_rows(r, dst, sems):
    each = dst.shape[0] // TP
    part = dst.at[pl.ds(pl.multiple_of(r * each, each), each)]
    pltpu.make_async_copy(part, part, sems.at[r]).wait()


def fold_order():
    old = jnp.arange(QW, dtype=jnp.int32)
    new = (old // HALF) % 2 * (GROUP * HALF) + old // HD * HALF + old % HALF
    return (new[:, None] == jnp.arange(QW, dtype=jnp.int32)[None, :]).astype(BF)


def cut_attn_kernel(w_ref, perm_ref, out):
    kv_cols = KV * HD
    for i in range(TP):
        q = jnp.dot(w_ref[:, QW * i : QW * (i + 1)], perm_ref[...], preferred_element_type=F32)
        out[i, :, :QW] = q.astype(BF)
        k = w_ref[:, D + HD * i : D + HD * (i + 1)]
        v = w_ref[:, D + kv_cols + HD * i : D + kv_cols + HD * (i + 1)]
        out[i, :, QW : QW + 2 * HD] = jnp.concatenate([k, v], axis=1)
        out[i, :, QW + 2 * HD :] = w_ref[:, D + 2 * kv_cols + QW * i : D + 2 * kv_cols + QW * (i + 1)]


def cut_attn(w_attn, perm):
    rows = w_attn.shape[0]
    return pl.pallas_call(
        cut_attn_kernel,
        out_shape=jax.ShapeDtypeStruct((TP, rows, AW), BF),
        in_specs=[VMEM, VMEM],
        out_specs=VMEM,
        cost_estimate=cost(0, 2 * w_attn.size * 2),
        name="cut_attn",
    )(w_attn, perm)


def cut_ffn_kernel(w_ref, *outs):
    for k, width in enumerate(WIDTHS):
        for i in range(TP):
            for n in range(3):
                at = n * FF + STARTS[k] + i * width
                outs[k][i, :, n * width : (n + 1) * width] = w_ref[:, at : at + width]


def cut_ffn(w_ffn):
    rows = w_ffn.shape[0]
    return pl.pallas_call(
        cut_ffn_kernel,
        out_shape=[jax.ShapeDtypeStruct((TP, rows, 3 * width), BF) for width in WIDTHS],
        in_specs=[VMEM],
        out_specs=[VMEM] * CHUNKS,
        cost_estimate=cost(0, 2 * w_ffn.size * 2),
        compiler_params=BIG,
        name="cut_ffn",
    )(w_ffn)


def paste_ffn_kernel(*refs):
    pieces, w, out, term = refs[:CHUNKS], *refs[CHUNKS:]
    each = min(WIDTHS)
    total = jnp.zeros((w.shape[0], each), F32)
    for k, width in enumerate(WIDTHS):
        for i in range(TP):
            for n in range(3):
                for part in range(0, width, each):
                    at = n * FF + STARTS[k] + i * width + part
                    grad = pieces[k][i, :, n * width + part : n * width + part + each].astype(F32)
                    out[:, at : at + each] = grad
                    if n < 2:
                        total += grad * w[:, at : at + each].astype(F32)
    term[...] = jnp.sum(total, axis=-1, keepdims=True)


def paste_ffn(pieces, w_ffn):
    rows = w_ffn.shape[0]
    return pl.pallas_call(
        paste_ffn_kernel,
        out_shape=(jax.ShapeDtypeStruct(w_ffn.shape, F32), jax.ShapeDtypeStruct((rows, 1), F32)),
        in_specs=[VMEM] * (CHUNKS + 1),
        out_specs=(VMEM, VMEM),
        cost_estimate=cost(0, 8 * w_ffn.size),
        compiler_params=BIG,
        name="paste_ffn",
    )(*pieces, w_ffn)


def paste_attn_kernel(piece, w, perm, out, term):
    kv_cols = KV * HD
    ones = jnp.zeros((w.shape[0], QW), F32)
    small = jnp.zeros((w.shape[0], HD), F32)
    for i in range(TP):
        q = mm(piece[i, :, :QW], perm[...], NT)
        out[:, QW * i : QW * (i + 1)] = q
        ones += q * w[:, QW * i : QW * (i + 1)].astype(F32)
        kv = piece[i, :, QW : QW + 2 * HD].astype(F32)
        for at, part in ((D + HD * i, kv[:, :HD]), (D + kv_cols + HD * i, kv[:, HD:])):
            out[:, at : at + HD] = part
            small += part * w[:, at : at + HD].astype(F32)
        at = D + 2 * kv_cols + QW * i
        out[:, at : at + QW] = piece[i, :, QW + 2 * HD :].astype(F32)
    term[...] = jnp.sum(ones, axis=-1, keepdims=True) + jnp.sum(small, axis=-1, keepdims=True)


def paste_attn(piece, w_attn, perm):
    rows = w_attn.shape[0]
    return pl.pallas_call(
        paste_attn_kernel,
        out_shape=(jax.ShapeDtypeStruct(w_attn.shape, F32), jax.ShapeDtypeStruct((rows, 1), F32)),
        in_specs=[VMEM] * 3,
        out_specs=(VMEM, VMEM),
        cost_estimate=cost(0, 8 * w_attn.size),
        compiler_params=BIG,
        name="paste_attn",
    )(piece, w_attn, perm)


def turn_kernel(x, out):
    rows = out.shape[1]
    turned = x[...].astype(F32).T.astype(BF)
    for i in range(TP):
        out[i] = turned[rows * i : rows * (i + 1)]


def turn(x):
    cols, wide = x.shape
    return pl.pallas_call(
        turn_kernel,
        out_shape=jax.ShapeDtypeStruct((TP, wide // TP, cols), BF),
        in_specs=[VMEM],
        out_specs=VMEM,
        cost_estimate=cost(0, 4 * x.size),
        compiler_params=BIG,
        name="turn",
    )(x)


def qkv_kernel(count, *refs):
    blocks = refs[:count]
    gain, w_all, cos, sin, n1, q_out, kv_out, x_s, w_s, sems, w_sem = refs[count:]
    w_copy = pltpu.make_async_copy(w_all.at[:, pl.ds(0, w_s.shape[1]), pl.ds(0, w_s.shape[2])], w_s, w_sem)
    w_copy.start()
    start_rows(blocks, x_s, sems)
    each = x_s.shape[0] // TP
    lane = lax.broadcasted_iota(jnp.int32, (each, 2 * HD), 1)
    w_copy.wait()

    def step(r, carry):
        at = pl.ds(pl.multiple_of(r * each, each), each)
        wait_rows(r, x_s, sems)
        x = x_s[at, :].astype(F32)
        scale = lax.rsqrt(jnp.mean(x * x, axis=-1, keepdims=True) + NORM_EPS)
        normed = (x * scale * gain[...]).astype(BF)
        n1[at, :] = normed
        qkv = jnp.dot(normed, w_s[...].reshape(D, QW + 2 * HD), preferred_element_type=F32)
        c, s = cos[at, :], sin[at, :]
        a, b = qkv[:, : QW // 2], qkv[:, QW // 2 : QW]
        q_out[at, : QW // 2] = (a * c - b * s).astype(BF)
        q_out[at, QW // 2 :] = (b * c + a * s).astype(BF)
        kv = qkv[:, QW:]
        ahead = pltpu.roll(kv, 2 * HD - HALF, 1)
        behind = pltpu.roll(kv, HALF, 1)
        turned = kv * c + jnp.where(lane < HALF, -ahead, behind) * s
        kv_out[at, :] = jnp.where(lane < HD, turned, kv).astype(BF)
        return carry

    lax.fori_loop(0, TP, step, 0)


def norm_qkv(blocks, gain, w_all, cos, sin):
    each = w_all.shape[1] - EXTRA
    tokens = cos.shape[0]
    return pl.pallas_call(
        functools.partial(qkv_kernel, len(blocks)),
        out_shape=(
            jax.ShapeDtypeStruct((tokens, D), BF),
            jax.ShapeDtypeStruct((tokens, QW), BF),
            jax.ShapeDtypeStruct((tokens, 2 * HD), BF),
        ),
        in_specs=[ANY] * len(blocks) + [VMEM, ANY, VMEM, VMEM],
        out_specs=(VMEM, VMEM, VMEM),
        scratch_shapes=[
            pltpu.VMEM((tokens, D), BF),
            pltpu.VMEM((w_all.shape[0], each, QW + 2 * HD), BF),
            pltpu.SemaphoreType.DMA((TP,)),
            pltpu.SemaphoreType.DMA,
        ],
        cost_estimate=cost(2 * tokens * D * (QW + 2 * HD), 4 * tokens * D),
        compiler_params=BIG,
        name="norm_qkv",
    )(*blocks, gain, w_all, cos, sin)


def spread_kv():
    src = jnp.arange(2 * HD, dtype=jnp.int32)[:, None]
    col = jnp.arange(QW, dtype=jnp.int32)[None, :]
    key = (src == col // (GROUP * HALF) * HALF + col % HALF).astype(BF)
    value = (src == HD + col % HD).astype(BF)
    return key, value


def attend_kernel(prev_at, index, q_ref, prev_ref, here_ref, lo_ref, ek, ev, o_ref, o_index_ref):
    tok = q_ref.shape[0]
    two = jnp.concatenate([prev_ref[...], here_ref[...]], axis=0)
    keys = jnp.dot(two, ek[...], preferred_element_type=F32).astype(BF)
    values = jnp.dot(two, ev[...], preferred_element_type=F32).astype(BF)
    q = q_ref[...]
    key_at = lax.broadcasted_iota(jnp.int32, (tok, 2 * tok), 1)
    row_at = lax.broadcasted_iota(jnp.int32, (tok, 2 * tok), 0)
    allowed = (lo_ref[...] <= key_at) & (key_at <= row_at + tok)
    q_lane = lax.broadcasted_iota(jnp.int32, (tok, QW), 1)
    v_lane = lax.broadcasted_iota(jnp.int32, (2 * tok, QW), 1)
    total = jnp.zeros((tok, QW), F32)
    for h in range(GROUP):
        mine = jnp.where((q_lane // HALF) % GROUP == h, q, jnp.zeros_like(q))
        s = jnp.where(allowed, mm(mine, keys, NT) * SCALE, -1e30)
        expo = jnp.exp(s - jnp.max(s, axis=-1, keepdims=True))
        probs = (expo / jnp.sum(expo, axis=-1, keepdims=True)).astype(BF)
        total += mm(probs, jnp.where(v_lane // HD == h, values, jnp.zeros_like(values)), NN)
    o_ref[...] = total.astype(BF)
    o_index_ref[0] = o_ref[...]


def attend(prev_at, index, q, kv9, lo_col, ek, ev):
    tokens = q.shape[0]
    tok = tokens // TP
    full = lambda shape: pl.BlockSpec(shape, lambda r, p, i: (0, 0))
    return pl.pallas_call(
        attend_kernel,
        out_shape=(jax.ShapeDtypeStruct((tokens, QW), BF), jax.ShapeDtypeStruct((TP, tok, QW), BF)),
        grid_spec=pltpu.PrefetchScalarGridSpec(
            num_scalar_prefetch=2,
            grid=(TP,),
            in_specs=[
                pl.BlockSpec((tok, QW), lambda r, p, i: (r, 0)),
                pl.BlockSpec((tok, 2 * HD), lambda r, p, i: (p[r], 0)),
                pl.BlockSpec((tok, 2 * HD), lambda r, p, i: (r, 0)),
                pl.BlockSpec((tok, 1), lambda r, p, i: (r, 0)),
                full((2 * HD, QW)),
                full((2 * HD, QW)),
            ],
            out_specs=(
                pl.BlockSpec((tok, QW), lambda r, p, i: (r, 0)),
                pl.BlockSpec((1, tok, QW), lambda r, p, i: (i[r], 0, 0)),
            ),
        ),
        cost_estimate=cost(4 * tokens * 2 * tok * QW * GROUP, 4 * tokens * QW),
        compiler_params=BIG,
        name="attend",
    )(prev_at, index, q, kv9, kv9, lo_col, ek, ev)


def attend_back_kernel(here_at, prev_at, q_ref, do_ref, prev_ref, here_ref, lo_ref, cos, sin, ek, ev, dq_ref, dkv_ref, carry):
    step = pl.program_id(0)
    tok = q_ref.shape[0]

    @pl.when(step == 0)
    def _():
        carry[...] = jnp.zeros_like(carry)

    @pl.when(step < TP)
    def _():
        two = jnp.concatenate([prev_ref[...], here_ref[...]], axis=0)
        keys = jnp.dot(two, ek[...], preferred_element_type=F32).astype(BF)
        values = jnp.dot(two, ev[...], preferred_element_type=F32).astype(BF)
        q, d_o = q_ref[...], do_ref[0]
        key_at = lax.broadcasted_iota(jnp.int32, (2 * tok, tok), 0)
        row_at = lax.broadcasted_iota(jnp.int32, (2 * tok, tok), 1)
        allowed = (lo_ref[0] <= key_at) & (key_at <= row_at + tok)
        lane = lax.broadcasted_iota(jnp.int32, (tok, QW), 1)
        key_lane = lax.broadcasted_iota(jnp.int32, (2 * tok, QW), 1)
        d_q = jnp.zeros((tok, QW), F32)
        d_k = jnp.zeros((2 * tok, QW), F32)
        d_v = jnp.zeros((2 * tok, QW), F32)
        for h in range(GROUP):
            q_h = jnp.where((lane // HALF) % GROUP == h, q, jnp.zeros_like(q))
            do_h = jnp.where(lane // HD == h, d_o, jnp.zeros_like(d_o))
            k_h = jnp.where((key_lane // HALF) % GROUP == h, keys, jnp.zeros_like(keys))
            s = jnp.where(allowed, mm(keys, q_h, NT) * SCALE, -1e30)
            expo = jnp.exp(s - jnp.max(s, axis=0, keepdims=True))
            probs = expo / jnp.sum(expo, axis=0, keepdims=True)
            d_p = mm(values, do_h, NT)
            shift = jnp.sum(d_p * probs, axis=0, keepdims=True)
            d_s = (probs * (d_p - shift)).astype(BF)
            d_v += mm(probs.astype(BF), do_h, NN)
            d_k += mm(d_s, q_h, NN)
            d_q += mm(d_s, k_h, TN)
        d_q = d_q * SCALE
        a, b = d_q[:, : QW // 2], d_q[:, QW // 2 :]
        c, s = cos[...], sin[...]
        dq_ref[:, : QW // 2] = (a * c + b * s).astype(BF)
        dq_ref[:, QW // 2 :] = (b * c - a * s).astype(BF)
        d_k = d_k * SCALE

        def fold(v):
            v = v + pltpu.roll(v, HD, 1)
            return v + pltpu.roll(v, HALF, 1)

        first, second = fold(d_k[:, : QW // 2]), fold(d_k[:, QW // 2 :])
        whole = d_v[:, : QW // 2] + d_v[:, QW // 2 :]
        whole = whole + pltpu.roll(whole, HD, 1)
        low = lax.broadcasted_iota(jnp.int32, (2 * tok, 2 * HD), 1)
        d_kv = jnp.where(low < HALF, first, jnp.where(low < HD, second, whole))
        dkv_ref[...] = carry[...] + d_kv[:tok]
        carry[...] = d_kv[tok:]

    @pl.when(step == TP)
    def _():
        dkv_ref[...] = carry[...]


def attend_back(here_at, prev_at, q, d_o, kv9, lo_row, cos, sin, ek, ev):
    tokens = q.shape[0]
    tok = tokens // TP
    last = TP - 1
    here = lambda cols: pl.BlockSpec((tok, cols), lambda s, h, p: (h[jnp.minimum(s, last)], 0))
    full = lambda shape: pl.BlockSpec(shape, lambda s, h, p: (0, 0))
    return pl.pallas_call(
        attend_back_kernel,
        out_shape=(
            jax.ShapeDtypeStruct((tokens, QW), BF),
            jax.ShapeDtypeStruct((tokens + tok, 2 * HD), F32),
        ),
        grid_spec=pltpu.PrefetchScalarGridSpec(
            num_scalar_prefetch=2,
            grid=(TP + 1,),
            in_specs=[
                here(QW),
                pl.BlockSpec((1, tok, QW), lambda s, h, p: (jnp.minimum(s, last), 0, 0)),
                pl.BlockSpec((tok, 2 * HD), lambda s, h, p: (p[jnp.minimum(s, last)], 0)),
                here(2 * HD),
                pl.BlockSpec((1, 1, tok), lambda s, h, p: (h[jnp.minimum(s, last)], 0, 0)),
                here(2 * HD),
                here(2 * HD),
                full((2 * HD, QW)),
                full((2 * HD, QW)),
            ],
            out_specs=(
                here(QW),
                pl.BlockSpec((tok, 2 * HD), lambda s, h, p: (jnp.where(s == 0, TP, h[jnp.maximum(s - 1, 0)]), 0)),
            ),
            scratch_shapes=[pltpu.VMEM((tok, 2 * HD), F32)],
        ),
        cost_estimate=cost(10 * tokens * 2 * tok * QW * GROUP, 8 * tokens * QW),
        compiler_params=BIG,
        name="attend_back",
    )(here_at, prev_at, q, d_o, kv9, kv9, lo_row, cos, sin, ek, ev)


def ffn_kernel(count, *refs):
    n2_blocks, dy_blocks = refs[:count], refs[count : 2 * count]
    w, act_out, dgu_out, grad_out, n2, dy, flat, held, n2_sems, dy_sems, out_sems = refs[2 * count :]
    start_rows(n2_blocks, n2, n2_sems)
    start_rows(dy_blocks, dy, dy_sems, dy.shape[0] // TP)
    each = n2.shape[0] // TP
    width = act_out.shape[1]
    two = 2 * width

    def forward(r, carry):
        at = pl.ds(pl.multiple_of(r * each, each), each)
        wait_rows(r, n2, n2_sems)
        wait_rows(r, dy, dy_sems)
        gate_up = jnp.dot(n2[at, :], w[:, :two], preferred_element_type=F32)
        d_act = jnp.dot(dy[at, :], w[:, two:], preferred_element_type=F32)
        g, u = gate_up[:, :width], gate_up[:, width:]
        sg = jax.nn.sigmoid(g)
        gs = g * sg
        act = (gs * u).astype(BF)
        d_g = (d_act * u * (sg * (1.0 + g * (1.0 - sg)))).astype(BF)
        d_u = (d_act * gs).astype(BF)
        act_out[at, :] = act
        dgu_out[at, :width] = d_g
        dgu_out[at, width:] = d_u
        flat[:width, at] = d_g.T
        flat[width:two, at] = d_u.T
        flat[two:, at] = act.T
        return carry

    lax.fori_loop(0, TP, forward, 0)
    planes, _, cols = grad_out.shape

    def leave(z):
        return pltpu.make_async_copy(held.at[lax.rem(z, 2)], grad_out.at[z], out_sems.at[lax.rem(z, 2)])

    def back(z, carry):
        at = pl.ds(pl.multiple_of(z * cols, cols), cols)
        slot = lax.rem(z, 2)

        @pl.when(z >= 2)
        def _():
            leave(z - 2).wait()

        held[slot, :two, :] = jnp.dot(flat[:two, :], n2[:, at], preferred_element_type=F32).astype(BF)
        held[slot, two:, :] = jnp.dot(flat[two:, :], dy[:, at], preferred_element_type=F32).astype(BF)
        leave(z).start()
        return carry

    lax.fori_loop(0, planes, back, 0)
    leave(planes - 2).wait()
    leave(planes - 1).wait()


def ffn_chunk(n2_blocks, dy_blocks, w):
    tokens = TP * n2_blocks[0].shape[0]
    planes = lax.axis_size("z")
    width = w.shape[1] // 3
    return pl.pallas_call(
        functools.partial(ffn_kernel, len(n2_blocks)),
        out_shape=(
            jax.ShapeDtypeStruct((tokens, width), BF),
            jax.ShapeDtypeStruct((tokens, 2 * width), BF),
            jax.ShapeDtypeStruct((planes, 3 * width, D // planes), BF),
        ),
        in_specs=[ANY] * (2 * len(n2_blocks)) + [VMEM],
        out_specs=(VMEM, VMEM, ANY),
        scratch_shapes=[
            pltpu.VMEM((tokens, D), BF),
            pltpu.VMEM((tokens, D), BF),
            pltpu.VMEM((3 * width, tokens), BF),
            pltpu.VMEM((2, 3 * width, D // planes), BF),
            pltpu.SemaphoreType.DMA((TP,)),
            pltpu.SemaphoreType.DMA((TP,)),
            pltpu.SemaphoreType.DMA((2,)),
        ],
        cost_estimate=cost(18 * tokens * D * width, 4 * tokens * D + 12 * width * D),
        compiler_params=BIG,
        name="ffn_chunk",
    )(*n2_blocks, *dy_blocks, w)


def down_kernel(parts, *refs):
    outs = refs[-2:]
    base = refs[2 * parts : -2]
    for at, out in enumerate(outs):
        term = base[at][0] if base else None
        for j in range(parts):
            more = mm(refs[j][0, at], refs[parts + j][...], NT)
            term = more if term is None else term + more
        out[0] = term.astype(out.dtype)


def down(parts, weights, last, groups, base=None, kind=BF):
    count = len(parts)
    tokens = parts[0].shape[0]
    tok = tokens // TP
    widths = [p.shape[1] for p in parts]
    columns = [w.shape[1] // width - 1 if last else 0 for w, width in zip(weights, widths)]
    pairs = [p.reshape(TP // 2, 2, tok, width) for p, width in zip(parts, widths)]
    rows = weights[0].shape[0]
    first, step = groups[0], groups[1] - groups[0]
    return pl.pallas_call(
        functools.partial(down_kernel, count),
        out_shape=[jax.ShapeDtypeStruct((len(groups), tok, rows), kind)] * 2,
        grid=(len(groups),),
        in_specs=[pl.BlockSpec((1, 2, tok, width), lambda s: (first + step * s, 0, 0, 0)) for width in widths]
        + [
            pl.BlockSpec((rows, width), lambda s, c=c: (0, c), pipeline_mode=pl.Buffered(1))
            for width, c in zip(widths, columns)
        ]
        + ([] if base is None else [pl.BlockSpec((1, tok, rows), lambda s: (first + step * s, 0, 0))] * 2),
        out_specs=[pl.BlockSpec((1, tok, rows), lambda s: (s, 0, 0))] * 2,
        cost_estimate=cost(4 * len(groups) * tok * sum(widths) * rows, rows * sum(widths) * 2 + len(groups) * tok * rows * 8),
        compiler_params=BIG,
        name="down",
    )(*pairs, *weights, *(() if base is None else base))


def start_wo(blocks, dst, sems):
    for r, ref in enumerate(blocks):
        pltpu.make_async_copy(ref, dst.at[r], sems.at[r]).start()


def wait_wo(r, dst, sems):
    pltpu.make_async_copy(dst.at[r], dst.at[r], sems.at[r]).wait()


def close_kernel(*refs):
    wo_blocks = refs[:TP]
    index, heads, x, gain, resid_out, n2_out, wo, sems = refs[TP:]
    start_wo(wo_blocks, wo, sems)
    y = x[...].astype(F32)
    for r in range(TP):
        wait_wo(r, wo, sems)
        y += mm(heads[index[r]], wo[r], NT)
    resid_out[...] = y
    n2_out[...] = (y * lax.rsqrt(jnp.mean(y * y, axis=-1, keepdims=True) + NORM_EPS) * gain[...]).astype(BF)


def close_attention(wo_blocks, index, heads, x, gain):
    tok = x.shape[0]
    return pl.pallas_call(
        close_kernel,
        out_shape=(jax.ShapeDtypeStruct((tok, D), F32), jax.ShapeDtypeStruct((tok, D), BF)),
        in_specs=[ANY] * TP + [SMEM] + [VMEM] * 3,
        out_specs=(VMEM, VMEM),
        scratch_shapes=[pltpu.VMEM((TP, D, QW), BF), pltpu.SemaphoreType.DMA((TP,))],
        cost_estimate=cost(2 * tok * D * D, 2 * D * D),
        compiler_params=BIG,
        name="close_attention",
    )(*wo_blocks, index, heads, x, gain)


def open_kernel(*refs):
    wo_blocks = refs[:TP]
    index, own, from_x, from_y, resid, dy, gain, back_out, att_out, heads, wo, sems = refs[TP:]
    start_wo(wo_blocks, wo, sems)
    d_n = own[...].astype(F32) + from_x[...].astype(F32) + from_y[...].astype(F32)
    y = resid[...]
    scale = lax.rsqrt(jnp.mean(y * y, axis=-1, keepdims=True) + NORM_EPS)
    unit = y * scale
    d_unit = d_n * gain[...]
    d_y = dy[...].astype(F32) + scale * (d_unit - unit * jnp.mean(d_unit * unit, axis=-1, keepdims=True))
    back_out[...] = d_y
    att_out[...] = d_y.astype(BF)
    att = att_out[...]
    for r in range(TP):
        wait_wo(r, wo, sems)
        heads[index[r]] = jnp.dot(att, wo[r], preferred_element_type=F32).astype(BF)


def open_attention(wo_blocks, index, terms, resid, dy, gain):
    tok = dy.shape[0]
    return pl.pallas_call(
        open_kernel,
        out_shape=(
            jax.ShapeDtypeStruct((tok, D), F32),
            jax.ShapeDtypeStruct((tok, D), BF),
            jax.ShapeDtypeStruct((TP, tok, QW), BF),
        ),
        in_specs=[ANY] * TP + [SMEM] + [VMEM] * 6,
        out_specs=(VMEM, VMEM, VMEM),
        scratch_shapes=[pltpu.VMEM((TP, D, QW), BF), pltpu.SemaphoreType.DMA((TP,))],
        cost_estimate=cost(2 * tok * D * D, 2 * D * D),
        compiler_params=BIG,
        name="open_attention",
    )(*wo_blocks, index, *terms, resid, dy, gain)


def turn_grad_kernel(count, *refs):
    blocks, left, out, rows, sems = refs[:count], *refs[count:]
    start_rows(blocks, rows, sems)
    for r in range(TP):
        wait_rows(r, rows, sems)
    planes, _, cols = out.shape

    def back(z, carry):
        at = pl.ds(pl.multiple_of(z * cols, cols), cols)
        out[z] = mm(left[...], rows[:, at], TN).astype(BF)
        return carry

    lax.fori_loop(0, planes, back, 0)


def turn_grad(left, blocks):
    tokens, cols = left.shape
    planes = lax.axis_size("z")
    return pl.pallas_call(
        functools.partial(turn_grad_kernel, len(blocks)),
        out_shape=jax.ShapeDtypeStruct((planes, cols, D // planes), BF),
        in_specs=[ANY] * len(blocks) + [VMEM],
        out_specs=VMEM,
        scratch_shapes=[pltpu.VMEM((tokens, D), BF), pltpu.SemaphoreType.DMA((TP,))],
        cost_estimate=cost(2 * tokens * D * cols, 2 * tokens * D),
        compiler_params=BIG,
        name="turn_grad",
    )(*blocks, left)


def after(value, *first):
    return lax.optimization_barrier((value, *first))[0]


def rms_norm(values, scales):
    return values * lax.rsqrt(jnp.mean(values * values, axis=-1, keepdims=True) + NORM_EPS) * scales


def to_pieces(pieces):
    rows, cols = pieces.shape[1:]
    return trade(pieces).reshape(TP * rows, cols)


def sum_z(grad):
    planes, cols, wide = grad.shape
    return lax.psum_scatter(grad.reshape(planes * cols, wide), "z", scatter_dimension=0, tiled=True)


def give_back(summed):
    return trade(turn(summed))


def by_plane(grad):
    planes = lax.axis_size("z")
    return grad.reshape(grad.shape[0], planes, D // planes).transpose(1, 0, 2)


def pick(blocks, at):
    return lax.dynamic_index_in_dim(blocks, at, 0, keepdims=False)


def on_device(hidden_in, segment_ids, w_attn, w_ffn, gains, out_grad):
    tok = hidden_in.shape[0]
    rows = w_attn.shape[0]
    me = lax.axis_index(PLANE)
    z = lax.axis_index("z")
    tokens = TP * tok
    steps = jnp.arange(TP, dtype=jnp.int32)
    rel = me ^ steps
    perm = fold_order()
    ek, ev = spread_kv()

    own_start = (z * TP + me) * tok
    own_lo = segment_ids - own_start + tok
    extra = jnp.zeros((EXTRA, AW), BF)
    extra = extra.at[0, : 2 * rows].set(gains.reshape(-1))
    extra = extra.at[1, :tok].set((own_lo // 2).astype(BF)).at[2, :tok].set((own_lo % 2).astype(BF))

    attn_pieces = cut_attn(w_attn, perm)
    attn_pieces = jnp.concatenate([attn_pieces, jnp.broadcast_to(extra, (TP, *extra.shape))], axis=1)
    attn_rows = to_pieces(attn_pieces)
    both_begun = gather_begin(jnp.concatenate([hidden_in, out_grad], axis=0))
    pieces = cut_ffn(w_ffn)
    rows_0 = to_pieces(after(pieces[0], *both_begun[1:]))
    w_0 = gather_z(rows_0)
    both_blocks = gather_end(*both_begun)
    attn_all = after(gather_z(attn_rows), rows_0).reshape(-1, rows + EXTRA, AW)
    w_own = attn_all[:, :rows].reshape(D, AW)
    wqkv, wo = w_own[:, : QW + 2 * HD], w_own[:, QW + 2 * HD :]
    gains_full = attn_all[:, rows, : 2 * rows].reshape(-1, 2, rows).transpose(1, 0, 2).reshape(2, D).astype(F32)

    plane_lo = attn_rows.reshape(TP, rows + EXTRA, -1)[:, rows + 1 : rows + 3, :tok].astype(jnp.int32)
    lo = jnp.take(2 * plane_lo[:, 0] + plane_lo[:, 1], rel, axis=0)
    positions = jnp.arange(tok, dtype=jnp.int32)[None] + tok - lo
    freqs = 1.0 / ROPE_BASE ** (jnp.arange(HALF, dtype=F32) * (2.0 / HD))
    angles = positions.reshape(tokens).astype(F32)[:, None] * freqs
    cosine = jnp.tile(jnp.cos(angles), (1, GROUP))
    sine = jnp.tile(jnp.sin(angles), (1, GROUP))

    n1, q, kv = norm_qkv(both_blocks, gains_full[:1], attn_all, cosine, sine)
    wo_begun = gather_begin(wo)
    q = after(q, *wo_begun[1:])
    rows_1 = to_pieces(after(pieces[1], n1))
    before = along_z(pick(kv.reshape(TP, tok, 2 * HD), me ^ (TP - 1)), 1)
    kv9 = jnp.concatenate([kv, before], axis=0)
    prev_at = jnp.where(rel == 0, TP, (rel - 1) ^ me)
    mixed, heads = attend(prev_at, rel, q, kv9, lo.reshape(tokens, 1), ek, ev)

    wo_blocks = gather_end(*wo_begun)
    heads = trade(after(heads, rows_1))
    w_1 = gather_z(rows_1)
    x_own = hidden_in.astype(F32)
    residual, normed_two = close_attention(wo_blocks, rel, heads, after(hidden_in, w_0), gains_full[1:])
    n2_blocks = gather_plane(normed_two)

    act_0, d_gu_0, grad_0 = ffn_chunk(n2_blocks, both_blocks, w_0)
    so_far = down([d_gu_0], [w_0], False, (0, 1, 2, 3), kind=F32)
    sum_0 = sum_z(grad_0)
    act_1, d_gu_1, grad_1 = ffn_chunk(n2_blocks, both_blocks, after(w_1, so_far[0]))
    sum_1 = sum_z(grad_1)
    d_n2_terms = scatter_plane(lambda groups: down([d_gu_1], [w_1], False, groups, so_far))
    d_resid, d_att, d_heads = open_attention(wo_blocks, rel, d_n2_terms, residual, out_grad, gains_full[1:])
    d_o = trade(d_heads)
    d_att_begun = gather_begin(after(d_att, d_o))

    here_at = me ^ steps
    prev_abs = jnp.where(steps == 0, TP, (steps - 1) ^ me)
    d_q, d_kv9 = attend_back(here_at, prev_abs, q, after(d_o, sum_0), kv9, lo.reshape(TP, 1, tok), cosine, sine, ek, ev)
    d_att_blocks = gather_end(after(d_att_begun[0], d_q), *d_att_begun[1:])
    wo_grad = turn_grad(mixed, d_att_blocks)
    back = along_z(d_kv9[tokens:].astype(BF), -1)
    last = me ^ (TP - 1)
    d_kv = d_kv9[:tokens].reshape(TP, tok, 2 * HD)
    d_kv = jnp.where((steps == last)[:, None, None], d_kv + back.astype(F32)[None], d_kv).reshape(tokens, 2 * HD)
    c, s = cosine[:, :HALF], sine[:, :HALF]
    a, b = d_kv[:, :HALF], d_kv[:, HALF:HD]
    d_qkv = jnp.concatenate(
        [d_q, (a * c + b * s).astype(BF), (b * c - a * s).astype(BF), d_kv[:, HD:].astype(BF)], axis=1
    )
    qkv_grad = by_plane(mm(d_qkv, n1, TN).astype(BF))
    attn_sum = jnp.concatenate([qkv_grad, wo_grad], axis=1)
    attn_back = give_back(sum_z(attn_sum))
    d_qkv = after(d_qkv, attn_sum)
    d_normed = total(*scatter_plane(lambda groups: down([d_qkv], [wqkv], False, groups)))
    acts = [after(act_0, attn_sum), act_1]
    f_terms = scatter_plane(lambda groups: down(acts, [w_0, w_1], True, groups))
    hidden_out = (residual + total(*f_terms)).astype(BF)
    ffn_back = [give_back(v) for v in (sum_0, sum_1)]
    scale = lax.rsqrt(jnp.mean(x_own * x_own, axis=-1, keepdims=True) + NORM_EPS)
    unit = x_own * scale
    d_unit = d_normed * gains_full[0]
    in_grad = d_resid + scale * (d_unit - unit * jnp.mean(d_unit * unit, axis=-1, keepdims=True))
    ffn_grad, term_two = paste_ffn(ffn_back, w_ffn)
    attn_grad, term_one = paste_attn(attn_back, w_attn, perm)
    gains_grad = jnp.concatenate([term_one, term_two], axis=1).T / gains.astype(F32)
    return hidden_out, in_grad.astype(BF), attn_grad, ffn_grad, gains_grad


def solution(mesh):
    fine = Mesh(mesh.devices.reshape(-1, 2, 2, 2), EVERY)
    rows = P(EVERY, None)
    in_specs = (rows, P(EVERY), rows, rows, P(None, EVERY), rows)
    out_specs = (rows, rows, rows, rows, P(None, EVERY))
    return jax.shard_map(
        on_device, mesh=fine, in_specs=in_specs, out_specs=out_specs, check_vma=False
    )
```

time: 1110 us -> 735 us (0.66)
  Pallas kernels: 0 us -> 246 us
  matrix products: 236 us -> 7.56 us
  local copies, waits for them, and re-layouts: 195 us -> 33 us
  blocking collectives: 163 us -> 62.3 us
  other arithmetic: 107 us -> 51.7 us
  starting transfers between devices: 93.9 us -> 54.6 us
  waiting for transfers between devices: 285 us -> 253 us
    pallas_call x0 -> x22, Pallas kernels: none -> 246 us  [the longest x2 76.5 us: ffn_chunk(): pl.pallas_call(functools.partial(ffn_kernel, len(n2_blocks)), out_shape=(...]
    dot_general x24 -> x1, matrix products: 186 us -> 7.56 us  [mm(): lax.dot_general(left, right, (dims, ((), ())), preferred_element_type=F32)]
    unnamed x14 -> x6, waiting for transfers between devices: 131 us -> 0.1 us
    unnamed x248 -> x86, local copies, waits for them, and re-layouts: 105 us -> 11.8 us
    all_gather x2 -> x0, blocking collectives: 90.4 us -> none  [the longest x1 51 us: on_device(): lax.all_gather(segment_ids, PLANE, axis=0, tiled=True).reshape(TP, tok)]
    ppermute x0 -> x7, waiting for transfers between devices: none -> 61.4 us  [swap_across(): lax.ppermute(value, PLANE, [(i, i ^ 2 + 2 * (i % 2)) for i in range(TP)])]
    dot_general x6 -> x0, matrix products: 49.9 us -> none  [the longest x1 14.9 us: on_device(): d_p = jnp.einsum('btrd,bsd->brts', d_o, v_two, preferred_element_type=F32)]
    all_to_all x7 -> x5, waiting for transfers between devices: 14.9 us -> 59.4 us  [trade(): return lax.all_to_all(blocks, PLANE, 0, 0, tiled=True)]
  transfers between devices with their start and end apart: 97 -> 56, of which waited for: 26 -> 21; matrix products, arithmetic and copies ran while one was open for 41% -> 11% of each run, Pallas kernels for 0% -> 33%
where the time goes in v2:
time: 735 us; the launch traced here: 723 us
  waiting for transfers between devices  253 us (34%)
  Pallas kernels  246 us (33%)
  blocking collectives  62.3 us (8%)
  starting transfers between devices  54.6 us (7%)
  other arithmetic  51.7 us (7%)
  local copies, waits for them, and re-layouts  33 us (4%)
  between operations  15.4 us (2%)
  matrix products  7.56 us (1%)
    ppermute x36, waiting for transfers between devices, swap(): return lax.ppermute(value, PLANE, [(i, i ^ rel) for i in range(TP)])  126 us
    pallas_call x2, Pallas kernels, ffn_chunk(): pl.pallas_call(functools.partial(ffn_kernel, len(n2_blocks)), out_shape=(...  76.5 us
    all_to_all x3, blocking collectives, trade(): return lax.all_to_all(blocks, PLANE, 0, 0, tiled=True)  62.3 us
    ppermute x7, waiting for transfers between devices, swap_across(): lax.ppermute(value, PLANE, [(i, i ^ 2 + 2 * (i % 2)) for i in range(TP)])  61.4 us
    pallas_call x7, Pallas kernels, down(): pl.pallas_call(functools.partial(down_kernel, count), out_shape=[jax.Shap...  61.2 us
    all_to_all x5, waiting for transfers between devices, trade(): return lax.all_to_all(blocks, PLANE, 0, 0, tiled=True)  59.4 us
    pallas_call x1, Pallas kernels, attend_back(): pl.pallas_call(attend_back_kernel, out_shape=(jax.ShapeDtypeStruct((token...  26.1 us
    all_to_all x5, starting transfers between devices, trade(): return lax.all_to_all(blocks, PLANE, 0, 0, tiled=True)  20 us
  transfers between devices with their start and end apart: 56, of which 21 were waited for; matrix products, arithmetic and copies ran while one was open for 11% of the time, Pallas kernels for 33%

profile of v2, /device:TPU:0, one launch (start us, length us, event | category | flops | bytes accessed | tf_op | source)
XLA Modules:
  0.0 723.4 jit_solution(6216898742349907182)
XLA Ops:
  13.4 17.2 %all_to_all.40 = bf16[8,72,640]{2,1,0:T(8,128)(2,1)} all-to-all(bf16[8,72,640]{2,1,0:T(8,128)(2,1)S(1)} %pad_maximum_fusion.2), channel_id=1, replica_groups=mesh['z'=4,'y'=2,'x'=2,'c'=2] {'y','x','c'}, dimensions={0} | all-to-all | bytes 1474560 | tf_op jit(solution)/shard_map/all_to_all | solution.py:99
  35.8 43.3 %collective-permute-done.1.refs_4_.refs_12_ = bf16[512,2048]{1,0:T(8,128)(2,1)} collective-permute-done((bf16[512,2048]{1,0:T(8,128)(2,1)S(1)}, bf16[512,2048]{1,0:T(8,128)(2,1)}, u32[]{:S(2)}, u32[]{:S(2)}) %collective-permute-start.1) | collective-permute-done | bytes 2097184 | tf_op jit(solution)/shard_map/ppermute | solution.py:53
  79.4 25.3 %all_to_all.41 = bf16[8,64,1536]{2,1,0:T(8,128)(2,1)} all-to-all(bf16[8,64,1536]{2,1,0:T(8,128)(2,1)} %get-tuple-element.92), channel_id=1, replica_groups=mesh['z'=4,'y'=2,'x'=2,'c'=2] {'y','x','c'}, dimensions={0} | all-to-all | bytes 3145728 | tf_op jit(solution)/shard_map/all_to_all | solution.py:99
  107.6 25.1 %collective-permute-done.12.refs_6_.refs_14_ = bf16[512,2048]{1,0:T(8,128)(2,1)} collective-permute-done((bf16[512,2048]{1,0:T(8,128)(2,1)S(1)}, bf16[512,2048]{1,0:T(8,128)(2,1)}, u32[]{:S(2)}, u32[]{:S(2)}) %collective-permute-start.12) | collective-permute-done | bytes 2097184 | tf_op jit(solution)/shard_map/ppermute | solution.py:57
  148.4 15.0 %norm_qkv.1 = (bf16[2048,2048]{1,0:T(8,128)(2,1)}, bf16[2048,256]{1,0:T(8,128)(2,1)}, bf16[2048,128]{1,0:T(8,128)(2,1)}) custom-call(bf16[512,2048]{1,0:T(8,128)(2,1)} %copy-done.9, bf16[512,2048]{1,0:T(8,128)(2,1)} %copy-done.15, bf16[512,2048]{1,0:T(8,128)(2,1)} %collective-permute-done.refs_2_.refs_10_, ...), custom_call_target="tpu_custom_call" | custom-call | flops 3221225472 | bytes 16777216 | tf_op jit(solution)/shard_map/norm_qkv/pallas_call | solution.py:289
  172.8 16.1 %all-to-all-done.2 = bf16[8,64,1536]{2,1,0:T(8,128)(2,1)} async-done(((bf16[8,64,1536]{2,1,0:T(8,128)(2,1)}), bf16[8,64,1536]{2,1,0:T(8,128)(2,1)}, u32[]{:S(2)}, u32[]{:S(2)}) %all-to-all-start.2) | async-done | bytes 1572896 | tf_op jit(solution)/shard_map/all_to_all | solution.py:99
  199.9 15.8 %attend.1 = (bf16[2048,256]{1,0:T(8,128)(2,1)}, bf16[8,256,256]{2,1,0:T(8,128)(2,1)}) custom-call(s32[8]{0:T(128)} %get-tuple-element.168.prev_at, s32[8]{0:T(128)} %iota_xor_fusion.index.refs_8_.here_at, bf16[2048,256]{1,0:T(8,128)(2,1)} %get-tuple-element.95.q_ref, bf16[2304,128]{1,0:T(8,128)(2,1)} %copy-done.30, bf16[2304,128]{1,0:T(8,128)(2,1)} %copy-done.30, ...), custom_call_target="tpu_custom_call" | custom-call | flops 4294967296 | bytes 2097152 | tf_op jit(solution)/shard_map/attend/pallas_call | solution.py:344
  220.9 14.5 %all-to-all-done.3.refs_9_ = bf16[8,256,256]{2,1,0:T(8,128)(2,1)} async-done(((bf16[8,256,256]{2,1,0:T(8,128)(2,1)}), bf16[8,256,256]{2,1,0:T(8,128)(2,1)}, u32[]{:S(2)}, u32[]{:S(2)}) %all-to-all-start.3) | async-done | bytes 1048608 | tf_op jit(solution)/shard_map/all_to_all | solution.py:99
  244.2 21.1 %collective-permute-done.18.refs_4_ = bf16[256,2048]{1,0:T(8,128)(2,1)S(1)} collective-permute-done((bf16[256,2048]{1,0:T(8,128)(2,1)}, bf16[256,2048]{1,0:T(8,128)(2,1)S(1)}, u32[]{:S(2)}, u32[]{:S(2)}) %collective-permute-start.18) | collective-permute-done | bytes 1048608 | tf_op jit(solution)/shard_map/ppermute | solution.py:53
  269.6 12.6 %collective-permute-done.20.refs_6_ = bf16[256,2048]{1,0:T(8,128)(2,1)S(1)} collective-permute-done((bf16[256,2048]{1,0:T(8,128)(2,1)S(1)}, bf16[256,2048]{1,0:T(8,128)(2,1)S(1)}, u32[]{:S(2)}, u32[]{:S(2)}) %collective-permute-start.20) | collective-permute-done | bytes 1048608 | tf_op jit(solution)/shard_map/ppermute | solution.py:57
  285.9 38.3 %ffn_chunk.2 = (bf16[2048,512]{1,0:T(8,128)(2,1)}, bf16[2048,1024]{1,0:T(8,128)(2,1)}, bf16[4,1536,512]{2,1,0:T(8,128)(2,1)}) custom-call(bf16[256,2048]{1,0:T(8,128)(2,1)} %get-tuple-element.104.refs_0_, bf16[256,2048]{1,0:T(8,128)(2,1)} %copy-done.36, bf16[256,2048]{1,0:T(8,128)(2,1)} %copy-done.25, bf16[256,2048]{1,0:T(8,128)(2,1)} %copy-done.38, ...), custom_call_target="tpu_custom_call" | custom-call | flops 38654705664 | bytes 29360128 | tf_op jit(solution)/shard_map/ffn_chunk/pallas_call | solution.py:523
  324.7 13.4 %down.7 = (f32[4,256,2048]{2,1,0:T(8,128)}, f32[4,256,2048]{2,1,0:T(8,128)}) custom-call(bf16[4,2,256,1024]{3,2,1,0:T(8,128)(2,1)} %bitcast.121, bf16[2048,1536]{1,0:T(8,128)(2,1)} %all-gather.6.cloned.1.call-done.refs_16_.refs_1_.refs_2_), custom_call_target="tpu_custom_call" | custom-call | flops 8589934592 | bytes 20971520 | tf_op jit(solution)/shard_map/down/pallas_call | solution.py:567
  338.1 38.2 %ffn_chunk.3 = (bf16[2048,512]{1,0:T(8,128)(2,1)}, bf16[2048,1024]{1,0:T(8,128)(2,1)}, bf16[4,1536,512]{2,1,0:T(8,128)(2,1)}) custom-call(bf16[256,2048]{1,0:T(8,128)(2,1)} %get-tuple-element.104.refs_0_, bf16[256,2048]{1,0:T(8,128)(2,1)} %copy-done.36, bf16[256,2048]{1,0:T(8,128)(2,1)} %copy-done.25, bf16[256,2048]{1,0:T(8,128)(2,1)} %copy-done.38, ...), custom_call_target="tpu_custom_call" | custom-call | flops 38654705664 | bytes 29360128 | tf_op jit(solution)/shard_map/ffn_chunk/pallas_call | solution.py:523
  376.4 10.2 %down.9 = (bf16[2,256,2048]{2,1,0:T(8,128)(2,1)}, bf16[2,256,2048]{2,1,0:T(8,128)(2,1)}) custom-call(bf16[4,2,256,1024]{3,2,1,0:T(8,128)(2,1)} %bitcast.93, bf16[2048,1536]{1,0:T(8,128)(2,1)} %all-gather.8.cloned.1.call-done.refs_16_.refs_1_.refs_3_, f32[4,256,2048]{2,1,0:T(8,128)} %get-tuple-element.107.refs_2_, f32[4,256,2048]{2,1,0:T(8,128)} %get-tuple-element.110.refs_3_), custom_call_target="tpu_custom_call" | custom-call | flops 4294967296 | bytes 12582912 | tf_op jit(solution)/shard_map/down/pallas_call | solution.py:567
  386.7 10.3 %down.8 = (bf16[2,256,2048]{2,1,0:T(8,128)(2,1)}, bf16[2,256,2048]{2,1,0:T(8,128)(2,1)}) custom-call(bf16[4,2,256,1024]{3,2,1,0:T(8,128)(2,1)} %bitcast.94, bf16[2048,1536]{1,0:T(8,128)(2,1)} %all-gather.8.cloned.1.call-done.refs_16_.refs_1_.refs_3_, f32[4,256,2048]{2,1,0:T(8,128)} %get-tuple-element.107.refs_2_, f32[4,256,2048]{2,1,0:T(8,128)} %get-tuple-element.110.refs_3_), custom_call_target="tpu_custom_call" | custom-call | flops 4294967296 | bytes 12582912 | tf_op jit(solution)/shard_map/down/pallas_call | solution.py:567
  404.9 10.6 %collective-permute-done.24 = bf16[256,2048]{1,0:T(8,128)(2,1)S(1)} collective-permute-done((bf16[256,2048]{1,0:T(8,128)(2,1)S(1)}, bf16[256,2048]{1,0:T(8,128)(2,1)S(1)}, u32[]{:S(2)}, u32[]{:S(2)}) %collective-permute-start.24) | collective-permute-done | bytes 1048608 | tf_op jit(solution)/shard_map/ppermute | solution.py:57
  420.6 20.0 %collective-permute-done.26.refs_11_ = bf16[256,2048]{1,0:T(8,128)(2,1)S(1)} collective-permute-done((bf16[256,2048]{1,0:T(8,128)(2,1)S(1)}, bf16[256,2048]{1,0:T(8,128)(2,1)S(1)}, u32[]{:S(2)}, u32[]{:S(2)}) %collective-permute-start.26) | collective-permute-done | bytes 1048608 | tf_op jit(solution)/shard_map/ppermute | solution.py:53
  443.0 11.3 %open_attention.1 = (f32[256,2048]{1,0:T(8,128)}, bf16[256,2048]{1,0:T(8,128)(2,1)}, bf16[8,256,256]{2,1,0:T(8,128)(2,1)}) custom-call(bf16[2048,256]{1,0:T(8,128)(2,1)} %slice.181.refs_0_, bf16[2048,256]{1,0:T(8,128)(2,1)} %collective-permute-done.3.refs_1_, bf16[2048,256]{1,0:T(8,128)(2,1)} %collective-permute-done.4.refs_2_, ...), custom_call_target="tpu_custom_call" | custom-call | flops 2147483648 | bytes 8388608 | tf_op jit(solution)/shard_map/open_attention/pallas_call | solution.py:639
  454.4 19.8 %all_to_all.42.do_ref = bf16[8,256,256]{2,1,0:T(8,128)(2,1)} all-to-all(bf16[8,256,256]{2,1,0:T(8,128)(2,1)} %get-tuple-element.115), channel_id=1, replica_groups=mesh['z'=4,'y'=2,'x'=2,'c'=2] {'y','x','c'}, dimensions={0} | all-to-all | bytes 2097152 | tf_op jit(solution)/shard_map/all_to_all | solution.py:99
  475.3 23.1 %collective-permute-done.31.refs_4_ = bf16[256,2048]{1,0:T(8,128)(2,1)S(1)} collective-permute-done((bf16[256,2048]{1,0:T(8,128)(2,1)S(1)}, bf16[256,2048]{1,0:T(8,128)(2,1)S(1)}, u32[]{:S(2)}, u32[]{:S(2)}) %collective-permute-start.31) | collective-permute-done | bytes 1048608 | tf_op jit(solution)/shard_map/ppermute | solution.py:53
  502.9 13.1 %collective-permute-done.33.refs_6_ = bf16[256,2048]{1,0:T(8,128)(2,1)} collective-permute-done((bf16[256,2048]{1,0:T(8,128)(2,1)}, bf16[256,2048]{1,0:T(8,128)(2,1)}, u32[]{:S(2)}, u32[]{:S(2)}) %collective-permute-start.33) | collective-permute-done | bytes 1048608 | tf_op jit(solution)/shard_map/ppermute | solution.py:57
  517.9 26.1 %attend_back.1 = (bf16[2048,256]{1,0:T(8,128)(2,1)}, f32[2304,128]{1,0:T(8,128)}) custom-call(s32[8]{0:T(128)} %iota_xor_fusion.index.refs_8_.here_at, s32[8]{0:T(128)} %get-tuple-element.167.prev_at, bf16[2048,256]{1,0:T(8,128)(2,1)} %get-tuple-element.95.q_ref, bf16[8,256,256]{2,1,0:T(8,128)(2,1)} %all_to_all.42.do_ref, bf16[2304,128]{1,0:T(8,128)(2,1)} %copy-done.30, ...), custom_call_target="tpu_custom_call" | custom-call | flops 10737418240 | bytes 4194304 | tf_op jit(solution)/shard_map/attend_back/pallas_call | solution.py:434
  638.5 28.9 %all-to-all-done.7.refs_1_ = bf16[8,64,1536]{2,1,0:T(8,128)(2,1)} async-done(((bf16[8,64,1536]{2,1,0:T(8,128)(2,1)}), bf16[8,64,1536]{2,1,0:T(8,128)(2,1)}, u32[]{:S(2)}, u32[]{:S(2)}) %all-to-all-start.7) | async-done | bytes 1572896 | tf_op jit(solution)/shard_map/all_to_all | solution.py:99
  692.7 11.6 %collective-permute-done.38 = bf16[256,2048]{1,0:T(8,128)(2,1)} collective-permute-done((bf16[256,2048]{1,0:T(8,128)(2,1)}, bf16[256,2048]{1,0:T(8,128)(2,1)}, u32[]{:S(2)}, u32[]{:S(2)}) %collective-permute-start.38) | collective-permute-done | bytes 1048608 | tf_op jit(solution)/shard_map/ppermute | solution.py:53
  (287 shorter events, 227.1 us)
Async XLA Ops:
  7.2 127.1 %all-gather.4.cloned.1.call-start = ((), (), s32[]{:S(2)}) async-start(), calls=%async_computation.11 | async-start | bytes 3686400 | tf_op jit(solution)/shard_map/all_gather | solution.py:110
  30.6 190.3 %all-gather.6.cloned.1.call-start = ((), (), s32[]{:S(2)}) async-start(), calls=%async_computation.12 | async-start | bytes 7864320 | tf_op jit(solution)/shard_map/all_gather | solution.py:110
  30.9 48.2 %collective-permute-start.1 = (bf16[512,2048]{1,0:T(8,128)(2,1)S(1)}, bf16[512,2048]{1,0:T(8,128)(2,1)}, u32[]{:S(2)}, u32[]{:S(2)}) collective-permute-start(bf16[512,2048]{1,0:T(8,128)(2,1)S(1)} %constant_dynamic-update-slice_fusion.refs_0_.refs_8_), channel_id=1, source_target_pairs={{0,4},{1,5},{2,6},{3,7},{4,0},{5,1},{6,2},{7,3},{8,12},{9,13},{10,... | collective-permute-start | bytes 6291464 | tf_op jit(solution)/shard_map/ppermute | solution.py:53
  31.6 47.8 %collective-permute-start = (bf16[512,2048]{1,0:T(8,128)(2,1)S(1)}, bf16[512,2048]{1,0:T(8,128)(2,1)}, u32[]{:S(2)}, u32[]{:S(2)}) collective-permute-start(bf16[512,2048]{1,0:T(8,128)(2,1)S(1)} %constant_dynamic-update-slice_fusion.refs_0_.refs_8_), channel_id=1, source_target_pairs={{0,2},{1,3},{2,0},{3,1},{4,6},{5,7},{6,4},{7,5},{8,10},{9,11},{10,... | collective-permute-start | bytes 6291464 | tf_op jit(solution)/shard_map/ppermute | solution.py:53
  107.1 41.3 %collective-permute-start.11 = (bf16[512,2048]{1,0:T(8,128)(2,1)}, bf16[512,2048]{1,0:T(8,128)(2,1)}, u32[]{:S(2)}, u32[]{:S(2)}) collective-permute-start(bf16[512,2048]{1,0:T(8,128)(2,1)} %collective-permute-done.1.refs_4_.refs_12_), channel_id=1, source_target_pairs={{0,1},{1,0},{2,3},{3,2},{4,5},{5,4},{6,7},{7,6},{8,9},{9,8},{10,11... | collective-permute-start | bytes 6291464 | tf_op jit(solution)/shard_map/ppermute | solution.py:53
  107.1 41.3 %collective-permute-start.10 = (bf16[512,2048]{1,0:T(8,128)(2,1)}, bf16[512,2048]{1,0:T(8,128)(2,1)}, u32[]{:S(2)}, u32[]{:S(2)}) collective-permute-start(bf16[512,2048]{1,0:T(8,128)(2,1)} %collective-permute-done.refs_2_.refs_10_), channel_id=1, source_target_pairs={{0,1},{1,0},{2,3},{3,2},{4,5},{5,4},{6,7},{7,6},{8,9},{9,8},{10,11... | collective-permute-start | bytes 6291464 | tf_op jit(solution)/shard_map/ppermute | solution.py:53
  137.3 30.9 %collective-permute-start.6 = (bf16[2048,256]{1,0:T(8,128)(2,1)}, bf16[2048,256]{1,0:T(8,128)(2,1)}, u32[]{:S(2)}, u32[]{:S(2)}) collective-permute-start(bf16[2048,256]{1,0:T(8,128)(2,1)} %slice.181.refs_0_), channel_id=1, source_target_pairs={{0,4},{1,5},{2,6},{3,7},{4,0},{5,1},{6,2},{7,3},{8,12},{9,13},{10,... | collective-permute-start | bytes 3145736 | tf_op jit(solution)/shard_map/ppermute | solution.py:53
  137.8 30.3 %collective-permute-start.4 = (bf16[2048,256]{1,0:T(8,128)(2,1)}, bf16[2048,256]{1,0:T(8,128)(2,1)}, u32[]{:S(2)}, u32[]{:S(2)}) collective-permute-start(bf16[2048,256]{1,0:T(8,128)(2,1)} %slice.181.refs_0_), channel_id=1, source_target_pairs={{0,2},{1,3},{2,0},{3,1},{4,6},{5,7},{6,4},{7,5},{8,10},{9,11},{10,... | collective-permute-start | bytes 3145736 | tf_op jit(solution)/shard_map/ppermute | solution.py:53
  167.8 170.4 %all-gather.8.cloned.1.call-start = ((), (), s32[]{:S(2)}) async-start(), calls=%async_computation.13 | async-start | bytes 7864320 | tf_op jit(solution)/shard_map/all_gather | solution.py:110
  220.0 297.9 %reduce-scatter.4.cloned.1.call-start = ((), (), s32[]{:S(2)}) async-start(), calls=%async_computation.14 | async-start | bytes 7864320 | tf_op jit(solution)/shard_map/reduce_scatter | solution.py:700
  324.2 281.2 %reduce-scatter.8.cloned.1.call-start = ((), (), s32[]{:S(2)}) async-start(), calls=%async_computation.16 | async-start | bytes 7864320 | tf_op jit(solution)/shard_map/reduce_scatter | solution.py:700
  502.2 44.0 %collective-permute-start.28 = (bf16[256,2048]{1,0:T(8,128)(2,1)}, bf16[256,2048]{1,0:T(8,128)(2,1)}, u32[]{:S(2)}, u32[]{:S(2)}) collective-permute-start(bf16[256,2048]{1,0:T(8,128)(2,1)} %get-tuple-element.122.refs_0_), channel_id=1, source_target_pairs={{0,1},{1,0},{2,3},{3,2},{4,5},{5,4},{6,7},{7,6},{8,9},{9,8},{10,11... | collective-permute-start | bytes 3145736 | tf_op jit(solution)/shard_map/ppermute | solution.py:53
  502.3 44.0 %collective-permute-start.32 = (bf16[256,2048]{1,0:T(8,128)(2,1)}, bf16[256,2048]{1,0:T(8,128)(2,1)}, u32[]{:S(2)}, u32[]{:S(2)}) collective-permute-start(bf16[256,2048]{1,0:T(8,128)(2,1)} %copy-done.11), channel_id=1, source_target_pairs={{0,1},{1,0},{2,3},{3,2},{4,5},{5,4},{6,7},{7,6},{8,9},{9,8},{10,11... | collective-permute-start | bytes 3145736 | tf_op jit(solution)/shard_map/ppermute | solution.py:53
  502.8 43.5 %collective-permute-start.30 = (bf16[256,2048]{1,0:T(8,128)(2,1)}, bf16[256,2048]{1,0:T(8,128)(2,1)}, u32[]{:S(2)}, u32[]{:S(2)}) collective-permute-start(bf16[256,2048]{1,0:T(8,128)(2,1)} %copy-done.12), channel_id=1, source_target_pairs={{0,1},{1,0},{2,3},{3,2},{4,5},{5,4},{6,7},{7,6},{8,9},{9,8},{10,11... | collective-permute-start | bytes 3145736 | tf_op jit(solution)/shard_map/ppermute | solution.py:53
  515.9 30.4 %collective-permute-start.34 = (bf16[256,2048]{1,0:T(8,128)(2,1)}, bf16[256,2048]{1,0:T(8,128)(2,1)}, u32[]{:S(2)}, u32[]{:S(2)}) collective-permute-start(bf16[256,2048]{1,0:T(8,128)(2,1)} %collective-permute-done.33.refs_6_), channel_id=1, source_target_pairs={{0,1},{1,0},{2,3},{3,2},{4,5},{5,4},{6,7},{7,6},{8,9},{9,8},{10,11... | collective-permute-start | bytes 3145736 | tf_op jit(solution)/shard_map/ppermute | solution.py:53
  575.2 33.5 %collective-permute-start.41 = (bf16[2,256,2048]{2,1,0:T(8,128)(2,1)}, bf16[2,256,2048]{2,1,0:T(8,128)(2,1)}, u32[]{:S(2)}, u32[]{:S(2)}) collective-permute-start(bf16[2,256,2048]{2,1,0:T(8,128)(2,1)} %get-tuple-element.135), channel_id=1, source_target_pairs={{0,1},{1,0},{2,3},{3,2},{4,5},{5,4},{6,7},{7,6},{8,9},{9,8},{10,11... | collective-permute-start | bytes 6291464 | tf_op jit(solution)/shard_map/ppermute | solution.py:53
  583.8 30.2 %collective-permute-start.36 = (bf16[2,256,2048]{2,1,0:T(8,128)(2,1)}, bf16[2,256,2048]{2,1,0:T(8,128)(2,1)}, u32[]{:S(2)}, u32[]{:S(2)}) collective-permute-start(bf16[2,256,2048]{2,1,0:T(8,128)(2,1)} %get-tuple-element.129), channel_id=1, source_target_pairs={{0,1},{1,0},{2,3},{3,2},{4,5},{5,4},{6,7},{7,6},{8,9},{9,8},{10,11... | collective-permute-start | bytes 6291464 | tf_op jit(solution)/shard_map/ppermute | solution.py:53
  587.6 32.9 %all-to-all-start.6 = ((bf16[8,64,1536]{2,1,0:T(8,128)(2,1)}), bf16[8,64,1536]{2,1,0:T(8,128)(2,1)S(1)}, u32[]{:S(2)}, u32[]{:S(2)}) async-start(bf16[8,64,1536]{2,1,0:T(8,128)(2,1)} %turn.4), calls=%async_computation.8 | async-start | bytes 3145728 | tf_op jit(solution)/shard_map/all_to_all | solution.py:99
  591.1 95.6 %reduce-scatter.6.cloned.1.call-start = ((), (), s32[]{:S(2)}) async-start(), calls=%async_computation.15 | async-start | bytes 3276800 | tf_op jit(solution)/shard_map/reduce_scatter | solution.py:700
  599.8 35.0 %collective-permute-start.35 = (bf16[2,256,2048]{2,1,0:T(8,128)(2,1)}, bf16[2,256,2048]{2,1,0:T(8,128)(2,1)}, u32[]{:S(2)}, u32[]{:S(2)}) collective-permute-start(bf16[2,256,2048]{2,1,0:T(8,128)(2,1)} %get-tuple-element.127), channel_id=1, source_target_pairs={{0,1},{1,0},{2,3},{3,2},{4,5},{5,4},{6,7},{7,6},{8,9},{9,8},{10,11... | collective-permute-start | bytes 6291464 | tf_op jit(solution)/shard_map/ppermute | solution.py:53
  618.8 55.6 %collective-permute-start.37 = (bf16[256,2048]{1,0:T(8,128)(2,1)}, bf16[256,2048]{1,0:T(8,128)(2,1)}, u32[]{:S(2)}, u32[]{:S(2)}) collective-permute-start(bf16[256,2048]{1,0:T(8,128)(2,1)} %slice_bitcast_fusion.5), channel_id=1, source_target_pairs={{0,2},{1,5},{2,0},{3,7},{4,6},{5,1},{6,4},{7,3},{8,10},{9,13},{10,... | collective-permute-start | bytes 3145736 | tf_op jit(solution)/shard_map/ppermute | solution.py:57
  620.5 47.0 %all-to-all-start.7 = ((bf16[8,64,1536]{2,1,0:T(8,128)(2,1)}), bf16[8,64,1536]{2,1,0:T(8,128)(2,1)}, u32[]{:S(2)}, u32[]{:S(2)}) async-start(bf16[8,64,1536]{2,1,0:T(8,128)(2,1)} %turn.5), calls=%async_computation.10 | async-start | bytes 3145728 | tf_op jit(solution)/shard_map/all_to_all | solution.py:99
  631.4 49.5 %collective-permute-start.43 = (bf16[256,2048]{1,0:T(8,128)(2,1)}, bf16[256,2048]{1,0:T(8,128)(2,1)}, u32[]{:S(2)}, u32[]{:S(2)}) collective-permute-start(bf16[256,2048]{1,0:T(8,128)(2,1)} %get-tuple-element.153), channel_id=1, source_target_pairs={{0,2},{1,3},{2,0},{3,1},{4,6},{5,7},{6,4},{7,5},{8,10},{9,11},{10,... | collective-permute-start | bytes 3145736 | tf_op jit(solution)/shard_map/ppermute | solution.py:53
  633.3 47.6 %collective-permute-start.44 = (bf16[256,2048]{1,0:T(8,128)(2,1)}, bf16[256,2048]{1,0:T(8,128)(2,1)}, u32[]{:S(2)}, u32[]{:S(2)}) collective-permute-start(bf16[256,2048]{1,0:T(8,128)(2,1)} %get-tuple-element.154), channel_id=1, source_target_pairs={{0,4},{1,5},{2,6},{3,7},{4,0},{5,1},{6,2},{7,3},{8,12},{9,13},{10,... | collective-permute-start | bytes 3145736 | tf_op jit(solution)/shard_map/ppermute | solution.py:53
  (72 other events, 1009.7 us)
Sparse Core Ops, SparseCore 0:
  30.7 59.6 all-gather.3
  104.8 114.7 all-gather.5
  221.1 114.8 all-gather.7
  338.7 108.9 reduce-scatter.3
  449.9 112.6 reduce-scatter.7
  605.6 57.3 reduce-scatter.5

commit v3 on v2

--- a/solution.py
+++ b/solution.py
@@ -49,6 +49,14 @@
 TN = ((0,), (0,))
 
 
+def after(value, *first):
+    return lax.optimization_barrier((value, *first))[0]
+
+
+def rms_norm(values, scales):
+    return values * lax.rsqrt(jnp.mean(values * values, axis=-1, keepdims=True) + NORM_EPS) * scales
+
+
 def swap(value, rel):
     return lax.ppermute(value, PLANE, [(i, i ^ rel) for i in range(TP)])
 
@@ -78,17 +86,18 @@
     return (left.astype(F32) + right.astype(F32)).astype(BF)
 
 
-def scatter_plane(part):
+def scatter_plane(part, wait=()):
     even, odd = part((3, 2))
     both = add(even, swap(odd, 1))
     across, over_y = swap_across(both[0]), both[1]
     even, odd = part((1, 0))
     both = add(even, swap(odd, 1))
     over_x, own = both[0], both[1]
+    across = after(across, *wait)
     first = on_first()
     over_x = jnp.where(first, over_x, add(over_x, across))
     over_y = jnp.where(first, add(over_y, across), over_y)
-    return own, swap(over_x, 2), swap(over_y, 4)
+    return (own, swap(over_x, 2), swap(over_y, 4)), (over_x, over_y)
 
 
 def total(own, from_x, from_y):
@@ -110,14 +119,14 @@
     return lax.all_gather(own, "z", axis=0, tiled=True)
 
 
-def start_rows(refs, dst, sems, first=0):
-    each = dst.shape[0] // TP
+def start_rows(refs, dst, sems):
+    each = dst.shape[0] // len(refs)
     for r, ref in enumerate(refs):
-        pltpu.make_async_copy(ref.at[pl.ds(first, each)], dst.at[pl.ds(r * each, each)], sems.at[r]).start()
-
-
-def wait_rows(r, dst, sems):
-    each = dst.shape[0] // TP
+        pltpu.make_async_copy(ref, dst.at[pl.ds(r * each, each)], sems.at[r]).start()
+
+
+def wait_rows(r, dst, sems, count=TP):
+    each = dst.shape[0] // count
     part = dst.at[pl.ds(pl.multiple_of(r * each, each), each)]
     pltpu.make_async_copy(part, part, sems.at[r]).wait()
 
@@ -257,13 +266,13 @@
     w_copy = pltpu.make_async_copy(w_all.at[:, pl.ds(0, w_s.shape[1]), pl.ds(0, w_s.shape[2])], w_s, w_sem)
     w_copy.start()
     start_rows(blocks, x_s, sems)
-    each = x_s.shape[0] // TP
+    each = x_s.shape[0] // count
     lane = lax.broadcasted_iota(jnp.int32, (each, 2 * HD), 1)
     w_copy.wait()
 
     def step(r, carry):
         at = pl.ds(pl.multiple_of(r * each, each), each)
-        wait_rows(r, x_s, sems)
+        wait_rows(r, x_s, sems, count)
         x = x_s[at, :].astype(F32)
         scale = lax.rsqrt(jnp.mean(x * x, axis=-1, keepdims=True) + NORM_EPS)
         normed = (x * scale * gain[...]).astype(BF)
@@ -280,7 +289,7 @@
         kv_out[at, :] = jnp.where(lane < HD, turned, kv).astype(BF)
         return carry
 
-    lax.fori_loop(0, TP, step, 0)
+    lax.fori_loop(0, count, step, 0)
 
 
 def norm_qkv(blocks, gain, w_all, cos, sin):
@@ -298,7 +307,7 @@
         scratch_shapes=[
             pltpu.VMEM((tokens, D), BF),
             pltpu.VMEM((w_all.shape[0], each, QW + 2 * HD), BF),
-            pltpu.SemaphoreType.DMA((TP,)),
+            pltpu.SemaphoreType.DMA((len(blocks),)),
             pltpu.SemaphoreType.DMA,
         ],
         cost_estimate=cost(2 * tokens * D * (QW + 2 * HD), 4 * tokens * D),
@@ -463,37 +472,30 @@
     )(here_at, prev_at, q, d_o, kv9, kv9, lo_row, cos, sin, ek, ev)
 
 
-def ffn_kernel(count, *refs):
-    n2_blocks, dy_blocks = refs[:count], refs[count : 2 * count]
-    w, act_out, dgu_out, grad_out, n2, dy, flat, held, n2_sems, dy_sems, out_sems = refs[2 * count :]
-    start_rows(n2_blocks, n2, n2_sems)
-    start_rows(dy_blocks, dy, dy_sems, dy.shape[0] // TP)
+def ffn_forward(r, n2, dy, w, act_out, dgu_out, flat):
     each = n2.shape[0] // TP
     width = act_out.shape[1]
     two = 2 * width
-
-    def forward(r, carry):
-        at = pl.ds(pl.multiple_of(r * each, each), each)
-        wait_rows(r, n2, n2_sems)
-        wait_rows(r, dy, dy_sems)
-        gate_up = jnp.dot(n2[at, :], w[:, :two], preferred_element_type=F32)
-        d_act = jnp.dot(dy[at, :], w[:, two:], preferred_element_type=F32)
-        g, u = gate_up[:, :width], gate_up[:, width:]
-        sg = jax.nn.sigmoid(g)
-        gs = g * sg
-        act = (gs * u).astype(BF)
-        d_g = (d_act * u * (sg * (1.0 + g * (1.0 - sg)))).astype(BF)
-        d_u = (d_act * gs).astype(BF)
-        act_out[at, :] = act
-        dgu_out[at, :width] = d_g
-        dgu_out[at, width:] = d_u
-        flat[:width, at] = d_g.T
-        flat[width:two, at] = d_u.T
-        flat[two:, at] = act.T
-        return carry
-
-    lax.fori_loop(0, TP, forward, 0)
-    planes, _, cols = grad_out.shape
+    at = pl.ds(pl.multiple_of(r * each, each), each)
+    gate_up = jnp.dot(n2[at, :], w[:, :two], preferred_element_type=F32)
+    d_act = jnp.dot(dy[at, :], w[:, two:], preferred_element_type=F32)
+    g, u = gate_up[:, :width], gate_up[:, width:]
+    sg = jax.nn.sigmoid(g)
+    gs = g * sg
+    act = (gs * u).astype(BF)
+    d_g = (d_act * u * (sg * (1.0 + g * (1.0 - sg)))).astype(BF)
+    d_u = (d_act * gs).astype(BF)
+    act_out[at, :] = act
+    dgu_out[at, :width] = d_g
+    dgu_out[at, width:] = d_u
+    flat[:width, at] = d_g.T
+    flat[width:two, at] = d_u.T
+    flat[two:, at] = act.T
+
+
+def ffn_back(flat, n2, dy, grad_out, held, out_sems):
+    planes, wide, cols = grad_out.shape
+    two = 2 * wide // 3
 
     def leave(z):
         return pltpu.make_async_copy(held.at[lax.rem(z, 2)], grad_out.at[z], out_sems.at[lax.rem(z, 2)])
@@ -516,32 +518,79 @@
     leave(planes - 1).wait()
 
 
-def ffn_chunk(n2_blocks, dy_blocks, w):
+def ffn_kernel(*refs):
+    n2_blocks, dy_blocks = refs[:TP], refs[TP : 2 * TP]
+    w, act_out, dgu_out, grad_out, n2, dy, flat, held, n2_sems, dy_sems, out_sems = refs[2 * TP :]
+    start_rows(n2_blocks, n2, n2_sems)
+    start_rows(dy_blocks, dy, dy_sems)
+
+    def forward(r, carry):
+        wait_rows(r, n2, n2_sems)
+        wait_rows(r, dy, dy_sems)
+        ffn_forward(r, n2, dy, w, act_out, dgu_out, flat)
+        return carry
+
+    lax.fori_loop(0, TP, forward, 0)
+    ffn_back(flat, n2, dy, grad_out, held, out_sems)
+
+
+def ffn_forward_kernel(*refs):
+    n2_blocks, dy_blocks = refs[:TP], refs[TP : 2 * TP]
+    w, act_out, dgu_out, flat, n2, dy, n2_sems, dy_sems = refs[2 * TP :]
+    start_rows(n2_blocks, n2, n2_sems)
+    start_rows(dy_blocks, dy, dy_sems)
+
+    def forward(r, carry):
+        wait_rows(r, n2, n2_sems)
+        wait_rows(r, dy, dy_sems)
+        ffn_forward(r, n2, dy, w, act_out, dgu_out, flat)
+        return carry
+
+    lax.fori_loop(0, TP, forward, 0)
+
+
+def ffn_back_kernel(*refs):
+    n2_blocks, dy_blocks = refs[:TP], refs[TP : 2 * TP]
+    flat, grad_out, n2, dy, held, n2_sems, dy_sems, out_sems = refs[2 * TP :]
+    start_rows(n2_blocks, n2, n2_sems)
+    start_rows(dy_blocks, dy, dy_sems)
+    for r in range(TP):
+        wait_rows(r, n2, n2_sems)
+    for r in range(TP):
+        wait_rows(r, dy, dy_sems)
+    ffn_back(flat, n2, dy, grad_out, held, out_sems)
+
+
+def ffn_call(kernel, n2_blocks, dy_blocks, last, outs, flops):
     tokens = TP * n2_blocks[0].shape[0]
     planes = lax.axis_size("z")
-    width = w.shape[1] // 3
-    return pl.pallas_call(
-        functools.partial(ffn_kernel, len(n2_blocks)),
-        out_shape=(
-            jax.ShapeDtypeStruct((tokens, width), BF),
-            jax.ShapeDtypeStruct((tokens, 2 * width), BF),
-            jax.ShapeDtypeStruct((planes, 3 * width, D // planes), BF),
-        ),
-        in_specs=[ANY] * (2 * len(n2_blocks)) + [VMEM],
-        out_specs=(VMEM, VMEM, ANY),
-        scratch_shapes=[
-            pltpu.VMEM((tokens, D), BF),
-            pltpu.VMEM((tokens, D), BF),
-            pltpu.VMEM((3 * width, tokens), BF),
-            pltpu.VMEM((2, 3 * width, D // planes), BF),
-            pltpu.SemaphoreType.DMA((TP,)),
-            pltpu.SemaphoreType.DMA((TP,)),
-            pltpu.SemaphoreType.DMA((2,)),
-        ],
-        cost_estimate=cost(18 * tokens * D * width, 4 * tokens * D + 12 * width * D),
-        compiler_params=BIG,
-        name="ffn_chunk",
-    )(*n2_blocks, *dy_blocks, w)
+    wide = last.shape[1] if 2 not in outs or 0 in outs else last.shape[0]
+    width = wide // 3
+    shapes, specs, extra, sems = [], [], [], []
+    if 0 in outs:
+        shapes += [jax.ShapeDtypeStruct((tokens, width), BF), jax.ShapeDtypeStruct((tokens, 2 * width), BF)]
+        specs += [VMEM, VMEM]
+    if 1 in outs:
+        shapes.append(jax.ShapeDtypeStruct((wide, tokens), BF))
+        specs.append(VMEM)
+    if 2 in outs:
+        shapes.append(jax.ShapeDtypeStruct((planes, wide, D // planes), BF))
+        specs.append(ANY)
+        extra = ([pltpu.VMEM((wide, tokens), BF)] if 0 in outs else []) + [pltpu.VMEM((2, wide, D // planes), BF)]
+        sems = [pltpu.SemaphoreType.DMA((2,))]
+    return pl.pallas_call(
+        kernel,
+        out_shape=shapes,
+        in_specs=[ANY] * (2 * TP) + [VMEM],
+        out_specs=specs,
+        scratch_shapes=[pltpu.VMEM((tokens, D), BF), pltpu.VMEM((tokens, D), BF)]
+        + extra
+        + [pltpu.SemaphoreType.DMA((TP,)), pltpu.SemaphoreType.DMA((TP,))]
+        + sems,
+        cost_estimate=cost(flops * tokens * D * width, 4 * tokens * D + 12 * width * D),
+        compiler_params=BIG,
+        name="ffn",
+    )(*n2_blocks, *dy_blocks, last)
 
 
 def down_kernel(parts, *refs):
@@ -682,14 +731,6 @@
     )(*blocks, left)
 
 
-def after(value, *first):
-    return lax.optimization_barrier((value, *first))[0]
-
-
-def rms_norm(values, scales):
-    return values * lax.rsqrt(jnp.mean(values * values, axis=-1, keepdims=True) + NORM_EPS) * scales
-
-
 def to_pieces(pieces):
     rows, cols = pieces.shape[1:]
     return trade(pieces).reshape(TP * rows, cols)
@@ -733,11 +774,12 @@
     attn_pieces = cut_attn(w_attn, perm)
     attn_pieces = jnp.concatenate([attn_pieces, jnp.broadcast_to(extra, (TP, *extra.shape))], axis=1)
     attn_rows = to_pieces(attn_pieces)
-    both_begun = gather_begin(jnp.concatenate([hidden_in, out_grad], axis=0))
-    pieces = cut_ffn(w_ffn)
-    rows_0 = to_pieces(after(pieces[0], *both_begun[1:]))
+    x_begun = gather_begin(hidden_in)
+    pieces = cut_ffn(after(w_ffn, attn_rows))
+    rows_0 = to_pieces(pieces[0])
     w_0 = gather_z(rows_0)
-    both_blocks = gather_end(*both_begun)
+    x_blocks = gather_end(*x_begun)
+    dy_begun = gather_begin(after(out_grad, *x_begun[1:]))
     attn_all = after(gather_z(attn_rows), rows_0).reshape(-1, rows + EXTRA, AW)
     w_own = attn_all[:, :rows].reshape(D, AW)
     wqkv, wo = w_own[:, : QW + 2 * HD], w_own[:, QW + 2 * HD :]
@@ -751,36 +793,49 @@
     cosine = jnp.tile(jnp.cos(angles), (1, GROUP))
     sine = jnp.tile(jnp.sin(angles), (1, GROUP))
 
-    n1, q, kv = norm_qkv(both_blocks, gains_full[:1], attn_all, cosine, sine)
+    early = 6
+    halves = []
+    for first, last in ((0, early), (early, TP)):
+        at = slice(first * tok, last * tok)
+        halves.append(norm_qkv(x_blocks[first:last], gains_full[:1], attn_all, cosine[at], sine[at]))
+    (n1, q, kv), (n1_late, q_late, kv_late) = halves
+    q, kv = jnp.concatenate([q, q_late], axis=0), jnp.concatenate([kv, kv_late], axis=0)
     wo_begun = gather_begin(wo)
-    q = after(q, *wo_begun[1:])
-    rows_1 = to_pieces(after(pieces[1], n1))
+    rows_1 = to_pieces(after(pieces[1], attn_all))
+    q = after(q, rows_1, *wo_begun[1:], *dy_begun[1:])
     before = along_z(pick(kv.reshape(TP, tok, 2 * HD), me ^ (TP - 1)), 1)
     kv9 = jnp.concatenate([kv, before], axis=0)
     prev_at = jnp.where(rel == 0, TP, (rel - 1) ^ me)
     mixed, heads = attend(prev_at, rel, q, kv9, lo.reshape(tokens, 1), ek, ev)
 
     wo_blocks = gather_end(*wo_begun)
-    heads = trade(after(heads, rows_1))
+    heads = trade(heads)
+    dy_blocks = gather_end(*after(dy_begun, mixed))
     w_1 = gather_z(rows_1)
     x_own = hidden_in.astype(F32)
     residual, normed_two = close_attention(wo_blocks, rel, heads, after(hidden_in, w_0), gains_full[1:])
     n2_blocks = gather_plane(normed_two)
 
-    act_0, d_gu_0, grad_0 = ffn_chunk(n2_blocks, both_blocks, w_0)
+    act_0, d_gu_0, grad_0 = ffn_call(ffn_kernel, n2_blocks, dy_blocks, w_0, (0, 2), 18)
     so_far = down([d_gu_0], [w_0], False, (0, 1, 2, 3), kind=F32)
     sum_0 = sum_z(grad_0)
-    act_1, d_gu_1, grad_1 = ffn_chunk(n2_blocks, both_blocks, after(w_1, so_far[0]))
+    act_1, d_gu_1, flat_1 = ffn_call(ffn_forward_kernel, n2_blocks, dy_blocks, after(w_1, so_far[0]), (0, 1), 9)
+    d_n2_parts = {groups: down([d_gu_1], [w_1], False, groups, so_far) for groups in ((3, 2), (1, 0))}
+    d_n2_terms, unused = scatter_plane(d_n2_parts.get)
+    (grad_1,) = ffn_call(ffn_back_kernel, n2_blocks, dy_blocks, after(flat_1, d_n2_parts[1, 0][0]), (2,), 9)
     sum_1 = sum_z(grad_1)
-    d_n2_terms = scatter_plane(lambda groups: down([d_gu_1], [w_1], False, groups, so_far))
+    acts, w_all = [after(act_0, grad_1), act_1], [w_0, w_1]
+    f_parts = {groups: down(acts, w_all, True, groups) for groups in ((3, 2), (1, 0))}
+    d_n2_terms = after(d_n2_terms, *f_parts.values())
     d_resid, d_att, d_heads = open_attention(wo_blocks, rel, d_n2_terms, residual, out_grad, gains_full[1:])
     d_o = trade(d_heads)
     d_att_begun = gather_begin(after(d_att, d_o))
-
     here_at = me ^ steps
     prev_abs = jnp.where(steps == 0, TP, (steps - 1) ^ me)
     d_q, d_kv9 = attend_back(here_at, prev_abs, q, after(d_o, sum_0), kv9, lo.reshape(TP, 1, tok), cosine, sine, ek, ev)
-    d_att_blocks = gather_end(after(d_att_begun[0], d_q), *d_att_begun[1:])
+    f_terms, unused = scatter_plane(lambda groups: after(f_parts[groups], d_heads), (d_q,))
+    hidden_out = (residual + total(*f_terms)).astype(BF)
+    d_att_blocks = gather_end(*after(d_att_begun, d_q))
     wo_grad = turn_grad(mixed, d_att_blocks)
     back = along_z(d_kv9[tokens:].astype(BF), -1)
     last = me ^ (TP - 1)
@@ -791,20 +846,19 @@
     d_qkv = jnp.concatenate(
         [d_q, (a * c + b * s).astype(BF), (b * c - a * s).astype(BF), d_kv[:, HD:].astype(BF)], axis=1
     )
-    qkv_grad = by_plane(mm(d_qkv, n1, TN).astype(BF))
+    cut = early * tok
+    qkv_grad = by_plane((mm(d_qkv[:cut], n1, TN) + mm(d_qkv[cut:], n1_late, TN)).astype(BF))
     attn_sum = jnp.concatenate([qkv_grad, wo_grad], axis=1)
     attn_back = give_back(sum_z(attn_sum))
-    d_qkv = after(d_qkv, attn_sum)
-    d_normed = total(*scatter_plane(lambda groups: down([d_qkv], [wqkv], False, groups)))
-    acts = [after(act_0, attn_sum), act_1]
-    f_terms = scatter_plane(lambda groups: down(acts, [w_0, w_1], True, groups))
-    hidden_out = (residual + total(*f_terms)).astype(BF)
-    ffn_back = [give_back(v) for v in (sum_0, sum_1)]
+    d_qkv = after(d_qkv, attn_sum, *f_terms)
+    d_n1_terms, unused = scatter_plane(lambda groups: down([d_qkv], [wqkv], False, groups))
+    d_normed = total(*d_n1_terms)
+    pieces = [give_back(v) for v in (sum_0, sum_1)]
     scale = lax.rsqrt(jnp.mean(x_own * x_own, axis=-1, keepdims=True) + NORM_EPS)
     unit = x_own * scale
     d_unit = d_normed * gains_full[0]
     in_grad = d_resid + scale * (d_unit - unit * jnp.mean(d_unit * unit, axis=-1, keepdims=True))
-    ffn_grad, term_two = paste_ffn(ffn_back, w_ffn)
+    ffn_grad, term_two = paste_ffn(pieces, w_ffn)
     attn_grad, term_one = paste_attn(attn_back, w_attn, perm)
     gains_grad = jnp.concatenate([term_one, term_two], axis=1).T / gains.astype(F32)
     return hidden_out, in_grad.astype(BF), attn_grad, ffn_grad, gains_grad

time: 735 us -> 682 us (0.928)
  waiting for transfers between devices: 253 us -> 184 us
  blocking collectives: 62.3 us -> 42.5 us
  Pallas kernels: 246 us -> 260 us
  local copies, waits for them, and re-layouts: 33 us -> 43.2 us
  starting transfers between devices: 54.6 us -> 64.5 us
    ppermute x36 -> x42, waiting for transfers between devices: 126 us -> 71.9 us  [swap(): return lax.ppermute(value, PLANE, [(i, i ^ rel) for i in range(TP)])]
    all_to_all x5 -> x6, waiting for transfers between devices: 59.4 us -> 34.3 us  [trade(): return lax.all_to_all(blocks, PLANE, 0, 0, tiled=True)]
    all_to_all x3 -> x2, blocking collectives: 62.3 us -> 42.5 us  [trade(): return lax.all_to_all(blocks, PLANE, 0, 0, tiled=True)]
    pallas_call x2 -> x3, Pallas kernels: 76.5 us -> 87.8 us  [ffn_call(): pl.pallas_call(kernel, out_shape=shapes, in_specs=[ANY] * (2 * TP) + [VME...]
    ppermute x7 -> x8, waiting for transfers between devices: 61.4 us -> 69 us  [swap_across(): lax.ppermute(value, PLANE, [(i, i ^ 2 + 2 * (i % 2)) for i in range(TP)])]
    all_to_all x5 -> x6, starting transfers between devices: 20 us -> 25.5 us  [trade(): return lax.all_to_all(blocks, PLANE, 0, 0, tiled=True)]
    ppermute x36 -> x42, starting transfers between devices: 18.2 us -> 22.7 us  [swap(): return lax.ppermute(value, PLANE, [(i, i ^ rel) for i in range(TP)])]
    pallas_call x1 -> x2, Pallas kernels: 15 us -> 17.8 us  [norm_qkv(): pl.pallas_call(functools.partial(qkv_kernel, len(blocks)), out_shape=(jax...]
  transfers between devices with their start and end apart: 56 -> 64, of which waited for: 21 -> 21; matrix products, arithmetic and copies ran while one was open for 11% -> 13% of each run, Pallas kernels for 33% -> 38%
where the time goes in v3:
time: 682 us; the launch traced here: 672 us
  Pallas kernels  260 us (38%)
  waiting for transfers between devices  184 us (27%)
  starting transfers between devices  64.5 us (9%)
  other arithmetic  58.6 us (9%)
  local copies, waits for them, and re-layouts  43.2 us (6%)
  blocking collectives  42.5 us (6%)
  between operations  15.7 us (2%)
    pallas_call x3, Pallas kernels, ffn_call(): pl.pallas_call(kernel, out_shape=shapes, in_specs=[ANY] * (2 * TP) + [VME...  87.8 us
    ppermute x42, waiting for transfers between devices, swap(): return lax.ppermute(value, PLANE, [(i, i ^ rel) for i in range(TP)])  71.9 us
    ppermute x8, waiting for transfers between devices, swap_across(): lax.ppermute(value, PLANE, [(i, i ^ 2 + 2 * (i % 2)) for i in range(TP)])  69 us
    pallas_call x7, Pallas kernels, down(): pl.pallas_call(functools.partial(down_kernel, count), out_shape=[jax.Shap...  61.2 us
    all_to_all x2, blocking collectives, trade(): return lax.all_to_all(blocks, PLANE, 0, 0, tiled=True)  42.5 us
    all_to_all x6, waiting for transfers between devices, trade(): return lax.all_to_all(blocks, PLANE, 0, 0, tiled=True)  34.3 us
    pallas_call x1, Pallas kernels, attend_back(): pl.pallas_call(attend_back_kernel, out_shape=(jax.ShapeDtypeStruct((token...  26.1 us
    all_to_all x6, starting transfers between devices, trade(): return lax.all_to_all(blocks, PLANE, 0, 0, tiled=True)  25.5 us
  transfers between devices with their start and end apart: 64, of which 21 were waited for; matrix products, arithmetic and copies ran while one was open for 13% of the time, Pallas kernels for 38%

profile of v3, /device:TPU:0, one launch (start us, length us, event | category | flops | bytes accessed | tf_op | source)
XLA Modules:
  0.0 672.3 jit_solution(13761800817334074988)
XLA Ops:
  13.3 17.1 %all_to_all.40 = bf16[8,72,640]{2,1,0:T(8,128)(2,1)} all-to-all(bf16[8,72,640]{2,1,0:T(8,128)(2,1)S(1)} %pad_maximum_fusion.3), channel_id=1, replica_groups=mesh['z'=4,'y'=2,'x'=2,'c'=2] {'y','x','c'}, dimensions={0} | all-to-all | bytes 1474560 | tf_op jit(solution)/shard_map/all_to_all | solution.py:108
  34.1 25.4 %all_to_all.41 = bf16[8,64,1536]{2,1,0:T(8,128)(2,1)} all-to-all(bf16[8,64,1536]{2,1,0:T(8,128)(2,1)} %get-tuple-element.111), channel_id=1, replica_groups=mesh['z'=4,'y'=2,'x'=2,'c'=2] {'y','x','c'}, dimensions={0} | all-to-all | bytes 3145728 | tf_op jit(solution)/shard_map/all_to_all | solution.py:108
  62.5 21.4 %collective-permute-done.10.refs_4_ = bf16[256,2048]{1,0:T(8,128)(2,1)} collective-permute-done((bf16[256,2048]{1,0:T(8,128)(2,1)S(1)}, bf16[256,2048]{1,0:T(8,128)(2,1)}, u32[]{:S(2)}, u32[]{:S(2)}) %collective-permute-start.10) | collective-permute-done | bytes 1048608 | tf_op jit(solution)/shard_map/ppermute | solution.py:61
  90.4 10.1 %collective-permute-done.12.refs_0_ = bf16[256,2048]{1,0:T(8,128)(2,1)} collective-permute-done((bf16[256,2048]{1,0:T(8,128)(2,1)S(1)}, bf16[256,2048]{1,0:T(8,128)(2,1)}, u32[]{:S(2)}, u32[]{:S(2)}) %collective-permute-start.12) | collective-permute-done | bytes 1048608 | tf_op jit(solution)/shard_map/ppermute | solution.py:65
  132.1 11.9 %norm_qkv.2 = (bf16[1536,2048]{1,0:T(8,128)(2,1)}, bf16[1536,256]{1,0:T(8,128)(2,1)}, bf16[1536,128]{1,0:T(8,128)(2,1)}) custom-call(bf16[256,2048]{1,0:T(8,128)(2,1)} %refs_10_, bf16[256,2048]{1,0:T(8,128)(2,1)} %collective-permute-done.7.refs_1_, bf16[256,2048]{1,0:T(8,128)(2,1)} %collective-permute-done.8.refs_2_, ...), custom_call_target="tpu_custom_call" | custom-call | flops 2415919104 | bytes 12582912 | tf_op jit(solution)/shard_map/norm_qkv/pallas_call | solution.py:298
  170.0 11.2 %collective-permute-done.5.refs_6_ = bf16[2048,256]{1,0:T(8,128)(2,1)} collective-permute-done((bf16[2048,256]{1,0:T(8,128)(2,1)}, bf16[2048,256]{1,0:T(8,128)(2,1)}, u32[]{:S(2)}, u32[]{:S(2)}) %collective-permute-start.5) | collective-permute-done | bytes 1048608 | tf_op jit(solution)/shard_map/ppermute | solution.py:65
  181.3 15.8 %attend.1 = (bf16[2048,256]{1,0:T(8,128)(2,1)}, bf16[8,256,256]{2,1,0:T(8,128)(2,1)}) custom-call(s32[8]{0:T(128)} %get-tuple-element.208.prev_at, s32[8]{0:T(128)} %iota_xor_fusion.index.refs_8_.here_at, bf16[2048,256]{1,0:T(8,128)(2,1)} %pad_maximum_fusion.2.q_ref, bf16[2304,128]{1,0:T(8,128)(2,1)} %copy-done.33, bf16[2304,128]{1,0:T(8,128)(2,1)} %copy-done.33, ...), custom_call_target="tpu_custom_call" | custom-call | flops 4294967296 | bytes 2097152 | tf_op jit(solution)/shard_map/attend/pallas_call | solution.py:353
  205.9 10.3 %all-to-all-done.3.refs_9_ = bf16[8,256,256]{2,1,0:T(8,128)(2,1)S(1)} async-done(((bf16[8,256,256]{2,1,0:T(8,128)(2,1)}), bf16[8,256,256]{2,1,0:T(8,128)(2,1)S(1)}, u32[]{:S(2)}, u32[]{:S(2)}) %all-to-all-start.3) | async-done | bytes 1048608 | tf_op jit(solution)/shard_map/all_to_all | solution.py:108
  229.7 21.7 %collective-permute-done.21.refs_4_ = bf16[256,2048]{1,0:T(8,128)(2,1)S(1)} collective-permute-done((bf16[256,2048]{1,0:T(8,128)(2,1)}, bf16[256,2048]{1,0:T(8,128)(2,1)S(1)}, u32[]{:S(2)}, u32[]{:S(2)}) %collective-permute-start.21) | collective-permute-done | bytes 1048608 | tf_op jit(solution)/shard_map/ppermute | solution.py:61
  252.2 8.8 %collective-permute-done.27.refs_14_ = bf16[256,2048]{1,0:T(8,128)(2,1)S(1)} collective-permute-done((bf16[256,2048]{1,0:T(8,128)(2,1)S(1)}, bf16[256,2048]{1,0:T(8,128)(2,1)S(1)}, u32[]{:S(2)}, u32[]{:S(2)}) %collective-permute-start.27) | collective-permute-done | bytes 1048608 | tf_op jit(solution)/shard_map/ppermute | solution.py:65
  262.0 10.2 %collective-permute-done.23.refs_6_ = bf16[256,2048]{1,0:T(8,128)(2,1)S(1)} collective-permute-done((bf16[256,2048]{1,0:T(8,128)(2,1)S(1)}, bf16[256,2048]{1,0:T(8,128)(2,1)S(1)}, u32[]{:S(2)}, u32[]{:S(2)}) %collective-permute-start.23) | collective-permute-done | bytes 1048608 | tf_op jit(solution)/shard_map/ppermute | solution.py:65
  276.3 38.6 %ffn.3 = (bf16[2048,512]{1,0:T(8,128)(2,1)}, bf16[2048,1024]{1,0:T(8,128)(2,1)}, bf16[4,1536,512]{2,1,0:T(8,128)(2,1)}) custom-call(bf16[256,2048]{1,0:T(8,128)(2,1)} %get-tuple-element.124.refs_0_, bf16[256,2048]{1,0:T(8,128)(2,1)} %copy-done.54, bf16[256,2048]{1,0:T(8,128)(2,1)} %copy-done.25, bf16[256,2048]{1,0:T(8,128)(2,1)} %copy-done.56, ...), custom_call_target="tpu_custom_call" | custom-call | flops 38654705664 | bytes 29360128 | tf_op jit(solution)/shard_map/ffn/pallas_call | solution.py:581
  315.4 13.4 %down.7 = (f32[4,256,2048]{2,1,0:T(8,128)}, f32[4,256,2048]{2,1,0:T(8,128)}) custom-call(bf16[4,2,256,1024]{3,2,1,0:T(8,128)(2,1)} %bitcast.140, bf16[2048,1536]{1,0:T(8,128)(2,1)} %all-gather.6.cloned.1.call-done.refs_16_.refs_1_.refs_2_), custom_call_target="tpu_custom_call" | custom-call | flops 8589934592 | bytes 20971520 | tf_op jit(solution)/shard_map/down/pallas_call | solution.py:616
  328.8 25.4 %ffn.4 = (bf16[2048,512]{1,0:T(8,128)(2,1)}, bf16[2048,1024]{1,0:T(8,128)(2,1)}, bf16[1536,2048]{1,0:T(8,128)(2,1)}) custom-call(bf16[256,2048]{1,0:T(8,128)(2,1)} %get-tuple-element.124.refs_0_, bf16[256,2048]{1,0:T(8,128)(2,1)} %copy-done.54, bf16[256,2048]{1,0:T(8,128)(2,1)} %copy-done.25, bf16[256,2048]{1,0:T(8,128)(2,1)} %copy-done.56, ...), custom_call_target="tpu_custom_call" | custom-call | flops 19327352832 | bytes 29360128 | tf_op jit(solution)/shard_map/ffn/pallas_call | solution.py:581
  354.2 10.3 %down.10 = (bf16[2,256,2048]{2,1,0:T(8,128)(2,1)}, bf16[2,256,2048]{2,1,0:T(8,128)(2,1)}) custom-call(bf16[4,2,256,1024]{3,2,1,0:T(8,128)(2,1)} %bitcast.110, bf16[2048,1536]{1,0:T(8,128)(2,1)} %all-gather.8.cloned.1.call-done.refs_16_.refs_1_.refs_3_, f32[4,256,2048]{2,1,0:T(8,128)} %get-tuple-element.132.refs_2_, f32[4,256,2048]{2,1,0:T(8,128)} %get-tuple-element.136.refs_3_), custom_call_target="tpu_custom_call" | custom-call | flops 4294967296 | bytes 12582912 | tf_op jit(solution)/shard_map/down/pallas_call | solution.py:616
  364.8 10.2 %down.8 = (bf16[2,256,2048]{2,1,0:T(8,128)(2,1)}, bf16[2,256,2048]{2,1,0:T(8,128)(2,1)}) custom-call(bf16[4,2,256,1024]{3,2,1,0:T(8,128)(2,1)} %bitcast.111, bf16[2048,1536]{1,0:T(8,128)(2,1)} %all-gather.8.cloned.1.call-done.refs_16_.refs_1_.refs_3_, f32[4,256,2048]{2,1,0:T(8,128)} %get-tuple-element.132.refs_2_, f32[4,256,2048]{2,1,0:T(8,128)} %get-tuple-element.136.refs_3_), custom_call_target="tpu_custom_call" | custom-call | flops 4294967296 | bytes 12582912 | tf_op jit(solution)/shard_map/down/pallas_call | solution.py:616
  378.1 23.8 %ffn.5 = bf16[4,1536,512]{2,1,0:T(8,128)(2,1)} custom-call(bf16[256,2048]{1,0:T(8,128)(2,1)} %get-tuple-element.124.refs_0_, bf16[256,2048]{1,0:T(8,128)(2,1)} %copy-done.54, bf16[256,2048]{1,0:T(8,128)(2,1)} %copy-done.25, bf16[256,2048]{1,0:T(8,128)(2,1)} %copy-done.56, bf16[256,2048]{1,0:T(8,128)(2,1)} %copy-done.24, bf16[256,2048]{1,0:T(8,128)(2,1)} %copy-done.55, ...), custom_call_target="tpu_custom_call" | custom-call | flops 19327352832 | bytes 29360128 | tf_op jit(solution)/shard_map/ffn/pallas_call | solution.py:581
  433.0 11.5 %open_attention.1 = (f32[256,2048]{1,0:T(8,128)}, bf16[256,2048]{1,0:T(8,128)(2,1)}, bf16[8,256,256]{2,1,0:T(8,128)(2,1)}) custom-call(bf16[2048,256]{1,0:T(8,128)(2,1)} %copy-done.5, bf16[2048,256]{1,0:T(8,128)(2,1)} %collective-permute-done.refs_1_, bf16[2048,256]{1,0:T(8,128)(2,1)} %copy-done.7, bf16[2048,256]{1,0:T(8,128)(2,1)} %collective-permute-done.2.refs_3_, ...), custom_call_target="tpu_custom_call" | custom-call | flops 2147483648 | bytes 8388608 | tf_op jit(solution)/shard_map/open_attention/pallas_call | solution.py:688
  475.1 26.1 %attend_back.1 = (bf16[2048,256]{1,0:T(8,128)(2,1)}, f32[2304,128]{1,0:T(8,128)}) custom-call(s32[8]{0:T(128)} %iota_xor_fusion.index.refs_8_.here_at, s32[8]{0:T(128)} %get-tuple-element.207.prev_at, bf16[2048,256]{1,0:T(8,128)(2,1)} %pad_maximum_fusion.2.q_ref, bf16[8,256,256]{2,1,0:T(8,128)(2,1)} %all-to-all-done.4.do_ref, bf16[2304,128]{1,0:T(8,128)(2,1)} %copy-done.33, ...), custom_call_target="tpu_custom_call" | custom-call | flops 10737418240 | bytes 4194304 | tf_op jit(solution)/shard_map/attend_back/pallas_call | solution.py:443
  516.4 9.1 %collective-permute-done.45.refs_6_ = bf16[256,2048]{1,0:T(8,128)(2,1)S(1)} collective-permute-done((bf16[256,2048]{1,0:T(8,128)(2,1)S(1)}, bf16[256,2048]{1,0:T(8,128)(2,1)S(1)}, u32[]{:S(2)}, u32[]{:S(2)}) %collective-permute-start.45) | collective-permute-done | bytes 1048608 | tf_op jit(solution)/shard_map/ppermute | solution.py:65
  531.8 8.7 %turn_grad.1 = bf16[4,256,512]{2,1,0:T(8,128)(2,1)} custom-call(bf16[256,2048]{1,0:T(8,128)(2,1)} %get-tuple-element.166.refs_0_, bf16[256,2048]{1,0:T(8,128)(2,1)} %collective-permute-done.42.refs_1_, bf16[256,2048]{1,0:T(8,128)(2,1)} %collective-permute-done.40.refs_2_, bf16[256,2048]{1,0:T(8,128)(2,1)} %copy-done.20, bf16[256,2048]{1,0:T(8,128)(2,1)} %copy-done.10, ...), custom_call_target="tpu_custom_call" | custom-call | flops 2147483648 | bytes 8388608 | tf_op jit(solution)/shard_map/turn_grad/pallas_call | solution.py:722
  574.1 19.5 %collective-permute-done.49 = bf16[256,2048]{1,0:T(8,128)(2,1)} collective-permute-done((bf16[256,2048]{1,0:T(8,128)(2,1)S(1)}, bf16[256,2048]{1,0:T(8,128)(2,1)}, u32[]{:S(2)}, u32[]{:S(2)}) %collective-permute-start.49) | collective-permute-done | bytes 1048608 | tf_op jit(solution)/shard_map/ppermute | solution.py:65
  609.7 10.0 %all-to-all-done.7.refs_1_ = bf16[8,64,1536]{2,1,0:T(8,128)(2,1)} async-done(((bf16[8,64,1536]{2,1,0:T(8,128)(2,1)}), bf16[8,64,1536]{2,1,0:T(8,128)(2,1)}, u32[]{:S(2)}, u32[]{:S(2)}) %all-to-all-start.7) | async-done | bytes 1572896 | tf_op jit(solution)/shard_map/all_to_all | solution.py:108
  626.7 14.1 %collective-permute-done.50 = bf16[256,2048]{1,0:T(8,128)(2,1)} collective-permute-done((bf16[256,2048]{1,0:T(8,128)(2,1)}, bf16[256,2048]{1,0:T(8,128)(2,1)}, u32[]{:S(2)}, u32[]{:S(2)}) %collective-permute-start.50) | collective-permute-done | bytes 1048608 | tf_op jit(solution)/shard_map/ppermute | solution.py:61
  (359 shorter events, 271.7 us)
Async XLA Ops:
  7.2 94.1 %all-gather.4.cloned.1.call-start = ((), (), s32[]{:S(2)}) async-start(), calls=%async_computation.11 | async-start | bytes 3686400 | tf_op jit(solution)/shard_map/all_gather | solution.py:119
  30.4 175.5 %all-gather.6.cloned.1.call-start = ((), (), s32[]{:S(2)}) async-start(), calls=%async_computation.12 | async-start | bytes 7864320 | tf_op jit(solution)/shard_map/all_gather | solution.py:119
  60.7 44.5 %collective-permute-start.7 = (bf16[256,2048]{1,0:T(8,128)(2,1)S(1)}, bf16[256,2048]{1,0:T(8,128)(2,1)}, u32[]{:S(2)}, u32[]{:S(2)}) collective-permute-start(bf16[256,2048]{1,0:T(8,128)(2,1)S(1)} %copy-done), channel_id=1, source_target_pairs={{0,1},{1,0},{2,3},{3,2},{4,5},{5,4},{6,7},{7,6},{8,9},{9,8},{10,11... | collective-permute-start | bytes 3145736 | tf_op jit(solution)/shard_map/ppermute | solution.py:61
  89.9 38.9 %collective-permute-start.11 = (bf16[256,2048]{1,0:T(8,128)(2,1)}, bf16[256,2048]{1,0:T(8,128)(2,1)}, u32[]{:S(2)}, u32[]{:S(2)}) collective-permute-start(bf16[256,2048]{1,0:T(8,128)(2,1)} %collective-permute-done.10.refs_4_), channel_id=1, source_target_pairs={{0,1},{1,0},{2,3},{3,2},{4,5},{5,4},{6,7},{7,6},{8,9},{9,8},{10,11... | collective-permute-start | bytes 3145736 | tf_op jit(solution)/shard_map/ppermute | solution.py:61
  89.9 40.6 %collective-permute-start.9 = (bf16[256,2048]{1,0:T(8,128)(2,1)}, bf16[256,2048]{1,0:T(8,128)(2,1)}, u32[]{:S(2)}, u32[]{:S(2)}) collective-permute-start(bf16[256,2048]{1,0:T(8,128)(2,1)} %collective-permute-done.8.refs_2_), channel_id=1, source_target_pairs={{0,1},{1,0},{2,3},{3,2},{4,5},{5,4},{6,7},{7,6},{8,9},{9,8},{10,11... | collective-permute-start | bytes 3145736 | tf_op jit(solution)/shard_map/ppermute | solution.py:61
  103.6 41.5 %collective-permute-start.3 = (bf16[2048,256]{1,0:T(8,128)(2,1)S(1)}, bf16[2048,256]{1,0:T(8,128)(2,1)S(1)}, u32[]{:S(2)}, u32[]{:S(2)}) collective-permute-start(bf16[2048,256]{1,0:T(8,128)(2,1)S(1)} %slice.230.refs_0_), channel_id=1, source_target_pairs={{0,4},{1,5},{2,6},{3,7},{4,0},{5,1},{6,2},{7,3},{8,12},{9,13},{10,... | collective-permute-start | bytes 3145736 | tf_op jit(solution)/shard_map/ppermute | solution.py:61
  105.2 40.0 %collective-permute-start.1 = (bf16[2048,256]{1,0:T(8,128)(2,1)S(1)}, bf16[2048,256]{1,0:T(8,128)(2,1)S(1)}, u32[]{:S(2)}, u32[]{:S(2)}) collective-permute-start(bf16[2048,256]{1,0:T(8,128)(2,1)S(1)} %slice.230.refs_0_), channel_id=1, source_target_pairs={{0,2},{1,3},{2,0},{3,1},{4,6},{5,7},{6,4},{7,5},{8,10},{9,11},{10,... | collective-permute-start | bytes 3145736 | tf_op jit(solution)/shard_map/ppermute | solution.py:61
  116.6 40.2 %all-to-all-start.2 = ((bf16[8,64,1536]{2,1,0:T(8,128)(2,1)}), bf16[8,64,1536]{2,1,0:T(8,128)(2,1)}, u32[]{:S(2)}, u32[]{:S(2)}) async-start(bf16[8,64,1536]{2,1,0:T(8,128)(2,1)} %get-tuple-element.116), calls=%async_computation.2 | async-start | bytes 3145728 | tf_op jit(solution)/shard_map/all_to_all | solution.py:108
  120.9 207.9 %all-gather.8.cloned.1.call-start = ((), (), s32[]{:S(2)}) async-start(), calls=%async_computation.13 | async-start | bytes 7864320 | tf_op jit(solution)/shard_map/all_gather | solution.py:119
  122.6 38.3 %collective-permute-start.16 = (bf16[256,2048]{1,0:T(8,128)(2,1)}, bf16[256,2048]{1,0:T(8,128)(2,1)}, u32[]{:S(2)}, u32[]{:S(2)}) collective-permute-start(bf16[256,2048]{1,0:T(8,128)(2,1)} %refs_13_.1), channel_id=1, source_target_pairs={{0,1},{1,0},{2,3},{3,2},{4,5},{5,4},{6,7},{7,6},{8,9},{9,8},{10,11... | collective-permute-start | bytes 3145736 | tf_op jit(solution)/shard_map/ppermute | solution.py:61
  128.8 40.3 %collective-permute-start.15 = (bf16[256,2048]{1,0:T(8,128)(2,1)}, bf16[256,2048]{1,0:T(8,128)(2,1)}, u32[]{:S(2)}, u32[]{:S(2)}) collective-permute-start(bf16[256,2048]{1,0:T(8,128)(2,1)} %refs_13_.1), channel_id=1, source_target_pairs={{0,4},{1,5},{2,6},{3,7},{4,0},{5,1},{6,2},{7,3},{8,12},{9,13},{10,... | collective-permute-start | bytes 3145736 | tf_op jit(solution)/shard_map/ppermute | solution.py:61
  130.6 39.5 %collective-permute-start.14 = (bf16[256,2048]{1,0:T(8,128)(2,1)}, bf16[256,2048]{1,0:T(8,128)(2,1)}, u32[]{:S(2)}, u32[]{:S(2)}) collective-permute-start(bf16[256,2048]{1,0:T(8,128)(2,1)} %refs_13_.1), channel_id=1, source_target_pairs={{0,2},{1,3},{2,0},{3,1},{4,6},{5,7},{6,4},{7,5},{8,10},{9,11},{10,... | collective-permute-start | bytes 3145736 | tf_op jit(solution)/shard_map/ppermute | solution.py:61
  161.0 44.9 %collective-permute-start.4 = (bf16[2048,256]{1,0:T(8,128)(2,1)S(1)}, bf16[2048,256]{1,0:T(8,128)(2,1)}, u32[]{:S(2)}, u32[]{:S(2)}) collective-permute-start(bf16[2048,256]{1,0:T(8,128)(2,1)S(1)} %collective-permute-done.3.refs_4_), channel_id=1, source_target_pairs={{0,1},{1,0},{2,3},{3,2},{4,5},{5,4},{6,7},{7,6},{8,9},{9,8},{10,11... | collective-permute-start | bytes 3145736 | tf_op jit(solution)/shard_map/ppermute | solution.py:61
  169.1 36.8 %collective-permute-start.2 = (bf16[2048,256]{1,0:T(8,128)(2,1)S(1)}, bf16[2048,256]{1,0:T(8,128)(2,1)}, u32[]{:S(2)}, u32[]{:S(2)}) collective-permute-start(bf16[2048,256]{1,0:T(8,128)(2,1)S(1)} %collective-permute-done.1.refs_2_), channel_id=1, source_target_pairs={{0,1},{1,0},{2,3},{3,2},{4,5},{5,4},{6,7},{7,6},{8,9},{9,8},{10,11... | collective-permute-start | bytes 3145736 | tf_op jit(solution)/shard_map/ppermute | solution.py:61
  200.8 274.3 %reduce-scatter.4.cloned.1.call-start = ((), (), s32[]{:S(2)}) async-start(), calls=%async_computation.14 | async-start | bytes 7864320 | tf_op jit(solution)/shard_map/reduce_scatter | solution.py:741
  315.0 253.0 %reduce-scatter.8.cloned.1.call-start = ((), (), s32[]{:S(2)}) async-start(), calls=%async_computation.16 | async-start | bytes 7864320 | tf_op jit(solution)/shard_map/reduce_scatter | solution.py:741
  449.4 193.7 %reduce-scatter.6.cloned.1.call-start = ((), (), s32[]{:S(2)}) async-start(), calls=%async_computation.15 | async-start | bytes 3276800 | tf_op jit(solution)/shard_map/reduce_scatter | solution.py:741
  464.8 39.0 %collective-permute-start.42 = (bf16[256,2048]{1,0:T(8,128)(2,1)}, bf16[256,2048]{1,0:T(8,128)(2,1)}, u32[]{:S(2)}, u32[]{:S(2)}) collective-permute-start(bf16[256,2048]{1,0:T(8,128)(2,1)} %get-tuple-element.166.refs_0_), channel_id=1, source_target_pairs={{0,1},{1,0},{2,3},{3,2},{4,5},{5,4},{6,7},{7,6},{8,9},{9,8},{10,11... | collective-permute-start | bytes 3145736 | tf_op jit(solution)/shard_map/ppermute | solution.py:61
  464.8 39.0 %collective-permute-start.41 = (bf16[256,2048]{1,0:T(8,128)(2,1)}, bf16[256,2048]{1,0:T(8,128)(2,1)S(1)}, u32[]{:S(2)}, u32[]{:S(2)}) collective-permute-start(bf16[256,2048]{1,0:T(8,128)(2,1)} %get-tuple-element.166.refs_0_), channel_id=1, source_target_pairs={{0,4},{1,5},{2,6},{3,7},{4,0},{5,1},{6,2},{7,3},{8,12},{9,13},{10,... | collective-permute-start | bytes 3145736 | tf_op jit(solution)/shard_map/ppermute | solution.py:61
  465.3 38.5 %collective-permute-start.40 = (bf16[256,2048]{1,0:T(8,128)(2,1)}, bf16[256,2048]{1,0:T(8,128)(2,1)}, u32[]{:S(2)}, u32[]{:S(2)}) collective-permute-start(bf16[256,2048]{1,0:T(8,128)(2,1)} %get-tuple-element.166.refs_0_), channel_id=1, source_target_pairs={{0,2},{1,3},{2,0},{3,1},{4,6},{5,7},{6,4},{7,5},{8,10},{9,11},{10,... | collective-permute-start | bytes 3145736 | tf_op jit(solution)/shard_map/ppermute | solution.py:61
  470.0 35.6 %collective-permute-start.36 = (bf16[256,2048]{1,0:T(8,128)(2,1)}, bf16[256,2048]{1,0:T(8,128)(2,1)}, u32[]{:S(2)}, u32[]{:S(2)}) collective-permute-start(bf16[256,2048]{1,0:T(8,128)(2,1)} %slice_bitcast_fusion.5), channel_id=1, source_target_pairs={{0,2},{1,5},{2,0},{3,7},{4,6},{5,1},{6,4},{7,3},{8,10},{9,13},{10,... | collective-permute-start | bytes 3145736 | tf_op jit(solution)/shard_map/ppermute | solution.py:65
  557.7 36.0 %all-to-all-start.6 = ((bf16[8,64,1536]{2,1,0:T(8,128)(2,1)}), bf16[8,64,1536]{2,1,0:T(8,128)(2,1)}, u32[]{:S(2)}, u32[]{:S(2)}) async-start(bf16[8,64,1536]{2,1,0:T(8,128)(2,1)} %turn.4), calls=%async_computation.8 | async-start | bytes 3145728 | tf_op jit(solution)/shard_map/all_to_all | solution.py:108
  601.9 38.9 %collective-permute-start.50 = (bf16[256,2048]{1,0:T(8,128)(2,1)}, bf16[256,2048]{1,0:T(8,128)(2,1)}, u32[]{:S(2)}, u32[]{:S(2)}) collective-permute-start(bf16[256,2048]{1,0:T(8,128)(2,1)} %get-tuple-element.191), channel_id=1, source_target_pairs={{0,2},{1,3},{2,0},{3,1},{4,6},{5,7},{6,4},{7,5},{8,10},{9,11},{10,... | collective-permute-start | bytes 3145736 | tf_op jit(solution)/shard_map/ppermute | solution.py:61
  603.7 37.0 %collective-permute-start.51 = (bf16[256,2048]{1,0:T(8,128)(2,1)}, bf16[256,2048]{1,0:T(8,128)(2,1)}, u32[]{:S(2)}, u32[]{:S(2)}) collective-permute-start(bf16[256,2048]{1,0:T(8,128)(2,1)} %get-tuple-element.192), channel_id=1, source_target_pairs={{0,4},{1,5},{2,6},{3,7},{4,0},{5,1},{6,2},{7,3},{8,12},{9,13},{10,... | collective-permute-start | bytes 3145736 | tf_op jit(solution)/shard_map/ppermute | solution.py:61
  (100 other events, 1431.6 us)
Sparse Core Ops, SparseCore 0:
  30.5 59.6 all-gather.3
  91.7 114.0 all-gather.5
  207.4 114.7 all-gather.7
  324.4 108.9 reduce-scatter.3
  435.6 112.6 reduce-scatter.7
  550.4 54.0 reduce-scatter.5

commit v4 on v3

--- a/solution.py
+++ b/solution.py
@@ -849,11 +849,13 @@
     cut = early * tok
     qkv_grad = by_plane((mm(d_qkv[:cut], n1, TN) + mm(d_qkv[cut:], n1_late, TN)).astype(BF))
     attn_sum = jnp.concatenate([qkv_grad, wo_grad], axis=1)
-    attn_back = give_back(sum_z(attn_sum))
+    turned = turn(sum_z(attn_sum))
+    attn_back = trade(turned)
     d_qkv = after(d_qkv, attn_sum, *f_terms)
     d_n1_terms, unused = scatter_plane(lambda groups: down([d_qkv], [wqkv], False, groups))
     d_normed = total(*d_n1_terms)
-    pieces = [give_back(v) for v in (sum_0, sum_1)]
+    pieces = [give_back(sum_0), give_back(sum_1)]
+    pieces[1] = after(pieces[1], turned)
     scale = lax.rsqrt(jnp.mean(x_own * x_own, axis=-1, keepdims=True) + NORM_EPS)
     unit = x_own * scale
     d_unit = d_normed * gains_full[0]

time: 682 us -> 670 us (0.982)
  waiting for transfers between devices: 184 us -> 169 us
    ppermute x8, waiting for transfers between devices: 69 us -> 54.4 us  [swap_across(): lax.ppermute(value, PLANE, [(i, i ^ 2 + 2 * (i % 2)) for i in range(TP)])]
    unnamed x126 -> x130, local copies, waits for them, and re-layouts: 14.1 us -> 15.5 us
  transfers between devices with their start and end apart: 64 -> 64, of which waited for: 21 -> 21; matrix products, arithmetic and copies ran while one was open for 13% -> 14% of each run, Pallas kernels for 38% -> 39%
where the time goes in v4:
time: 670 us; the launch traced here: 660 us
  Pallas kernels  260 us (39%)
  waiting for transfers between devices  169 us (25%)
  starting transfers between devices  65.1 us (10%)
  other arithmetic  58.3 us (9%)
  local copies, waits for them, and re-layouts  45.4 us (7%)
  blocking collectives  42.5 us (6%)
  between operations  15.8 us (2%)
    pallas_call x3, Pallas kernels, ffn_call(): pl.pallas_call(kernel, out_shape=shapes, in_specs=[ANY] * (2 * TP) + [VME...  87.8 us
    ppermute x42, waiting for transfers between devices, swap(): return lax.ppermute(value, PLANE, [(i, i ^ rel) for i in range(TP)])  70.5 us
    pallas_call x7, Pallas kernels, down(): pl.pallas_call(functools.partial(down_kernel, count), out_shape=[jax.Shap...  61.3 us
    ppermute x8, waiting for transfers between devices, swap_across(): lax.ppermute(value, PLANE, [(i, i ^ 2 + 2 * (i % 2)) for i in range(TP)])  54.4 us
    all_to_all x2, blocking collectives, trade(): return lax.all_to_all(blocks, PLANE, 0, 0, tiled=True)  42.5 us
    all_to_all x6, waiting for transfers between devices, trade(): return lax.all_to_all(blocks, PLANE, 0, 0, tiled=True)  35.4 us
    pallas_call x1, Pallas kernels, attend_back(): pl.pallas_call(attend_back_kernel, out_shape=(jax.ShapeDtypeStruct((token...  26.1 us
    all_to_all x6, starting transfers between devices, trade(): return lax.all_to_all(blocks, PLANE, 0, 0, tiled=True)  25.2 us
  transfers between devices with their start and end apart: 64, of which 21 were waited for; matrix products, arithmetic and copies ran while one was open for 14% of the time, Pallas kernels for 39%

profile of v4, /device:TPU:0, one launch (start us, length us, event | category | flops | bytes accessed | tf_op | source)
XLA Modules:
  0.0 659.7 jit_solution(510801639313048999)
XLA Ops:
  13.3 17.1 %all_to_all.40 = bf16[8,72,640]{2,1,0:T(8,128)(2,1)} all-to-all(bf16[8,72,640]{2,1,0:T(8,128)(2,1)S(1)} %pad_maximum_fusion.3), channel_id=1, replica_groups=mesh['z'=4,'y'=2,'x'=2,'c'=2] {'y','x','c'}, dimensions={0} | all-to-all | bytes 1474560 | tf_op jit(solution)/shard_map/all_to_all | solution.py:108
  34.1 25.4 %all_to_all.41 = bf16[8,64,1536]{2,1,0:T(8,128)(2,1)} all-to-all(bf16[8,64,1536]{2,1,0:T(8,128)(2,1)} %get-tuple-element.112), channel_id=1, replica_groups=mesh['z'=4,'y'=2,'x'=2,'c'=2] {'y','x','c'}, dimensions={0} | all-to-all | bytes 3145728 | tf_op jit(solution)/shard_map/all_to_all | solution.py:108
  62.5 21.4 %collective-permute-done.10.refs_4_ = bf16[256,2048]{1,0:T(8,128)(2,1)} collective-permute-done((bf16[256,2048]{1,0:T(8,128)(2,1)S(1)}, bf16[256,2048]{1,0:T(8,128)(2,1)}, u32[]{:S(2)}, u32[]{:S(2)}) %collective-permute-start.10) | collective-permute-done | bytes 1048608 | tf_op jit(solution)/shard_map/ppermute | solution.py:61
  90.4 10.1 %collective-permute-done.12.refs_0_ = bf16[256,2048]{1,0:T(8,128)(2,1)} collective-permute-done((bf16[256,2048]{1,0:T(8,128)(2,1)S(1)}, bf16[256,2048]{1,0:T(8,128)(2,1)}, u32[]{:S(2)}, u32[]{:S(2)}) %collective-permute-start.12) | collective-permute-done | bytes 1048608 | tf_op jit(solution)/shard_map/ppermute | solution.py:65
  132.1 11.9 %norm_qkv.2 = (bf16[1536,2048]{1,0:T(8,128)(2,1)}, bf16[1536,256]{1,0:T(8,128)(2,1)}, bf16[1536,128]{1,0:T(8,128)(2,1)}) custom-call(bf16[256,2048]{1,0:T(8,128)(2,1)} %refs_10_, bf16[256,2048]{1,0:T(8,128)(2,1)} %collective-permute-done.7.refs_1_, bf16[256,2048]{1,0:T(8,128)(2,1)} %collective-permute-done.8.refs_2_, ...), custom_call_target="tpu_custom_call" | custom-call | flops 2415919104 | bytes 12582912 | tf_op jit(solution)/shard_map/norm_qkv/pallas_call | solution.py:298
  170.0 11.2 %collective-permute-done.5.refs_6_ = bf16[2048,256]{1,0:T(8,128)(2,1)} collective-permute-done((bf16[2048,256]{1,0:T(8,128)(2,1)}, bf16[2048,256]{1,0:T(8,128)(2,1)}, u32[]{:S(2)}, u32[]{:S(2)}) %collective-permute-start.5) | collective-permute-done | bytes 1048608 | tf_op jit(solution)/shard_map/ppermute | solution.py:65
  181.3 15.9 %attend.1 = (bf16[2048,256]{1,0:T(8,128)(2,1)}, bf16[8,256,256]{2,1,0:T(8,128)(2,1)}) custom-call(s32[8]{0:T(128)} %get-tuple-element.210.prev_at, s32[8]{0:T(128)} %iota_xor_fusion.index.refs_8_.here_at, bf16[2048,256]{1,0:T(8,128)(2,1)} %pad_maximum_fusion.2.q_ref, bf16[2304,128]{1,0:T(8,128)(2,1)} %copy-done.35, bf16[2304,128]{1,0:T(8,128)(2,1)} %copy-done.35, ...), custom_call_target="tpu_custom_call" | custom-call | flops 4294967296 | bytes 2097152 | tf_op jit(solution)/shard_map/attend/pallas_call | solution.py:353
  205.9 10.3 %all-to-all-done.3.refs_9_ = bf16[8,256,256]{2,1,0:T(8,128)(2,1)S(1)} async-done(((bf16[8,256,256]{2,1,0:T(8,128)(2,1)}), bf16[8,256,256]{2,1,0:T(8,128)(2,1)S(1)}, u32[]{:S(2)}, u32[]{:S(2)}) %all-to-all-start.3) | async-done | bytes 1048608 | tf_op jit(solution)/shard_map/all_to_all | solution.py:108
  229.7 21.7 %collective-permute-done.21.refs_4_ = bf16[256,2048]{1,0:T(8,128)(2,1)S(1)} collective-permute-done((bf16[256,2048]{1,0:T(8,128)(2,1)}, bf16[256,2048]{1,0:T(8,128)(2,1)S(1)}, u32[]{:S(2)}, u32[]{:S(2)}) %collective-permute-start.21) | collective-permute-done | bytes 1048608 | tf_op jit(solution)/shard_map/ppermute | solution.py:61
  252.1 8.8 %collective-permute-done.27.refs_14_ = bf16[256,2048]{1,0:T(8,128)(2,1)S(1)} collective-permute-done((bf16[256,2048]{1,0:T(8,128)(2,1)S(1)}, bf16[256,2048]{1,0:T(8,128)(2,1)S(1)}, u32[]{:S(2)}, u32[]{:S(2)}) %collective-permute-start.27) | collective-permute-done | bytes 1048608 | tf_op jit(solution)/shard_map/ppermute | solution.py:65
  262.0 10.2 %collective-permute-done.23.refs_6_ = bf16[256,2048]{1,0:T(8,128)(2,1)S(1)} collective-permute-done((bf16[256,2048]{1,0:T(8,128)(2,1)S(1)}, bf16[256,2048]{1,0:T(8,128)(2,1)S(1)}, u32[]{:S(2)}, u32[]{:S(2)}) %collective-permute-start.23) | collective-permute-done | bytes 1048608 | tf_op jit(solution)/shard_map/ppermute | solution.py:65
  276.3 38.6 %ffn.3 = (bf16[2048,512]{1,0:T(8,128)(2,1)}, bf16[2048,1024]{1,0:T(8,128)(2,1)}, bf16[4,1536,512]{2,1,0:T(8,128)(2,1)}) custom-call(bf16[256,2048]{1,0:T(8,128)(2,1)} %get-tuple-element.125.refs_0_, bf16[256,2048]{1,0:T(8,128)(2,1)} %copy-done.56, bf16[256,2048]{1,0:T(8,128)(2,1)} %copy-done.27, bf16[256,2048]{1,0:T(8,128)(2,1)} %copy-done.58, ...), custom_call_target="tpu_custom_call" | custom-call | flops 38654705664 | bytes 29360128 | tf_op jit(solution)/shard_map/ffn/pallas_call | solution.py:581
  315.4 13.4 %down.7 = (f32[4,256,2048]{2,1,0:T(8,128)}, f32[4,256,2048]{2,1,0:T(8,128)}) custom-call(bf16[4,2,256,1024]{3,2,1,0:T(8,128)(2,1)} %bitcast.140, bf16[2048,1536]{1,0:T(8,128)(2,1)} %all-gather.6.cloned.1.call-done.refs_16_.refs_1_.refs_2_), custom_call_target="tpu_custom_call" | custom-call | flops 8589934592 | bytes 20971520 | tf_op jit(solution)/shard_map/down/pallas_call | solution.py:616
  328.8 25.4 %ffn.4 = (bf16[2048,512]{1,0:T(8,128)(2,1)}, bf16[2048,1024]{1,0:T(8,128)(2,1)}, bf16[1536,2048]{1,0:T(8,128)(2,1)}) custom-call(bf16[256,2048]{1,0:T(8,128)(2,1)} %get-tuple-element.125.refs_0_, bf16[256,2048]{1,0:T(8,128)(2,1)} %copy-done.56, bf16[256,2048]{1,0:T(8,128)(2,1)} %copy-done.27, bf16[256,2048]{1,0:T(8,128)(2,1)} %copy-done.58, ...), custom_call_target="tpu_custom_call" | custom-call | flops 19327352832 | bytes 29360128 | tf_op jit(solution)/shard_map/ffn/pallas_call | solution.py:581
  354.2 10.2 %down.10 = (bf16[2,256,2048]{2,1,0:T(8,128)(2,1)}, bf16[2,256,2048]{2,1,0:T(8,128)(2,1)}) custom-call(bf16[4,2,256,1024]{3,2,1,0:T(8,128)(2,1)} %bitcast.110, bf16[2048,1536]{1,0:T(8,128)(2,1)} %all-gather.8.cloned.1.call-done.refs_16_.refs_1_.refs_3_, f32[4,256,2048]{2,1,0:T(8,128)} %get-tuple-element.133.refs_2_, f32[4,256,2048]{2,1,0:T(8,128)} %get-tuple-element.137.refs_3_), custom_call_target="tpu_custom_call" | custom-call | flops 4294967296 | bytes 12582912 | tf_op jit(solution)/shard_map/down/pallas_call | solution.py:616
  364.7 10.3 %down.8 = (bf16[2,256,2048]{2,1,0:T(8,128)(2,1)}, bf16[2,256,2048]{2,1,0:T(8,128)(2,1)}) custom-call(bf16[4,2,256,1024]{3,2,1,0:T(8,128)(2,1)} %bitcast.111, bf16[2048,1536]{1,0:T(8,128)(2,1)} %all-gather.8.cloned.1.call-done.refs_16_.refs_1_.refs_3_, f32[4,256,2048]{2,1,0:T(8,128)} %get-tuple-element.133.refs_2_, f32[4,256,2048]{2,1,0:T(8,128)} %get-tuple-element.137.refs_3_), custom_call_target="tpu_custom_call" | custom-call | flops 4294967296 | bytes 12582912 | tf_op jit(solution)/shard_map/down/pallas_call | solution.py:616
  378.0 23.7 %ffn.5 = bf16[4,1536,512]{2,1,0:T(8,128)(2,1)} custom-call(bf16[256,2048]{1,0:T(8,128)(2,1)} %get-tuple-element.125.refs_0_, bf16[256,2048]{1,0:T(8,128)(2,1)} %copy-done.56, bf16[256,2048]{1,0:T(8,128)(2,1)} %copy-done.27, bf16[256,2048]{1,0:T(8,128)(2,1)} %copy-done.58, bf16[256,2048]{1,0:T(8,128)(2,1)} %copy-done.26, bf16[256,2048]{1,0:T(8,128)(2,1)} %copy-done.57, ...), custom_call_target="tpu_custom_call" | custom-call | flops 19327352832 | bytes 29360128 | tf_op jit(solution)/shard_map/ffn/pallas_call | solution.py:581
  417.1 8.3 %down.9 = (bf16[2,256,2048]{2,1,0:T(8,128)(2,1)}, bf16[2,256,2048]{2,1,0:T(8,128)(2,1)}) custom-call(bf16[4,2,256,512]{3,2,1,0:T(8,128)(2,1)} %bitcast.118, bf16[4,2,256,512]{3,2,1,0:T(8,128)(2,1)} %bitcast.120, bf16[2048,1536]{1,0:T(8,128)(2,1)} %all-gather.6.cloned.1.call-done.refs_16_.refs_1_.refs_2_, ...), custom_call_target="tpu_custom_call" | custom-call | flops 4294967296 | bytes 12582912 | tf_op jit(solution)/shard_map/down/pallas_call | solution.py:616
  433.1 11.4 %open_attention.1 = (f32[256,2048]{1,0:T(8,128)}, bf16[256,2048]{1,0:T(8,128)(2,1)}, bf16[8,256,256]{2,1,0:T(8,128)(2,1)}) custom-call(bf16[2048,256]{1,0:T(8,128)(2,1)} %copy-done.5, bf16[2048,256]{1,0:T(8,128)(2,1)} %collective-permute-done.refs_1_, bf16[2048,256]{1,0:T(8,128)(2,1)} %copy-done.7, bf16[2048,256]{1,0:T(8,128)(2,1)} %collective-permute-done.2.refs_3_, ...), custom_call_target="tpu_custom_call" | custom-call | flops 2147483648 | bytes 8388608 | tf_op jit(solution)/shard_map/open_attention/pallas_call | solution.py:688
  475.1 26.1 %attend_back.1 = (bf16[2048,256]{1,0:T(8,128)(2,1)}, f32[2304,128]{1,0:T(8,128)}) custom-call(s32[8]{0:T(128)} %iota_xor_fusion.index.refs_8_.here_at, s32[8]{0:T(128)} %get-tuple-element.209.prev_at, bf16[2048,256]{1,0:T(8,128)(2,1)} %pad_maximum_fusion.2.q_ref, bf16[8,256,256]{2,1,0:T(8,128)(2,1)} %all-to-all-done.4.do_ref, bf16[2304,128]{1,0:T(8,128)(2,1)} %copy-done.35, ...), custom_call_target="tpu_custom_call" | custom-call | flops 10737418240 | bytes 4194304 | tf_op jit(solution)/shard_map/attend_back/pallas_call | solution.py:443
  516.4 9.2 %collective-permute-done.45.refs_6_ = bf16[256,2048]{1,0:T(8,128)(2,1)S(1)} collective-permute-done((bf16[256,2048]{1,0:T(8,128)(2,1)S(1)}, bf16[256,2048]{1,0:T(8,128)(2,1)S(1)}, u32[]{:S(2)}, u32[]{:S(2)}) %collective-permute-start.45) | collective-permute-done | bytes 1048608 | tf_op jit(solution)/shard_map/ppermute | solution.py:65
  531.8 8.7 %turn_grad.1 = bf16[4,256,512]{2,1,0:T(8,128)(2,1)} custom-call(bf16[256,2048]{1,0:T(8,128)(2,1)} %get-tuple-element.167.refs_0_, bf16[256,2048]{1,0:T(8,128)(2,1)} %collective-permute-done.42.refs_1_, bf16[256,2048]{1,0:T(8,128)(2,1)} %collective-permute-done.40.refs_2_, bf16[256,2048]{1,0:T(8,128)(2,1)} %copy-done.22, bf16[256,2048]{1,0:T(8,128)(2,1)} %copy-done.11, ...), custom_call_target="tpu_custom_call" | custom-call | flops 2147483648 | bytes 8388608 | tf_op jit(solution)/shard_map/turn_grad/pallas_call | solution.py:722
  604.0 12.5 %collective-permute-done.50 = bf16[256,2048]{1,0:T(8,128)(2,1)} collective-permute-done((bf16[256,2048]{1,0:T(8,128)(2,1)}, bf16[256,2048]{1,0:T(8,128)(2,1)}, u32[]{:S(2)}, u32[]{:S(2)}) %collective-permute-start.50) | collective-permute-done | bytes 1048608 | tf_op jit(solution)/shard_map/ppermute | solution.py:61
  621.0 11.6 %all-to-all-done.7.refs_1_ = bf16[8,64,1536]{2,1,0:T(8,128)(2,1)} async-done(((bf16[8,64,1536]{2,1,0:T(8,128)(2,1)}), bf16[8,64,1536]{2,1,0:T(8,128)(2,1)}, u32[]{:S(2)}, u32[]{:S(2)}) %all-to-all-start.7) | async-done | bytes 1572896 | tf_op jit(solution)/shard_map/all_to_all | solution.py:108
  (363 shorter events, 270.3 us)
Async XLA Ops:
  7.2 94.1 %all-gather.4.cloned.1.call-start = ((), (), s32[]{:S(2)}) async-start(), calls=%async_computation.11 | async-start | bytes 3686400 | tf_op jit(solution)/shard_map/all_gather | solution.py:119
  30.4 175.5 %all-gather.6.cloned.1.call-start = ((), (), s32[]{:S(2)}) async-start(), calls=%async_computation.12 | async-start | bytes 7864320 | tf_op jit(solution)/shard_map/all_gather | solution.py:119
  60.7 44.5 %collective-permute-start.7 = (bf16[256,2048]{1,0:T(8,128)(2,1)S(1)}, bf16[256,2048]{1,0:T(8,128)(2,1)}, u32[]{:S(2)}, u32[]{:S(2)}) collective-permute-start(bf16[256,2048]{1,0:T(8,128)(2,1)S(1)} %copy-done), channel_id=1, source_target_pairs={{0,1},{1,0},{2,3},{3,2},{4,5},{5,4},{6,7},{7,6},{8,9},{9,8},{10,11... | collective-permute-start | bytes 3145736 | tf_op jit(solution)/shard_map/ppermute | solution.py:61
  89.9 38.9 %collective-permute-start.11 = (bf16[256,2048]{1,0:T(8,128)(2,1)}, bf16[256,2048]{1,0:T(8,128)(2,1)}, u32[]{:S(2)}, u32[]{:S(2)}) collective-permute-start(bf16[256,2048]{1,0:T(8,128)(2,1)} %collective-permute-done.10.refs_4_), channel_id=1, source_target_pairs={{0,1},{1,0},{2,3},{3,2},{4,5},{5,4},{6,7},{7,6},{8,9},{9,8},{10,11... | collective-permute-start | bytes 3145736 | tf_op jit(solution)/shard_map/ppermute | solution.py:61
  89.9 40.6 %collective-permute-start.9 = (bf16[256,2048]{1,0:T(8,128)(2,1)}, bf16[256,2048]{1,0:T(8,128)(2,1)}, u32[]{:S(2)}, u32[]{:S(2)}) collective-permute-start(bf16[256,2048]{1,0:T(8,128)(2,1)} %collective-permute-done.8.refs_2_), channel_id=1, source_target_pairs={{0,1},{1,0},{2,3},{3,2},{4,5},{5,4},{6,7},{7,6},{8,9},{9,8},{10,11... | collective-permute-start | bytes 3145736 | tf_op jit(solution)/shard_map/ppermute | solution.py:61
  103.6 41.5 %collective-permute-start.3 = (bf16[2048,256]{1,0:T(8,128)(2,1)S(1)}, bf16[2048,256]{1,0:T(8,128)(2,1)S(1)}, u32[]{:S(2)}, u32[]{:S(2)}) collective-permute-start(bf16[2048,256]{1,0:T(8,128)(2,1)S(1)} %slice.230.refs_0_), channel_id=1, source_target_pairs={{0,4},{1,5},{2,6},{3,7},{4,0},{5,1},{6,2},{7,3},{8,12},{9,13},{10,... | collective-permute-start | bytes 3145736 | tf_op jit(solution)/shard_map/ppermute | solution.py:61
  105.2 40.0 %collective-permute-start.1 = (bf16[2048,256]{1,0:T(8,128)(2,1)S(1)}, bf16[2048,256]{1,0:T(8,128)(2,1)S(1)}, u32[]{:S(2)}, u32[]{:S(2)}) collective-permute-start(bf16[2048,256]{1,0:T(8,128)(2,1)S(1)} %slice.230.refs_0_), channel_id=1, source_target_pairs={{0,2},{1,3},{2,0},{3,1},{4,6},{5,7},{6,4},{7,5},{8,10},{9,11},{10,... | collective-permute-start | bytes 3145736 | tf_op jit(solution)/shard_map/ppermute | solution.py:61
  116.6 40.2 %all-to-all-start.2 = ((bf16[8,64,1536]{2,1,0:T(8,128)(2,1)}), bf16[8,64,1536]{2,1,0:T(8,128)(2,1)}, u32[]{:S(2)}, u32[]{:S(2)}) async-start(bf16[8,64,1536]{2,1,0:T(8,128)(2,1)} %get-tuple-element.117), calls=%async_computation.2 | async-start | bytes 3145728 | tf_op jit(solution)/shard_map/all_to_all | solution.py:108
  120.9 207.9 %all-gather.8.cloned.1.call-start = ((), (), s32[]{:S(2)}) async-start(), calls=%async_computation.13 | async-start | bytes 7864320 | tf_op jit(solution)/shard_map/all_gather | solution.py:119
  122.6 38.3 %collective-permute-start.16 = (bf16[256,2048]{1,0:T(8,128)(2,1)}, bf16[256,2048]{1,0:T(8,128)(2,1)}, u32[]{:S(2)}, u32[]{:S(2)}) collective-permute-start(bf16[256,2048]{1,0:T(8,128)(2,1)} %refs_13_.1), channel_id=1, source_target_pairs={{0,1},{1,0},{2,3},{3,2},{4,5},{5,4},{6,7},{7,6},{8,9},{9,8},{10,11... | collective-permute-start | bytes 3145736 | tf_op jit(solution)/shard_map/ppermute | solution.py:61
  128.8 40.2 %collective-permute-start.15 = (bf16[256,2048]{1,0:T(8,128)(2,1)}, bf16[256,2048]{1,0:T(8,128)(2,1)}, u32[]{:S(2)}, u32[]{:S(2)}) collective-permute-start(bf16[256,2048]{1,0:T(8,128)(2,1)} %refs_13_.1), channel_id=1, source_target_pairs={{0,4},{1,5},{2,6},{3,7},{4,0},{5,1},{6,2},{7,3},{8,12},{9,13},{10,... | collective-permute-start | bytes 3145736 | tf_op jit(solution)/shard_map/ppermute | solution.py:61
  130.6 39.5 %collective-permute-start.14 = (bf16[256,2048]{1,0:T(8,128)(2,1)}, bf16[256,2048]{1,0:T(8,128)(2,1)}, u32[]{:S(2)}, u32[]{:S(2)}) collective-permute-start(bf16[256,2048]{1,0:T(8,128)(2,1)} %refs_13_.1), channel_id=1, source_target_pairs={{0,2},{1,3},{2,0},{3,1},{4,6},{5,7},{6,4},{7,5},{8,10},{9,11},{10,... | collective-permute-start | bytes 3145736 | tf_op jit(solution)/shard_map/ppermute | solution.py:61
  160.9 44.9 %collective-permute-start.4 = (bf16[2048,256]{1,0:T(8,128)(2,1)S(1)}, bf16[2048,256]{1,0:T(8,128)(2,1)}, u32[]{:S(2)}, u32[]{:S(2)}) collective-permute-start(bf16[2048,256]{1,0:T(8,128)(2,1)S(1)} %collective-permute-done.3.refs_4_), channel_id=1, source_target_pairs={{0,1},{1,0},{2,3},{3,2},{4,5},{5,4},{6,7},{7,6},{8,9},{9,8},{10,11... | collective-permute-start | bytes 3145736 | tf_op jit(solution)/shard_map/ppermute | solution.py:61
  169.1 36.8 %collective-permute-start.2 = (bf16[2048,256]{1,0:T(8,128)(2,1)S(1)}, bf16[2048,256]{1,0:T(8,128)(2,1)}, u32[]{:S(2)}, u32[]{:S(2)}) collective-permute-start(bf16[2048,256]{1,0:T(8,128)(2,1)S(1)} %collective-permute-done.1.refs_2_), channel_id=1, source_target_pairs={{0,1},{1,0},{2,3},{3,2},{4,5},{5,4},{6,7},{7,6},{8,9},{9,8},{10,11... | collective-permute-start | bytes 3145736 | tf_op jit(solution)/shard_map/ppermute | solution.py:61
  200.8 274.3 %reduce-scatter.4.cloned.1.call-start = ((), (), s32[]{:S(2)}) async-start(), calls=%async_computation.14 | async-start | bytes 7864320 | tf_op jit(solution)/shard_map/reduce_scatter | solution.py:741
  314.9 270.9 %reduce-scatter.8.cloned.1.call-start = ((), (), s32[]{:S(2)}) async-start(), calls=%async_computation.16 | async-start | bytes 7864320 | tf_op jit(solution)/shard_map/reduce_scatter | solution.py:741
  449.3 169.5 %reduce-scatter.6.cloned.1.call-start = ((), (), s32[]{:S(2)}) async-start(), calls=%async_computation.15 | async-start | bytes 3276800 | tf_op jit(solution)/shard_map/reduce_scatter | solution.py:741
  464.7 39.1 %collective-permute-start.42 = (bf16[256,2048]{1,0:T(8,128)(2,1)}, bf16[256,2048]{1,0:T(8,128)(2,1)}, u32[]{:S(2)}, u32[]{:S(2)}) collective-permute-start(bf16[256,2048]{1,0:T(8,128)(2,1)} %get-tuple-element.167.refs_0_), channel_id=1, source_target_pairs={{0,1},{1,0},{2,3},{3,2},{4,5},{5,4},{6,7},{7,6},{8,9},{9,8},{10,11... | collective-permute-start | bytes 3145736 | tf_op jit(solution)/shard_map/ppermute | solution.py:61
  464.7 39.1 %collective-permute-start.41 = (bf16[256,2048]{1,0:T(8,128)(2,1)}, bf16[256,2048]{1,0:T(8,128)(2,1)S(1)}, u32[]{:S(2)}, u32[]{:S(2)}) collective-permute-start(bf16[256,2048]{1,0:T(8,128)(2,1)} %get-tuple-element.167.refs_0_), channel_id=1, source_target_pairs={{0,4},{1,5},{2,6},{3,7},{4,0},{5,1},{6,2},{7,3},{8,12},{9,13},{10,... | collective-permute-start | bytes 3145736 | tf_op jit(solution)/shard_map/ppermute | solution.py:61
  465.3 38.6 %collective-permute-start.40 = (bf16[256,2048]{1,0:T(8,128)(2,1)}, bf16[256,2048]{1,0:T(8,128)(2,1)}, u32[]{:S(2)}, u32[]{:S(2)}) collective-permute-start(bf16[256,2048]{1,0:T(8,128)(2,1)} %get-tuple-element.167.refs_0_), channel_id=1, source_target_pairs={{0,2},{1,3},{2,0},{3,1},{4,6},{5,7},{6,4},{7,5},{8,10},{9,11},{10,... | collective-permute-start | bytes 3145736 | tf_op jit(solution)/shard_map/ppermute | solution.py:61
  470.0 35.7 %collective-permute-start.36 = (bf16[256,2048]{1,0:T(8,128)(2,1)}, bf16[256,2048]{1,0:T(8,128)(2,1)}, u32[]{:S(2)}, u32[]{:S(2)}) collective-permute-start(bf16[256,2048]{1,0:T(8,128)(2,1)} %slice_bitcast_fusion.5), channel_id=1, source_target_pairs={{0,2},{1,5},{2,0},{3,7},{4,6},{5,1},{6,4},{7,3},{8,10},{9,13},{10,... | collective-permute-start | bytes 3145736 | tf_op jit(solution)/shard_map/ppermute | solution.py:65
  580.6 35.9 %collective-permute-start.50 = (bf16[256,2048]{1,0:T(8,128)(2,1)}, bf16[256,2048]{1,0:T(8,128)(2,1)}, u32[]{:S(2)}, u32[]{:S(2)}) collective-permute-start(bf16[256,2048]{1,0:T(8,128)(2,1)} %get-tuple-element.193), channel_id=1, source_target_pairs={{0,2},{1,3},{2,0},{3,1},{4,6},{5,7},{6,4},{7,5},{8,10},{9,11},{10,... | collective-permute-start | bytes 3145736 | tf_op jit(solution)/shard_map/ppermute | solution.py:61
  581.5 35.0 %collective-permute-start.51 = (bf16[256,2048]{1,0:T(8,128)(2,1)}, bf16[256,2048]{1,0:T(8,128)(2,1)}, u32[]{:S(2)}, u32[]{:S(2)}) collective-permute-start(bf16[256,2048]{1,0:T(8,128)(2,1)} %get-tuple-element.194), channel_id=1, source_target_pairs={{0,4},{1,5},{2,6},{3,7},{4,0},{5,1},{6,2},{7,3},{8,12},{9,13},{10,... | collective-permute-start | bytes 3145736 | tf_op jit(solution)/shard_map/ppermute | solution.py:61
  595.4 37.2 %all-to-all-start.7 = ((bf16[8,64,1536]{2,1,0:T(8,128)(2,1)}), bf16[8,64,1536]{2,1,0:T(8,128)(2,1)}, u32[]{:S(2)}, u32[]{:S(2)}) async-start(bf16[8,64,1536]{2,1,0:T(8,128)(2,1)} %turn.5), calls=%async_computation.10 | async-start | bytes 3145728 | tf_op jit(solution)/shard_map/all_to_all | solution.py:108
  (102 other events, 1432.5 us)
Sparse Core Ops, SparseCore 0:
  30.5 59.6 all-gather.3
  91.7 114.0 all-gather.5
  207.4 114.7 all-gather.7
  324.4 108.9 reduce-scatter.3
  435.6 112.6 reduce-scatter.7
  551.0 53.4 reduce-scatter.5

commit v5 on v4

--- a/solution.py
+++ b/solution.py
@@ -832,11 +832,13 @@
     d_att_begun = gather_begin(after(d_att, d_o))
     here_at = me ^ steps
     prev_abs = jnp.where(steps == 0, TP, (steps - 1) ^ me)
-    d_q, d_kv9 = attend_back(here_at, prev_abs, q, after(d_o, sum_0), kv9, lo.reshape(TP, 1, tok), cosine, sine, ek, ev)
+    turned_0 = turn(sum_0)
+    d_q, d_kv9 = attend_back(here_at, prev_abs, q, after(d_o, turned_0), kv9, lo.reshape(TP, 1, tok), cosine, sine, ek, ev)
     f_terms, unused = scatter_plane(lambda groups: after(f_parts[groups], d_heads), (d_q,))
     hidden_out = (residual + total(*f_terms)).astype(BF)
     d_att_blocks = gather_end(*after(d_att_begun, d_q))
-    wo_grad = turn_grad(mixed, d_att_blocks)
+    piece_0 = trade(turned_0)
+    wo_grad = turn_grad(after(mixed, piece_0), d_att_blocks)
     back = along_z(d_kv9[tokens:].astype(BF), -1)
     last = me ^ (TP - 1)
     d_kv = d_kv9[:tokens].reshape(TP, tok, 2 * HD)
@@ -854,7 +856,7 @@
     d_qkv = after(d_qkv, attn_sum, *f_terms)
     d_n1_terms, unused = scatter_plane(lambda groups: down([d_qkv], [wqkv], False, groups))
     d_normed = total(*d_n1_terms)
-    pieces = [give_back(sum_0), give_back(sum_1)]
+    pieces = [piece_0, give_back(sum_1)]
     pieces[1] = after(pieces[1], turned)
     scale = lax.rsqrt(jnp.mean(x_own * x_own, axis=-1, keepdims=True) + NORM_EPS)
     unit = x_own * scale

time: 670 us -> 665 us (level)
  waiting for transfers between devices: 169 us -> 179 us
    ppermute x8, waiting for transfers between devices: 54.4 us -> 65.9 us  [swap_across(): lax.ppermute(value, PLANE, [(i, i ^ 2 + 2 * (i % 2)) for i in range(TP)])]
    unnamed x130 -> x116, local copies, waits for them, and re-layouts: 15.5 us -> 10.5 us
  transfers between devices with their start and end apart: 64 -> 64, of which waited for: 21 -> 23; matrix products, arithmetic and copies ran while one was open for 14% -> 13% of each run, Pallas kernels for 39% -> 39%
where the time goes in v5:
time: 665 us; the launch traced here: 655 us
  Pallas kernels  260 us (39%)
  waiting for transfers between devices  179 us (27%)
  starting transfers between devices  61.6 us (9%)
  other arithmetic  53.1 us (8%)
  blocking collectives  42.5 us (6%)
  local copies, waits for them, and re-layouts  39.7 us (6%)
  between operations  15.7 us (2%)
    pallas_call x3, Pallas kernels, ffn_call(): pl.pallas_call(kernel, out_shape=shapes, in_specs=[ANY] * (2 * TP) + [VME...  87.7 us
    ppermute x42, waiting for transfers between devices, swap(): return lax.ppermute(value, PLANE, [(i, i ^ rel) for i in range(TP)])  73.4 us
    ppermute x8, waiting for transfers between devices, swap_across(): lax.ppermute(value, PLANE, [(i, i ^ 2 + 2 * (i % 2)) for i in range(TP)])  65.9 us
    pallas_call x7, Pallas kernels, down(): pl.pallas_call(functools.partial(down_kernel, count), out_shape=[jax.Shap...  61 us
    all_to_all x2, blocking collectives, trade(): return lax.all_to_all(blocks, PLANE, 0, 0, tiled=True)  42.5 us
    all_to_all x6, waiting for transfers between devices, trade(): return lax.all_to_all(blocks, PLANE, 0, 0, tiled=True)  30 us
    pallas_call x1, Pallas kernels, attend_back(): pl.pallas_call(attend_back_kernel, out_shape=(jax.ShapeDtypeStruct((token...  26.1 us
    all_to_all x6, starting transfers between devices, trade(): return lax.all_to_all(blocks, PLANE, 0, 0, tiled=True)  25.4 us
  transfers between devices with their start and end apart: 64, of which 23 were waited for; matrix products, arithmetic and copies ran while one was open for 13% of the time, Pallas kernels for 39%

profile of v5, /device:TPU:0, one launch (start us, length us, event | category | flops | bytes accessed | tf_op | source)
XLA Modules:
  0.0 655.4 jit_solution(6656566764055691662)
XLA Ops:
  13.3 17.1 %all_to_all.40 = bf16[8,72,640]{2,1,0:T(8,128)(2,1)} all-to-all(bf16[8,72,640]{2,1,0:T(8,128)(2,1)S(1)} %pad_maximum_fusion.3), channel_id=1, replica_groups=mesh['z'=4,'y'=2,'x'=2,'c'=2] {'y','x','c'}, dimensions={0} | all-to-all | bytes 1474560 | tf_op jit(solution)/shard_map/all_to_all | solution.py:108
  34.1 25.4 %all_to_all.41 = bf16[8,64,1536]{2,1,0:T(8,128)(2,1)} all-to-all(bf16[8,64,1536]{2,1,0:T(8,128)(2,1)} %get-tuple-element.113), channel_id=1, replica_groups=mesh['z'=4,'y'=2,'x'=2,'c'=2] {'y','x','c'}, dimensions={0} | all-to-all | bytes 3145728 | tf_op jit(solution)/shard_map/all_to_all | solution.py:108
  62.6 21.4 %collective-permute-done.10.refs_4_ = bf16[256,2048]{1,0:T(8,128)(2,1)} collective-permute-done((bf16[256,2048]{1,0:T(8,128)(2,1)S(1)}, bf16[256,2048]{1,0:T(8,128)(2,1)}, u32[]{:S(2)}, u32[]{:S(2)}) %collective-permute-start.10) | collective-permute-done | bytes 1048608 | tf_op jit(solution)/shard_map/ppermute | solution.py:61
  90.5 10.1 %collective-permute-done.12.refs_0_ = bf16[256,2048]{1,0:T(8,128)(2,1)} collective-permute-done((bf16[256,2048]{1,0:T(8,128)(2,1)S(1)}, bf16[256,2048]{1,0:T(8,128)(2,1)}, u32[]{:S(2)}, u32[]{:S(2)}) %collective-permute-start.12) | collective-permute-done | bytes 1048608 | tf_op jit(solution)/shard_map/ppermute | solution.py:65
  132.1 12.0 %norm_qkv.2 = (bf16[1536,2048]{1,0:T(8,128)(2,1)}, bf16[1536,256]{1,0:T(8,128)(2,1)}, bf16[1536,128]{1,0:T(8,128)(2,1)}) custom-call(bf16[256,2048]{1,0:T(8,128)(2,1)} %refs_10_, bf16[256,2048]{1,0:T(8,128)(2,1)} %collective-permute-done.7.refs_1_, bf16[256,2048]{1,0:T(8,128)(2,1)} %collective-permute-done.8.refs_2_, ...), custom_call_target="tpu_custom_call" | custom-call | flops 2415919104 | bytes 12582912 | tf_op jit(solution)/shard_map/norm_qkv/pallas_call | solution.py:298
  170.1 11.2 %collective-permute-done.5.refs_6_ = bf16[2048,256]{1,0:T(8,128)(2,1)} collective-permute-done((bf16[2048,256]{1,0:T(8,128)(2,1)}, bf16[2048,256]{1,0:T(8,128)(2,1)}, u32[]{:S(2)}, u32[]{:S(2)}) %collective-permute-start.5) | collective-permute-done | bytes 1048608 | tf_op jit(solution)/shard_map/ppermute | solution.py:65
  181.3 15.9 %attend.1 = (bf16[2048,256]{1,0:T(8,128)(2,1)}, bf16[8,256,256]{2,1,0:T(8,128)(2,1)}) custom-call(s32[8]{0:T(128)} %get-tuple-element.212.prev_at, s32[8]{0:T(128)} %iota_xor_fusion.index.refs_8_.here_at, bf16[2048,256]{1,0:T(8,128)(2,1)} %pad_maximum_fusion.2.q_ref, bf16[2304,128]{1,0:T(8,128)(2,1)} %copy-done.28, bf16[2304,128]{1,0:T(8,128)(2,1)} %copy-done.28, ...), custom_call_target="tpu_custom_call" | custom-call | flops 4294967296 | bytes 2097152 | tf_op jit(solution)/shard_map/attend/pallas_call | solution.py:353
  205.9 10.4 %all-to-all-done.3.refs_9_ = bf16[8,256,256]{2,1,0:T(8,128)(2,1)S(1)} async-done(((bf16[8,256,256]{2,1,0:T(8,128)(2,1)}), bf16[8,256,256]{2,1,0:T(8,128)(2,1)S(1)}, u32[]{:S(2)}, u32[]{:S(2)}) %all-to-all-start.3) | async-done | bytes 1048608 | tf_op jit(solution)/shard_map/all_to_all | solution.py:108
  229.8 21.7 %collective-permute-done.21.refs_4_ = bf16[256,2048]{1,0:T(8,128)(2,1)S(1)} collective-permute-done((bf16[256,2048]{1,0:T(8,128)(2,1)}, bf16[256,2048]{1,0:T(8,128)(2,1)S(1)}, u32[]{:S(2)}, u32[]{:S(2)}) %collective-permute-start.21) | collective-permute-done | bytes 1048608 | tf_op jit(solution)/shard_map/ppermute | solution.py:61
  252.2 8.8 %collective-permute-done.27.refs_14_ = bf16[256,2048]{1,0:T(8,128)(2,1)S(1)} collective-permute-done((bf16[256,2048]{1,0:T(8,128)(2,1)S(1)}, bf16[256,2048]{1,0:T(8,128)(2,1)S(1)}, u32[]{:S(2)}, u32[]{:S(2)}) %collective-permute-start.27) | collective-permute-done | bytes 1048608 | tf_op jit(solution)/shard_map/ppermute | solution.py:65
  262.1 10.2 %collective-permute-done.23.refs_6_ = bf16[256,2048]{1,0:T(8,128)(2,1)S(1)} collective-permute-done((bf16[256,2048]{1,0:T(8,128)(2,1)S(1)}, bf16[256,2048]{1,0:T(8,128)(2,1)S(1)}, u32[]{:S(2)}, u32[]{:S(2)}) %collective-permute-start.23) | collective-permute-done | bytes 1048608 | tf_op jit(solution)/shard_map/ppermute | solution.py:65
  276.4 38.6 %ffn.3 = (bf16[2048,512]{1,0:T(8,128)(2,1)}, bf16[2048,1024]{1,0:T(8,128)(2,1)}, bf16[4,1536,512]{2,1,0:T(8,128)(2,1)}) custom-call(bf16[256,2048]{1,0:T(8,128)(2,1)} %get-tuple-element.126.refs_0_, bf16[256,2048]{1,0:T(8,128)(2,1)} %copy-done.49, bf16[256,2048]{1,0:T(8,128)(2,1)} %copy-done.21, bf16[256,2048]{1,0:T(8,128)(2,1)} %copy-done.51, ...), custom_call_target="tpu_custom_call" | custom-call | flops 38654705664 | bytes 29360128 | tf_op jit(solution)/shard_map/ffn/pallas_call | solution.py:581
  315.5 13.4 %down.7 = (f32[4,256,2048]{2,1,0:T(8,128)}, f32[4,256,2048]{2,1,0:T(8,128)}) custom-call(bf16[4,2,256,1024]{3,2,1,0:T(8,128)(2,1)} %bitcast.140, bf16[2048,1536]{1,0:T(8,128)(2,1)} %all-gather.6.cloned.1.call-done.refs_16_.refs_1_.refs_2_), custom_call_target="tpu_custom_call" | custom-call | flops 8589934592 | bytes 20971520 | tf_op jit(solution)/shard_map/down/pallas_call | solution.py:616
  328.9 25.4 %ffn.4 = (bf16[2048,512]{1,0:T(8,128)(2,1)}, bf16[2048,1024]{1,0:T(8,128)(2,1)}, bf16[1536,2048]{1,0:T(8,128)(2,1)}) custom-call(bf16[256,2048]{1,0:T(8,128)(2,1)} %get-tuple-element.126.refs_0_, bf16[256,2048]{1,0:T(8,128)(2,1)} %copy-done.49, bf16[256,2048]{1,0:T(8,128)(2,1)} %copy-done.21, bf16[256,2048]{1,0:T(8,128)(2,1)} %copy-done.51, ...), custom_call_target="tpu_custom_call" | custom-call | flops 19327352832 | bytes 29360128 | tf_op jit(solution)/shard_map/ffn/pallas_call | solution.py:581
  354.3 10.2 %down.10 = (bf16[2,256,2048]{2,1,0:T(8,128)(2,1)}, bf16[2,256,2048]{2,1,0:T(8,128)(2,1)}) custom-call(bf16[4,2,256,1024]{3,2,1,0:T(8,128)(2,1)} %bitcast.110, bf16[2048,1536]{1,0:T(8,128)(2,1)} %all-gather.8.cloned.1.call-done.refs_16_.refs_1_.refs_3_, f32[4,256,2048]{2,1,0:T(8,128)} %get-tuple-element.134.refs_2_, f32[4,256,2048]{2,1,0:T(8,128)} %get-tuple-element.138.refs_3_), custom_call_target="tpu_custom_call" | custom-call | flops 4294967296 | bytes 12582912 | tf_op jit(solution)/shard_map/down/pallas_call | solution.py:616
  364.8 10.3 %down.8 = (bf16[2,256,2048]{2,1,0:T(8,128)(2,1)}, bf16[2,256,2048]{2,1,0:T(8,128)(2,1)}) custom-call(bf16[4,2,256,1024]{3,2,1,0:T(8,128)(2,1)} %bitcast.111, bf16[2048,1536]{1,0:T(8,128)(2,1)} %all-gather.8.cloned.1.call-done.refs_16_.refs_1_.refs_3_, f32[4,256,2048]{2,1,0:T(8,128)} %get-tuple-element.134.refs_2_, f32[4,256,2048]{2,1,0:T(8,128)} %get-tuple-element.138.refs_3_), custom_call_target="tpu_custom_call" | custom-call | flops 4294967296 | bytes 12582912 | tf_op jit(solution)/shard_map/down/pallas_call | solution.py:616
  378.1 23.7 %ffn.5 = bf16[4,1536,512]{2,1,0:T(8,128)(2,1)} custom-call(bf16[256,2048]{1,0:T(8,128)(2,1)} %get-tuple-element.126.refs_0_, bf16[256,2048]{1,0:T(8,128)(2,1)} %copy-done.49, bf16[256,2048]{1,0:T(8,128)(2,1)} %copy-done.21, bf16[256,2048]{1,0:T(8,128)(2,1)} %copy-done.51, bf16[256,2048]{1,0:T(8,128)(2,1)} %copy-done.20, bf16[256,2048]{1,0:T(8,128)(2,1)} %copy-done.50, ...), custom_call_target="tpu_custom_call" | custom-call | flops 19327352832 | bytes 29360128 | tf_op jit(solution)/shard_map/ffn/pallas_call | solution.py:581
  433.0 11.4 %open_attention.1 = (f32[256,2048]{1,0:T(8,128)}, bf16[256,2048]{1,0:T(8,128)(2,1)}, bf16[8,256,256]{2,1,0:T(8,128)(2,1)}) custom-call(bf16[2048,256]{1,0:T(8,128)(2,1)} %copy-done.5, bf16[2048,256]{1,0:T(8,128)(2,1)} %collective-permute-done.refs_1_, bf16[2048,256]{1,0:T(8,128)(2,1)} %copy-done.7, bf16[2048,256]{1,0:T(8,128)(2,1)} %collective-permute-done.2.refs_3_, ...), custom_call_target="tpu_custom_call" | custom-call | flops 2147483648 | bytes 8388608 | tf_op jit(solution)/shard_map/open_attention/pallas_call | solution.py:688
  482.6 26.1 %attend_back.1 = (bf16[2048,256]{1,0:T(8,128)(2,1)}, f32[2304,128]{1,0:T(8,128)}) custom-call(s32[8]{0:T(128)} %iota_xor_fusion.index.refs_8_.here_at, s32[8]{0:T(128)} %get-tuple-element.211.prev_at, bf16[2048,256]{1,0:T(8,128)(2,1)} %pad_maximum_fusion.2.q_ref, bf16[8,256,256]{2,1,0:T(8,128)(2,1)} %all-to-all-done.4.do_ref, bf16[2304,128]{1,0:T(8,128)(2,1)} %copy-done.28, ...), custom_call_target="tpu_custom_call" | custom-call | flops 10737418240 | bytes 4194304 | tf_op jit(solution)/shard_map/attend_back/pallas_call | solution.py:443
  524.9 14.9 %collective-permute-done.45.refs_6_ = bf16[256,2048]{1,0:T(8,128)(2,1)} collective-permute-done((bf16[256,2048]{1,0:T(8,128)(2,1)S(1)}, bf16[256,2048]{1,0:T(8,128)(2,1)}, u32[]{:S(2)}, u32[]{:S(2)}) %collective-permute-start.45) | collective-permute-done | bytes 1048608 | tf_op jit(solution)/shard_map/ppermute | solution.py:65
  543.7 8.9 %turn_grad.1 = bf16[4,256,512]{2,1,0:T(8,128)(2,1)} custom-call(bf16[256,2048]{1,0:T(8,128)(2,1)} %get-tuple-element.168.refs_0_, bf16[256,2048]{1,0:T(8,128)(2,1)} %collective-permute-done.42.refs_1_, bf16[256,2048]{1,0:T(8,128)(2,1)} %collective-permute-done.40.refs_2_, bf16[256,2048]{1,0:T(8,128)(2,1)} %collective-permute-done.43.refs_3_, ...), custom_call_target="tpu_custom_call" | custom-call | flops 2147483648 | bytes 8388608 | tf_op jit(solution)/shard_map/turn_grad/pallas_call | solution.py:722
  571.8 10.6 %collective-permute-done.49 = bf16[256,2048]{1,0:T(8,128)(2,1)S(1)} collective-permute-done((bf16[256,2048]{1,0:T(8,128)(2,1)S(1)}, bf16[256,2048]{1,0:T(8,128)(2,1)S(1)}, u32[]{:S(2)}, u32[]{:S(2)}) %collective-permute-start.49) | collective-permute-done | bytes 1048608 | tf_op jit(solution)/shard_map/ppermute | solution.py:65
  599.0 11.6 %collective-permute-done.50 = bf16[256,2048]{1,0:T(8,128)(2,1)} collective-permute-done((bf16[256,2048]{1,0:T(8,128)(2,1)}, bf16[256,2048]{1,0:T(8,128)(2,1)}, u32[]{:S(2)}, u32[]{:S(2)}) %collective-permute-start.50) | collective-permute-done | bytes 1048608 | tf_op jit(solution)/shard_map/ppermute | solution.py:61
  615.9 12.5 %all-to-all-done.7.refs_1_ = bf16[8,64,1536]{2,1,0:T(8,128)(2,1)} async-done(((bf16[8,64,1536]{2,1,0:T(8,128)(2,1)}), bf16[8,64,1536]{2,1,0:T(8,128)(2,1)}, u32[]{:S(2)}, u32[]{:S(2)}) %all-to-all-start.7) | async-done | bytes 1572896 | tf_op jit(solution)/shard_map/all_to_all | solution.py:108
  (349 shorter events, 257.7 us)
Async XLA Ops:
  7.2 94.2 %all-gather.4.cloned.1.call-start = ((), (), s32[]{:S(2)}) async-start(), calls=%async_computation.11 | async-start | bytes 3686400 | tf_op jit(solution)/shard_map/all_gather | solution.py:119
  30.4 175.5 %all-gather.6.cloned.1.call-start = ((), (), s32[]{:S(2)}) async-start(), calls=%async_computation.12 | async-start | bytes 7864320 | tf_op jit(solution)/shard_map/all_gather | solution.py:119
  60.7 44.5 %collective-permute-start.7 = (bf16[256,2048]{1,0:T(8,128)(2,1)S(1)}, bf16[256,2048]{1,0:T(8,128)(2,1)}, u32[]{:S(2)}, u32[]{:S(2)}) collective-permute-start(bf16[256,2048]{1,0:T(8,128)(2,1)S(1)} %copy-done), channel_id=1, source_target_pairs={{0,1},{1,0},{2,3},{3,2},{4,5},{5,4},{6,7},{7,6},{8,9},{9,8},{10,11... | collective-permute-start | bytes 3145736 | tf_op jit(solution)/shard_map/ppermute | solution.py:61
  89.9 38.9 %collective-permute-start.11 = (bf16[256,2048]{1,0:T(8,128)(2,1)}, bf16[256,2048]{1,0:T(8,128)(2,1)}, u32[]{:S(2)}, u32[]{:S(2)}) collective-permute-start(bf16[256,2048]{1,0:T(8,128)(2,1)} %collective-permute-done.10.refs_4_), channel_id=1, source_target_pairs={{0,1},{1,0},{2,3},{3,2},{4,5},{5,4},{6,7},{7,6},{8,9},{9,8},{10,11... | collective-permute-start | bytes 3145736 | tf_op jit(solution)/shard_map/ppermute | solution.py:61
  90.0 40.6 %collective-permute-start.9 = (bf16[256,2048]{1,0:T(8,128)(2,1)}, bf16[256,2048]{1,0:T(8,128)(2,1)}, u32[]{:S(2)}, u32[]{:S(2)}) collective-permute-start(bf16[256,2048]{1,0:T(8,128)(2,1)} %collective-permute-done.8.refs_2_), channel_id=1, source_target_pairs={{0,1},{1,0},{2,3},{3,2},{4,5},{5,4},{6,7},{7,6},{8,9},{9,8},{10,11... | collective-permute-start | bytes 3145736 | tf_op jit(solution)/shard_map/ppermute | solution.py:61
  103.6 41.5 %collective-permute-start.3 = (bf16[2048,256]{1,0:T(8,128)(2,1)S(1)}, bf16[2048,256]{1,0:T(8,128)(2,1)S(1)}, u32[]{:S(2)}, u32[]{:S(2)}) collective-permute-start(bf16[2048,256]{1,0:T(8,128)(2,1)S(1)} %slice.230.refs_0_), channel_id=1, source_target_pairs={{0,4},{1,5},{2,6},{3,7},{4,0},{5,1},{6,2},{7,3},{8,12},{9,13},{10,... | collective-permute-start | bytes 3145736 | tf_op jit(solution)/shard_map/ppermute | solution.py:61
  105.2 40.0 %collective-permute-start.1 = (bf16[2048,256]{1,0:T(8,128)(2,1)S(1)}, bf16[2048,256]{1,0:T(8,128)(2,1)S(1)}, u32[]{:S(2)}, u32[]{:S(2)}) collective-permute-start(bf16[2048,256]{1,0:T(8,128)(2,1)S(1)} %slice.230.refs_0_), channel_id=1, source_target_pairs={{0,2},{1,3},{2,0},{3,1},{4,6},{5,7},{6,4},{7,5},{8,10},{9,11},{10,... | collective-permute-start | bytes 3145736 | tf_op jit(solution)/shard_map/ppermute | solution.py:61
  116.6 40.2 %all-to-all-start.2 = ((bf16[8,64,1536]{2,1,0:T(8,128)(2,1)}), bf16[8,64,1536]{2,1,0:T(8,128)(2,1)}, u32[]{:S(2)}, u32[]{:S(2)}) async-start(bf16[8,64,1536]{2,1,0:T(8,128)(2,1)} %get-tuple-element.118), calls=%async_computation.2 | async-start | bytes 3145728 | tf_op jit(solution)/shard_map/all_to_all | solution.py:108
  120.9 208.0 %all-gather.8.cloned.1.call-start = ((), (), s32[]{:S(2)}) async-start(), calls=%async_computation.13 | async-start | bytes 7864320 | tf_op jit(solution)/shard_map/all_gather | solution.py:119
  122.6 38.3 %collective-permute-start.16 = (bf16[256,2048]{1,0:T(8,128)(2,1)}, bf16[256,2048]{1,0:T(8,128)(2,1)}, u32[]{:S(2)}, u32[]{:S(2)}) collective-permute-start(bf16[256,2048]{1,0:T(8,128)(2,1)} %refs_13_.1), channel_id=1, source_target_pairs={{0,1},{1,0},{2,3},{3,2},{4,5},{5,4},{6,7},{7,6},{8,9},{9,8},{10,11... | collective-permute-start | bytes 3145736 | tf_op jit(solution)/shard_map/ppermute | solution.py:61
  128.8 40.3 %collective-permute-start.15 = (bf16[256,2048]{1,0:T(8,128)(2,1)}, bf16[256,2048]{1,0:T(8,128)(2,1)}, u32[]{:S(2)}, u32[]{:S(2)}) collective-permute-start(bf16[256,2048]{1,0:T(8,128)(2,1)} %refs_13_.1), channel_id=1, source_target_pairs={{0,4},{1,5},{2,6},{3,7},{4,0},{5,1},{6,2},{7,3},{8,12},{9,13},{10,... | collective-permute-start | bytes 3145736 | tf_op jit(solution)/shard_map/ppermute | solution.py:61
  130.6 39.5 %collective-permute-start.14 = (bf16[256,2048]{1,0:T(8,128)(2,1)}, bf16[256,2048]{1,0:T(8,128)(2,1)}, u32[]{:S(2)}, u32[]{:S(2)}) collective-permute-start(bf16[256,2048]{1,0:T(8,128)(2,1)} %refs_13_.1), channel_id=1, source_target_pairs={{0,2},{1,3},{2,0},{3,1},{4,6},{5,7},{6,4},{7,5},{8,10},{9,11},{10,... | collective-permute-start | bytes 3145736 | tf_op jit(solution)/shard_map/ppermute | solution.py:61
  160.9 44.9 %collective-permute-start.4 = (bf16[2048,256]{1,0:T(8,128)(2,1)S(1)}, bf16[2048,256]{1,0:T(8,128)(2,1)}, u32[]{:S(2)}, u32[]{:S(2)}) collective-permute-start(bf16[2048,256]{1,0:T(8,128)(2,1)S(1)} %collective-permute-done.3.refs_4_), channel_id=1, source_target_pairs={{0,1},{1,0},{2,3},{3,2},{4,5},{5,4},{6,7},{7,6},{8,9},{9,8},{10,11... | collective-permute-start | bytes 3145736 | tf_op jit(solution)/shard_map/ppermute | solution.py:61
  169.1 36.8 %collective-permute-start.2 = (bf16[2048,256]{1,0:T(8,128)(2,1)S(1)}, bf16[2048,256]{1,0:T(8,128)(2,1)}, u32[]{:S(2)}, u32[]{:S(2)}) collective-permute-start(bf16[2048,256]{1,0:T(8,128)(2,1)S(1)} %collective-permute-done.1.refs_2_), channel_id=1, source_target_pairs={{0,1},{1,0},{2,3},{3,2},{4,5},{5,4},{6,7},{7,6},{8,9},{9,8},{10,11... | collective-permute-start | bytes 3145736 | tf_op jit(solution)/shard_map/ppermute | solution.py:61
  200.8 274.5 %reduce-scatter.4.cloned.1.call-start = ((), (), s32[]{:S(2)}) async-start(), calls=%async_computation.14 | async-start | bytes 7864320 | tf_op jit(solution)/shard_map/reduce_scatter | solution.py:741
  315.0 272.2 %reduce-scatter.8.cloned.1.call-start = ((), (), s32[]{:S(2)}) async-start(), calls=%async_computation.16 | async-start | bytes 7864320 | tf_op jit(solution)/shard_map/reduce_scatter | solution.py:741
  464.9 46.2 %collective-permute-start.42 = (bf16[256,2048]{1,0:T(8,128)(2,1)}, bf16[256,2048]{1,0:T(8,128)(2,1)}, u32[]{:S(2)}, u32[]{:S(2)}) collective-permute-start(bf16[256,2048]{1,0:T(8,128)(2,1)} %get-tuple-element.168.refs_0_), channel_id=1, source_target_pairs={{0,1},{1,0},{2,3},{3,2},{4,5},{5,4},{6,7},{7,6},{8,9},{9,8},{10,11... | collective-permute-start | bytes 3145736 | tf_op jit(solution)/shard_map/ppermute | solution.py:61
  464.9 46.2 %collective-permute-start.41 = (bf16[256,2048]{1,0:T(8,128)(2,1)}, bf16[256,2048]{1,0:T(8,128)(2,1)S(1)}, u32[]{:S(2)}, u32[]{:S(2)}) collective-permute-start(bf16[256,2048]{1,0:T(8,128)(2,1)} %get-tuple-element.168.refs_0_), channel_id=1, source_target_pairs={{0,4},{1,5},{2,6},{3,7},{4,0},{5,1},{6,2},{7,3},{8,12},{9,13},{10,... | collective-permute-start | bytes 3145736 | tf_op jit(solution)/shard_map/ppermute | solution.py:61
  465.5 45.7 %collective-permute-start.40 = (bf16[256,2048]{1,0:T(8,128)(2,1)}, bf16[256,2048]{1,0:T(8,128)(2,1)}, u32[]{:S(2)}, u32[]{:S(2)}) collective-permute-start(bf16[256,2048]{1,0:T(8,128)(2,1)} %get-tuple-element.168.refs_0_), channel_id=1, source_target_pairs={{0,2},{1,3},{2,0},{3,1},{4,6},{5,7},{6,4},{7,5},{8,10},{9,11},{10,... | collective-permute-start | bytes 3145736 | tf_op jit(solution)/shard_map/ppermute | solution.py:61
  470.1 43.7 %collective-permute-start.36 = (bf16[256,2048]{1,0:T(8,128)(2,1)}, bf16[256,2048]{1,0:T(8,128)(2,1)}, u32[]{:S(2)}, u32[]{:S(2)}) collective-permute-start(bf16[256,2048]{1,0:T(8,128)(2,1)} %slice_bitcast_fusion.5), channel_id=1, source_target_pairs={{0,2},{1,5},{2,0},{3,7},{4,6},{5,1},{6,4},{7,3},{8,10},{9,13},{10,... | collective-permute-start | bytes 3145736 | tf_op jit(solution)/shard_map/ppermute | solution.py:65
  478.3 65.4 %all-to-all-start.5 = ((bf16[8,64,1536]{2,1,0:T(8,128)(2,1)}), bf16[8,64,1536]{2,1,0:T(8,128)(2,1)}, u32[]{:S(2)}, u32[]{:S(2)}) async-start(bf16[8,64,1536]{2,1,0:T(8,128)(2,1)} %turn.3), calls=%async_computation.6 | async-start | bytes 3145728 | tf_op jit(solution)/shard_map/all_to_all | solution.py:108
  482.6 131.1 %reduce-scatter.6.cloned.1.call-start = ((), (), s32[]{:S(2)}) async-start(), calls=%async_computation.15 | async-start | bytes 3276800 | tf_op jit(solution)/shard_map/reduce_scatter | solution.py:741
  517.0 38.6 %collective-permute-start.37 = (bf16[256,2048]{1,0:T(8,128)(2,1)}, bf16[256,2048]{1,0:T(8,128)(2,1)}, u32[]{:S(2)}, u32[]{:S(2)}) collective-permute-start(bf16[256,2048]{1,0:T(8,128)(2,1)} %get-tuple-element.197), channel_id=1, source_target_pairs={{0,2},{1,3},{2,0},{3,1},{4,6},{5,7},{6,4},{7,5},{8,10},{9,11},{10,... | collective-permute-start | bytes 3145736 | tf_op jit(solution)/shard_map/ppermute | solution.py:61
  590.3 38.1 %all-to-all-start.7 = ((bf16[8,64,1536]{2,1,0:T(8,128)(2,1)}), bf16[8,64,1536]{2,1,0:T(8,128)(2,1)}, u32[]{:S(2)}, u32[]{:S(2)}) async-start(bf16[8,64,1536]{2,1,0:T(8,128)(2,1)} %turn.5), calls=%async_computation.10 | async-start | bytes 3145728 | tf_op jit(solution)/shard_map/all_to_all | solution.py:108
  (95 other events, 1438.6 us)
Sparse Core Ops, SparseCore 0:
  30.5 59.6 all-gather.3
  91.8 114.0 all-gather.5
  207.4 114.7 all-gather.7
  324.4 108.9 reduce-scatter.3
  435.6 112.6 reduce-scatter.7
  561.4 52.2 reduce-scatter.5

commit v6 on v5

--- a/solution.py
+++ b/solution.py
@@ -88,12 +88,11 @@
 
 def scatter_plane(part, wait=()):
     even, odd = part((3, 2))
-    both = add(even, swap(odd, 1))
+    both = add(even, after(swap(odd, 1), *wait))
     across, over_y = swap_across(both[0]), both[1]
     even, odd = part((1, 0))
-    both = add(even, swap(odd, 1))
+    both = add(even, after(swap(odd, 1), *wait))
     over_x, own = both[0], both[1]
-    across = after(across, *wait)
     first = on_first()
     over_x = jnp.where(first, over_x, add(over_x, across))
     over_y = jnp.where(first, add(over_y, across), over_y)

time: 665 us -> 684 us (1.029)
  waiting for transfers between devices: 179 us -> 197 us
    ppermute x8, waiting for transfers between devices: 65.9 us -> 74.5 us  [swap_across(): lax.ppermute(value, PLANE, [(i, i ^ 2 + 2 * (i % 2)) for i in range(TP)])]
    ppermute x42, waiting for transfers between devices: 73.4 us -> 80.8 us  [swap(): return lax.ppermute(value, PLANE, [(i, i ^ rel) for i in range(TP)])]
    unnamed x116 -> x120, local copies, waits for them, and re-layouts: 10.5 us -> 13.9 us
  transfers between devices with their start and end apart: 64 -> 64, of which waited for: 23 -> 27; matrix products, arithmetic and copies ran while one was open for 13% -> 12% of each run, Pallas kernels for 39% -> 38%
where the time goes in v6:
time: 684 us; the launch traced here: 674 us
  Pallas kernels  261 us (38%)
  waiting for transfers between devices  197 us (29%)
  starting transfers between devices  61.9 us (9%)
  other arithmetic  50.4 us (7%)
  blocking collectives  42.5 us (6%)
  local copies, waits for them, and re-layouts  42 us (6%)
  between operations  15.7 us (2%)
    pallas_call x3, Pallas kernels, ffn_call(): pl.pallas_call(kernel, out_shape=shapes, in_specs=[ANY] * (2 * TP) + [VME...  88.6 us
    ppermute x42, waiting for transfers between devices, swap(): return lax.ppermute(value, PLANE, [(i, i ^ rel) for i in range(TP)])  80.8 us
    ppermute x8, waiting for transfers between devices, swap_across(): lax.ppermute(value, PLANE, [(i, i ^ 2 + 2 * (i % 2)) for i in range(TP)])  74.5 us
    pallas_call x7, Pallas kernels, down(): pl.pallas_call(functools.partial(down_kernel, count), out_shape=[jax.Shap...  60.7 us
    all_to_all x2, blocking collectives, trade(): return lax.all_to_all(blocks, PLANE, 0, 0, tiled=True)  42.5 us
    all_to_all x6, waiting for transfers between devices, trade(): return lax.all_to_all(blocks, PLANE, 0, 0, tiled=True)  34.2 us
    pallas_call x1, Pallas kernels, attend_back(): pl.pallas_call(attend_back_kernel, out_shape=(jax.ShapeDtypeStruct((token...  26.1 us
    all_to_all x6, starting transfers between devices, trade(): return lax.all_to_all(blocks, PLANE, 0, 0, tiled=True)  24 us
  transfers between devices with their start and end apart: 64, of which 27 were waited for; matrix products, arithmetic and copies ran while one was open for 12% of the time, Pallas kernels for 38%

profile of v6, /device:TPU:0, one launch (start us, length us, event | category | flops | bytes accessed | tf_op | source)
XLA Modules:
  0.0 673.6 jit_solution(1748238341955288892)
XLA Ops:
  13.3 17.1 %all_to_all.40 = bf16[8,72,640]{2,1,0:T(8,128)(2,1)} all-to-all(bf16[8,72,640]{2,1,0:T(8,128)(2,1)S(1)} %pad_maximum_fusion.3), channel_id=1, replica_groups=mesh['z'=4,'y'=2,'x'=2,'c'=2] {'y','x','c'}, dimensions={0} | all-to-all | bytes 1474560 | tf_op jit(solution)/shard_map/all_to_all | solution.py:107
  34.2 25.4 %all_to_all.41 = bf16[8,64,1536]{2,1,0:T(8,128)(2,1)} all-to-all(bf16[8,64,1536]{2,1,0:T(8,128)(2,1)} %get-tuple-element.114), channel_id=1, replica_groups=mesh['z'=4,'y'=2,'x'=2,'c'=2] {'y','x','c'}, dimensions={0} | all-to-all | bytes 3145728 | tf_op jit(solution)/shard_map/all_to_all | solution.py:107
  62.5 21.5 %collective-permute-done.10.refs_4_ = bf16[256,2048]{1,0:T(8,128)(2,1)} collective-permute-done((bf16[256,2048]{1,0:T(8,128)(2,1)S(1)}, bf16[256,2048]{1,0:T(8,128)(2,1)}, u32[]{:S(2)}, u32[]{:S(2)}) %collective-permute-start.10) | collective-permute-done | bytes 1048608 | tf_op jit(solution)/shard_map/ppermute | solution.py:61
  90.5 10.1 %collective-permute-done.12.refs_0_ = bf16[256,2048]{1,0:T(8,128)(2,1)} collective-permute-done((bf16[256,2048]{1,0:T(8,128)(2,1)S(1)}, bf16[256,2048]{1,0:T(8,128)(2,1)}, u32[]{:S(2)}, u32[]{:S(2)}) %collective-permute-start.12) | collective-permute-done | bytes 1048608 | tf_op jit(solution)/shard_map/ppermute | solution.py:65
  132.1 11.9 %norm_qkv.2 = (bf16[1536,2048]{1,0:T(8,128)(2,1)}, bf16[1536,256]{1,0:T(8,128)(2,1)}, bf16[1536,128]{1,0:T(8,128)(2,1)}) custom-call(bf16[256,2048]{1,0:T(8,128)(2,1)} %refs_10_, bf16[256,2048]{1,0:T(8,128)(2,1)} %collective-permute-done.7.refs_1_, bf16[256,2048]{1,0:T(8,128)(2,1)} %collective-permute-done.8.refs_2_, ...), custom_call_target="tpu_custom_call" | custom-call | flops 2415919104 | bytes 12582912 | tf_op jit(solution)/shard_map/norm_qkv/pallas_call | solution.py:297
  170.1 11.2 %collective-permute-done.5.refs_6_ = bf16[2048,256]{1,0:T(8,128)(2,1)} collective-permute-done((bf16[2048,256]{1,0:T(8,128)(2,1)}, bf16[2048,256]{1,0:T(8,128)(2,1)}, u32[]{:S(2)}, u32[]{:S(2)}) %collective-permute-start.5) | collective-permute-done | bytes 1048608 | tf_op jit(solution)/shard_map/ppermute | solution.py:65
  181.3 15.9 %attend.1 = (bf16[2048,256]{1,0:T(8,128)(2,1)}, bf16[8,256,256]{2,1,0:T(8,128)(2,1)}) custom-call(s32[8]{0:T(128)} %get-tuple-element.214.prev_at, s32[8]{0:T(128)} %iota_xor_fusion.index.refs_8_.here_at, bf16[2048,256]{1,0:T(8,128)(2,1)} %pad_maximum_fusion.2.q_ref, bf16[2304,128]{1,0:T(8,128)(2,1)} %copy-done.31, bf16[2304,128]{1,0:T(8,128)(2,1)} %copy-done.31, ...), custom_call_target="tpu_custom_call" | custom-call | flops 4294967296 | bytes 2097152 | tf_op jit(solution)/shard_map/attend/pallas_call | solution.py:352
  205.9 10.4 %all-to-all-done.3.refs_9_ = bf16[8,256,256]{2,1,0:T(8,128)(2,1)S(1)} async-done(((bf16[8,256,256]{2,1,0:T(8,128)(2,1)}), bf16[8,256,256]{2,1,0:T(8,128)(2,1)S(1)}, u32[]{:S(2)}, u32[]{:S(2)}) %all-to-all-start.3) | async-done | bytes 1048608 | tf_op jit(solution)/shard_map/all_to_all | solution.py:107
  229.6 21.7 %collective-permute-done.21.refs_4_ = bf16[256,2048]{1,0:T(8,128)(2,1)S(1)} collective-permute-done((bf16[256,2048]{1,0:T(8,128)(2,1)}, bf16[256,2048]{1,0:T(8,128)(2,1)S(1)}, u32[]{:S(2)}, u32[]{:S(2)}) %collective-permute-start.21) | collective-permute-done | bytes 1048608 | tf_op jit(solution)/shard_map/ppermute | solution.py:61
  261.9 10.2 %collective-permute-done.23.refs_6_ = bf16[256,2048]{1,0:T(8,128)(2,1)S(1)} collective-permute-done((bf16[256,2048]{1,0:T(8,128)(2,1)S(1)}, bf16[256,2048]{1,0:T(8,128)(2,1)S(1)}, u32[]{:S(2)}, u32[]{:S(2)}) %collective-permute-start.23) | collective-permute-done | bytes 1048608 | tf_op jit(solution)/shard_map/ppermute | solution.py:65
  274.9 38.7 %ffn.3 = (bf16[2048,512]{1,0:T(8,128)(2,1)}, bf16[2048,1024]{1,0:T(8,128)(2,1)}, bf16[4,1536,512]{2,1,0:T(8,128)(2,1)}) custom-call(bf16[256,2048]{1,0:T(8,128)(2,1)} %get-tuple-element.127.refs_0_, bf16[256,2048]{1,0:T(8,128)(2,1)} %copy-done.52, bf16[256,2048]{1,0:T(8,128)(2,1)} %copy-done.23, bf16[256,2048]{1,0:T(8,128)(2,1)} %copy-done.54, ...), custom_call_target="tpu_custom_call" | custom-call | flops 38654705664 | bytes 29360128 | tf_op jit(solution)/shard_map/ffn/pallas_call | solution.py:580
  314.1 13.4 %down.7 = (f32[4,256,2048]{2,1,0:T(8,128)}, f32[4,256,2048]{2,1,0:T(8,128)}) custom-call(bf16[4,2,256,1024]{3,2,1,0:T(8,128)(2,1)} %bitcast.140, bf16[2048,1536]{1,0:T(8,128)(2,1)} %all-gather.6.cloned.1.call-done.refs_16_.refs_1_.refs_2_), custom_call_target="tpu_custom_call" | custom-call | flops 8589934592 | bytes 20971520 | tf_op jit(solution)/shard_map/down/pallas_call | solution.py:615
  327.5 26.1 %ffn.4 = (bf16[2048,512]{1,0:T(8,128)(2,1)}, bf16[2048,1024]{1,0:T(8,128)(2,1)}, bf16[1536,2048]{1,0:T(8,128)(2,1)}) custom-call(bf16[256,2048]{1,0:T(8,128)(2,1)} %get-tuple-element.127.refs_0_, bf16[256,2048]{1,0:T(8,128)(2,1)} %copy-done.52, bf16[256,2048]{1,0:T(8,128)(2,1)} %copy-done.23, bf16[256,2048]{1,0:T(8,128)(2,1)} %copy-done.54, ...), custom_call_target="tpu_custom_call" | custom-call | flops 19327352832 | bytes 29360128 | tf_op jit(solution)/shard_map/ffn/pallas_call | solution.py:580
  353.6 10.2 %down.10 = (bf16[2,256,2048]{2,1,0:T(8,128)(2,1)}, bf16[2,256,2048]{2,1,0:T(8,128)(2,1)}) custom-call(bf16[4,2,256,1024]{3,2,1,0:T(8,128)(2,1)} %bitcast.110, bf16[2048,1536]{1,0:T(8,128)(2,1)} %all-gather.8.cloned.1.call-done.refs_16_.refs_1_.refs_3_, f32[4,256,2048]{2,1,0:T(8,128)} %get-tuple-element.135.refs_2_, f32[4,256,2048]{2,1,0:T(8,128)} %get-tuple-element.139.refs_3_), custom_call_target="tpu_custom_call" | custom-call | flops 4294967296 | bytes 12582912 | tf_op jit(solution)/shard_map/down/pallas_call | solution.py:615
  364.2 10.1 %down.8 = (bf16[2,256,2048]{2,1,0:T(8,128)(2,1)}, bf16[2,256,2048]{2,1,0:T(8,128)(2,1)}) custom-call(bf16[4,2,256,1024]{3,2,1,0:T(8,128)(2,1)} %bitcast.111, bf16[2048,1536]{1,0:T(8,128)(2,1)} %all-gather.8.cloned.1.call-done.refs_16_.refs_1_.refs_3_, f32[4,256,2048]{2,1,0:T(8,128)} %get-tuple-element.135.refs_2_, f32[4,256,2048]{2,1,0:T(8,128)} %get-tuple-element.139.refs_3_), custom_call_target="tpu_custom_call" | custom-call | flops 4294967296 | bytes 12582912 | tf_op jit(solution)/shard_map/down/pallas_call | solution.py:615
  374.4 23.8 %ffn.5 = bf16[4,1536,512]{2,1,0:T(8,128)(2,1)} custom-call(bf16[256,2048]{1,0:T(8,128)(2,1)} %get-tuple-element.127.refs_0_, bf16[256,2048]{1,0:T(8,128)(2,1)} %copy-done.52, bf16[256,2048]{1,0:T(8,128)(2,1)} %copy-done.23, bf16[256,2048]{1,0:T(8,128)(2,1)} %copy-done.54, bf16[256,2048]{1,0:T(8,128)(2,1)} %copy-done.22, bf16[256,2048]{1,0:T(8,128)(2,1)} %copy-done.53, ...), custom_call_target="tpu_custom_call" | custom-call | flops 19327352832 | bytes 29360128 | tf_op jit(solution)/shard_map/ffn/pallas_call | solution.py:580
  406.4 10.7 %collective-permute-done.31 = bf16[256,2048]{1,0:T(8,128)(2,1)S(1)} collective-permute-done((bf16[256,2048]{1,0:T(8,128)(2,1)S(1)}, bf16[256,2048]{1,0:T(8,128)(2,1)S(1)}, u32[]{:S(2)}, u32[]{:S(2)}) %collective-permute-start.31) | collective-permute-done | bytes 1048608 | tf_op jit(solution)/shard_map/ppermute | solution.py:65
  444.8 11.4 %open_attention.1 = (f32[256,2048]{1,0:T(8,128)}, bf16[256,2048]{1,0:T(8,128)(2,1)}, bf16[8,256,256]{2,1,0:T(8,128)(2,1)}) custom-call(bf16[2048,256]{1,0:T(8,128)(2,1)} %copy-done.5, bf16[2048,256]{1,0:T(8,128)(2,1)} %collective-permute-done.refs_1_, bf16[2048,256]{1,0:T(8,128)(2,1)} %copy-done.7, bf16[2048,256]{1,0:T(8,128)(2,1)} %collective-permute-done.2.refs_3_, ...), custom_call_target="tpu_custom_call" | custom-call | flops 2147483648 | bytes 8388608 | tf_op jit(solution)/shard_map/open_attention/pallas_call | solution.py:687
  461.7 13.7 %all-to-all-done.4.do_ref = bf16[8,256,256]{2,1,0:T(8,128)(2,1)S(1)} async-done(((bf16[8,256,256]{2,1,0:T(8,128)(2,1)}), bf16[8,256,256]{2,1,0:T(8,128)(2,1)S(1)}, u32[]{:S(2)}, u32[]{:S(2)}) %all-to-all-start.4) | async-done | bytes 1048608 | tf_op jit(solution)/shard_map/all_to_all | solution.py:107
  490.3 26.1 %attend_back.1 = (bf16[2048,256]{1,0:T(8,128)(2,1)}, f32[2304,128]{1,0:T(8,128)}) custom-call(s32[8]{0:T(128)} %iota_xor_fusion.index.refs_8_.here_at, s32[8]{0:T(128)} %get-tuple-element.213.prev_at, bf16[2048,256]{1,0:T(8,128)(2,1)} %pad_maximum_fusion.2.q_ref, bf16[8,256,256]{2,1,0:T(8,128)(2,1)} %copy-done.24, bf16[2304,128]{1,0:T(8,128)(2,1)} %copy-done.31, ...), custom_call_target="tpu_custom_call" | custom-call | flops 10737418240 | bytes 4194304 | tf_op jit(solution)/shard_map/attend_back/pallas_call | solution.py:442
  536.0 11.1 %collective-permute-done.36 = bf16[256,2048]{1,0:T(8,128)(2,1)S(1)} collective-permute-done((bf16[256,2048]{1,0:T(8,128)(2,1)S(1)}, bf16[256,2048]{1,0:T(8,128)(2,1)S(1)}, u32[]{:S(2)}, u32[]{:S(2)}) %collective-permute-start.36) | collective-permute-done | bytes 1048608 | tf_op jit(solution)/shard_map/ppermute | solution.py:65
  591.2 11.0 %collective-permute-done.49 = bf16[256,2048]{1,0:T(8,128)(2,1)S(1)} collective-permute-done((bf16[256,2048]{1,0:T(8,128)(2,1)S(1)}, bf16[256,2048]{1,0:T(8,128)(2,1)S(1)}, u32[]{:S(2)}, u32[]{:S(2)}) %collective-permute-start.49) | collective-permute-done | bytes 1048608 | tf_op jit(solution)/shard_map/ppermute | solution.py:65
  618.1 12.4 %collective-permute-done.50 = bf16[256,2048]{1,0:T(8,128)(2,1)} collective-permute-done((bf16[256,2048]{1,0:T(8,128)(2,1)}, bf16[256,2048]{1,0:T(8,128)(2,1)}, u32[]{:S(2)}, u32[]{:S(2)}) %collective-permute-start.50) | collective-permute-done | bytes 1048608 | tf_op jit(solution)/shard_map/ppermute | solution.py:61
  636.3 10.2 %all-to-all-done.7.refs_1_ = bf16[8,64,1536]{2,1,0:T(8,128)(2,1)} async-done(((bf16[8,64,1536]{2,1,0:T(8,128)(2,1)}), bf16[8,64,1536]{2,1,0:T(8,128)(2,1)}, u32[]{:S(2)}, u32[]{:S(2)}) %all-to-all-start.7) | async-done | bytes 1572896 | tf_op jit(solution)/shard_map/all_to_all | solution.py:107
  (353 shorter events, 273.6 us)
Async XLA Ops:
  7.2 94.2 %all-gather.4.cloned.1.call-start = ((), (), s32[]{:S(2)}) async-start(), calls=%async_computation.11 | async-start | bytes 3686400 | tf_op jit(solution)/shard_map/all_gather | solution.py:118
  30.4 175.5 %all-gather.6.cloned.1.call-start = ((), (), s32[]{:S(2)}) async-start(), calls=%async_computation.12 | async-start | bytes 7864320 | tf_op jit(solution)/shard_map/all_gather | solution.py:118
  60.8 44.5 %collective-permute-start.7 = (bf16[256,2048]{1,0:T(8,128)(2,1)S(1)}, bf16[256,2048]{1,0:T(8,128)(2,1)}, u32[]{:S(2)}, u32[]{:S(2)}) collective-permute-start(bf16[256,2048]{1,0:T(8,128)(2,1)S(1)} %copy-done), channel_id=1, source_target_pairs={{0,1},{1,0},{2,3},{3,2},{4,5},{5,4},{6,7},{7,6},{8,9},{9,8},{10,11... | collective-permute-start | bytes 3145736 | tf_op jit(solution)/shard_map/ppermute | solution.py:61
  89.9 38.9 %collective-permute-start.11 = (bf16[256,2048]{1,0:T(8,128)(2,1)}, bf16[256,2048]{1,0:T(8,128)(2,1)}, u32[]{:S(2)}, u32[]{:S(2)}) collective-permute-start(bf16[256,2048]{1,0:T(8,128)(2,1)} %collective-permute-done.10.refs_4_), channel_id=1, source_target_pairs={{0,1},{1,0},{2,3},{3,2},{4,5},{5,4},{6,7},{7,6},{8,9},{9,8},{10,11... | collective-permute-start | bytes 3145736 | tf_op jit(solution)/shard_map/ppermute | solution.py:61
  90.0 40.6 %collective-permute-start.9 = (bf16[256,2048]{1,0:T(8,128)(2,1)}, bf16[256,2048]{1,0:T(8,128)(2,1)}, u32[]{:S(2)}, u32[]{:S(2)}) collective-permute-start(bf16[256,2048]{1,0:T(8,128)(2,1)} %collective-permute-done.8.refs_2_), channel_id=1, source_target_pairs={{0,1},{1,0},{2,3},{3,2},{4,5},{5,4},{6,7},{7,6},{8,9},{9,8},{10,11... | collective-permute-start | bytes 3145736 | tf_op jit(solution)/shard_map/ppermute | solution.py:61
  103.7 41.5 %collective-permute-start.3 = (bf16[2048,256]{1,0:T(8,128)(2,1)S(1)}, bf16[2048,256]{1,0:T(8,128)(2,1)S(1)}, u32[]{:S(2)}, u32[]{:S(2)}) collective-permute-start(bf16[2048,256]{1,0:T(8,128)(2,1)S(1)} %slice.230.refs_0_), channel_id=1, source_target_pairs={{0,4},{1,5},{2,6},{3,7},{4,0},{5,1},{6,2},{7,3},{8,12},{9,13},{10,... | collective-permute-start | bytes 3145736 | tf_op jit(solution)/shard_map/ppermute | solution.py:61
  105.2 40.0 %collective-permute-start.1 = (bf16[2048,256]{1,0:T(8,128)(2,1)S(1)}, bf16[2048,256]{1,0:T(8,128)(2,1)S(1)}, u32[]{:S(2)}, u32[]{:S(2)}) collective-permute-start(bf16[2048,256]{1,0:T(8,128)(2,1)S(1)} %slice.230.refs_0_), channel_id=1, source_target_pairs={{0,2},{1,3},{2,0},{3,1},{4,6},{5,7},{6,4},{7,5},{8,10},{9,11},{10,... | collective-permute-start | bytes 3145736 | tf_op jit(solution)/shard_map/ppermute | solution.py:61
  116.6 40.2 %all-to-all-start.2 = ((bf16[8,64,1536]{2,1,0:T(8,128)(2,1)}), bf16[8,64,1536]{2,1,0:T(8,128)(2,1)}, u32[]{:S(2)}, u32[]{:S(2)}) async-start(bf16[8,64,1536]{2,1,0:T(8,128)(2,1)} %get-tuple-element.119), calls=%async_computation.2 | async-start | bytes 3145728 | tf_op jit(solution)/shard_map/all_to_all | solution.py:107
  120.9 206.6 %all-gather.8.cloned.1.call-start = ((), (), s32[]{:S(2)}) async-start(), calls=%async_computation.13 | async-start | bytes 7864320 | tf_op jit(solution)/shard_map/all_gather | solution.py:118
  122.6 38.3 %collective-permute-start.16 = (bf16[256,2048]{1,0:T(8,128)(2,1)}, bf16[256,2048]{1,0:T(8,128)(2,1)}, u32[]{:S(2)}, u32[]{:S(2)}) collective-permute-start(bf16[256,2048]{1,0:T(8,128)(2,1)} %refs_13_.1), channel_id=1, source_target_pairs={{0,1},{1,0},{2,3},{3,2},{4,5},{5,4},{6,7},{7,6},{8,9},{9,8},{10,11... | collective-permute-start | bytes 3145736 | tf_op jit(solution)/shard_map/ppermute | solution.py:61
  128.9 40.3 %collective-permute-start.15 = (bf16[256,2048]{1,0:T(8,128)(2,1)}, bf16[256,2048]{1,0:T(8,128)(2,1)}, u32[]{:S(2)}, u32[]{:S(2)}) collective-permute-start(bf16[256,2048]{1,0:T(8,128)(2,1)} %refs_13_.1), channel_id=1, source_target_pairs={{0,4},{1,5},{2,6},{3,7},{4,0},{5,1},{6,2},{7,3},{8,12},{9,13},{10,... | collective-permute-start | bytes 3145736 | tf_op jit(solution)/shard_map/ppermute | solution.py:61
  130.6 39.5 %collective-permute-start.14 = (bf16[256,2048]{1,0:T(8,128)(2,1)}, bf16[256,2048]{1,0:T(8,128)(2,1)}, u32[]{:S(2)}, u32[]{:S(2)}) collective-permute-start(bf16[256,2048]{1,0:T(8,128)(2,1)} %refs_13_.1), channel_id=1, source_target_pairs={{0,2},{1,3},{2,0},{3,1},{4,6},{5,7},{6,4},{7,5},{8,10},{9,11},{10,... | collective-permute-start | bytes 3145736 | tf_op jit(solution)/shard_map/ppermute | solution.py:61
  161.0 44.9 %collective-permute-start.4 = (bf16[2048,256]{1,0:T(8,128)(2,1)S(1)}, bf16[2048,256]{1,0:T(8,128)(2,1)}, u32[]{:S(2)}, u32[]{:S(2)}) collective-permute-start(bf16[2048,256]{1,0:T(8,128)(2,1)S(1)} %collective-permute-done.3.refs_4_), channel_id=1, source_target_pairs={{0,1},{1,0},{2,3},{3,2},{4,5},{5,4},{6,7},{7,6},{8,9},{9,8},{10,11... | collective-permute-start | bytes 3145736 | tf_op jit(solution)/shard_map/ppermute | solution.py:61
  169.1 36.8 %collective-permute-start.2 = (bf16[2048,256]{1,0:T(8,128)(2,1)S(1)}, bf16[2048,256]{1,0:T(8,128)(2,1)}, u32[]{:S(2)}, u32[]{:S(2)}) collective-permute-start(bf16[2048,256]{1,0:T(8,128)(2,1)S(1)} %collective-permute-done.1.refs_2_), channel_id=1, source_target_pairs={{0,1},{1,0},{2,3},{3,2},{4,5},{5,4},{6,7},{7,6},{8,9},{9,8},{10,11... | collective-permute-start | bytes 3145736 | tf_op jit(solution)/shard_map/ppermute | solution.py:61
  200.9 282.7 %reduce-scatter.4.cloned.1.call-start = ((), (), s32[]{:S(2)}) async-start(), calls=%async_computation.14 | async-start | bytes 7864320 | tf_op jit(solution)/shard_map/reduce_scatter | solution.py:740
  313.7 292.8 %reduce-scatter.8.cloned.1.call-start = ((), (), s32[]{:S(2)}) async-start(), calls=%async_computation.16 | async-start | bytes 7864320 | tf_op jit(solution)/shard_map/reduce_scatter | solution.py:740
  460.1 60.9 %collective-permute-start.34 = (bf16[2,256,2048]{2,1,0:T(8,128)(2,1)}, bf16[2,256,2048]{2,1,0:T(8,128)(2,1)}, u32[]{:S(2)}, u32[]{:S(2)}) collective-permute-start(bf16[2,256,2048]{2,1,0:T(8,128)(2,1)} %get-tuple-element.156), channel_id=1, source_target_pairs={{0,1},{1,0},{2,3},{3,2},{4,5},{5,4},{6,7},{7,6},{8,9},{9,8},{10,11... | collective-permute-start | bytes 6291464 | tf_op jit(solution)/shard_map/ppermute | solution.py:61
  460.6 62.4 %collective-permute-start.35 = (bf16[2,256,2048]{2,1,0:T(8,128)(2,1)}, bf16[2,256,2048]{2,1,0:T(8,128)(2,1)}, u32[]{:S(2)}, u32[]{:S(2)}) collective-permute-start(bf16[2,256,2048]{2,1,0:T(8,128)(2,1)} %get-tuple-element.162), channel_id=1, source_target_pairs={{0,1},{1,0},{2,3},{3,2},{4,5},{5,4},{6,7},{7,6},{8,9},{9,8},{10,11... | collective-permute-start | bytes 6291464 | tf_op jit(solution)/shard_map/ppermute | solution.py:61
  475.3 42.2 %collective-permute-start.42 = (bf16[256,2048]{1,0:T(8,128)(2,1)}, bf16[256,2048]{1,0:T(8,128)(2,1)}, u32[]{:S(2)}, u32[]{:S(2)}) collective-permute-start(bf16[256,2048]{1,0:T(8,128)(2,1)} %get-tuple-element.170.refs_0_), channel_id=1, source_target_pairs={{0,1},{1,0},{2,3},{3,2},{4,5},{5,4},{6,7},{7,6},{8,9},{9,8},{10,11... | collective-permute-start | bytes 3145736 | tf_op jit(solution)/shard_map/ppermute | solution.py:61
  475.3 43.7 %collective-permute-start.41 = (bf16[256,2048]{1,0:T(8,128)(2,1)}, bf16[256,2048]{1,0:T(8,128)(2,1)}, u32[]{:S(2)}, u32[]{:S(2)}) collective-permute-start(bf16[256,2048]{1,0:T(8,128)(2,1)} %get-tuple-element.170.refs_0_), channel_id=1, source_target_pairs={{0,4},{1,5},{2,6},{3,7},{4,0},{5,1},{6,2},{7,3},{8,12},{9,13},{10,... | collective-permute-start | bytes 3145736 | tf_op jit(solution)/shard_map/ppermute | solution.py:61
  475.9 43.2 %collective-permute-start.40 = (bf16[256,2048]{1,0:T(8,128)(2,1)}, bf16[256,2048]{1,0:T(8,128)(2,1)}, u32[]{:S(2)}, u32[]{:S(2)}) collective-permute-start(bf16[256,2048]{1,0:T(8,128)(2,1)} %get-tuple-element.170.refs_0_), channel_id=1, source_target_pairs={{0,2},{1,3},{2,0},{3,1},{4,6},{5,7},{6,4},{7,5},{8,10},{9,11},{10,... | collective-permute-start | bytes 3145736 | tf_op jit(solution)/shard_map/ppermute | solution.py:61
  486.6 68.7 %all-to-all-start.5 = ((bf16[8,64,1536]{2,1,0:T(8,128)(2,1)}), bf16[8,64,1536]{2,1,0:T(8,128)(2,1)S(1)}, u32[]{:S(2)}, u32[]{:S(2)}) async-start(bf16[8,64,1536]{2,1,0:T(8,128)(2,1)} %turn.3), calls=%async_computation.6 | async-start | bytes 3145728 | tf_op jit(solution)/shard_map/all_to_all | solution.py:107
  490.2 143.9 %reduce-scatter.6.cloned.1.call-start = ((), (), s32[]{:S(2)}) async-start(), calls=%async_computation.15 | async-start | bytes 3276800 | tf_op jit(solution)/shard_map/reduce_scatter | solution.py:740
  609.4 37.0 %all-to-all-start.7 = ((bf16[8,64,1536]{2,1,0:T(8,128)(2,1)}), bf16[8,64,1536]{2,1,0:T(8,128)(2,1)}, u32[]{:S(2)}, u32[]{:S(2)}) async-start(bf16[8,64,1536]{2,1,0:T(8,128)(2,1)} %turn.5), calls=%async_computation.10 | async-start | bytes 3145728 | tf_op jit(solution)/shard_map/all_to_all | solution.py:107
  (97 other events, 1474.2 us)
Sparse Core Ops, SparseCore 0:
  30.5 59.6 all-gather.3
  91.8 114.0 all-gather.5
  207.4 114.7 all-gather.7
  324.4 108.9 reduce-scatter.3
  435.6 112.6 reduce-scatter.7
  580.7 53.4 reduce-scatter.5
